TPU v7x, 32 devices: a whole 2x2x4 slice. The times are simulated.
32 devices in a mesh: seq: 2 (over x), ctx: 4 (over y, core), fsdp: 4 (over z).
Axes of the slice: x: 2, y: 2, z: 4, core: 2. Of those that a mesh axis runs over, the one named last changes fastest.
Arguments:
- tokens: bfloat16 [8, 1024, 2048], P(('seq', 'fsdp'), 'ctx'), may hold values from -6 to 6
- doc_lengths: int32 [8, 8], P(('seq', 'fsdp')), may hold values from 1 to 832, 1024 in all within a row
- keep_mask: int32 [8, 1024], P(('seq', 'fsdp'), 'ctx'), may hold values 0 or 1
- ln_gain: bfloat16 [2, 2048], P(None, ('ctx', 'fsdp')), may hold values from 0.5 to 1.5
- ln_bias: bfloat16 [2, 2048], P(None, ('ctx', 'fsdp')), may hold values from -2 to 2
- qkv_weight: bfloat16 [2, 2048, 6144], P(None, ('ctx', 'fsdp')), may hold values from -0.125 to 0.125
- qkv_bias: bfloat16 [2, 6144], P(None, ('ctx', 'fsdp')), may hold values from -2 to 2
- out_weight: bfloat16 [2, 2048, 2048], P(None, ('ctx', 'fsdp')), may hold values from -0.5 to 0.5
- out_bias: bfloat16 [2, 2048], P(None, ('ctx', 'fsdp')), may hold values from -2 to 2
- up_weight: bfloat16 [2, 2048, 8192], P(None, ('ctx', 'fsdp')), may hold values from -0.125 to 0.125
- up_bias: bfloat16 [2, 8192], P(None, ('ctx', 'fsdp')), may hold values from -2 to 2
- down_weight: bfloat16 [2, 8192, 2048], P(None, ('ctx', 'fsdp')), may hold values from -0.0625 to 0.0625
- down_bias: bfloat16 [2, 2048], P(None, ('ctx', 'fsdp')), may hold values from -2 to 2
- cotangent: bfloat16 [8, 1024, 2048], P(('seq', 'fsdp'), 'ctx'), may hold values from -6 to 6
Outputs:
- result: bfloat16 [8, 1024, 2048], P(('seq', 'fsdp'), 'ctx')
- grad_tokens: float32 [8, 1024, 2048], P(('seq', 'fsdp'), 'ctx')
- grad_ln_gain: float32 [2, 2048], P(None, ('ctx', 'fsdp'))
- grad_ln_bias: float32 [2, 2048], P(None, ('ctx', 'fsdp'))
- grad_qkv_weight: float32 [2, 2048, 6144], P(None, ('ctx', 'fsdp'))
- grad_qkv_bias: float32 [2, 6144], P(None, ('ctx', 'fsdp'))
- grad_out_weight: float32 [2, 2048, 2048], P(None, ('ctx', 'fsdp'))
- grad_out_bias: float32 [2, 2048], P(None, ('ctx', 'fsdp'))
- grad_up_weight: float32 [2, 2048, 8192], P(None, ('ctx', 'fsdp'))
- grad_up_bias: float32 [2, 8192], P(None, ('ctx', 'fsdp'))
- grad_down_weight: float32 [2, 8192, 2048], P(None, ('ctx', 'fsdp'))
- grad_down_bias: float32 [2, 2048], P(None, ('ctx', 'fsdp'))
Inputs may be any that keep to these rules, and one draw needn't show every extreme that they name: `doc_lengths`: each row lists the 8 document lengths of one sequence in order; they sum to 1024, and the longest is exactly 832.
All inputs are finite; a program needn't handle non-finite values. No bound on the sum of `keep_mask` on one device may be relied on, other than what follows from the above.
Results may differ from a plain program's by a relative error of at most 0.02.
Values may be sent and summed in bfloat16 or wider, within the bound.
A program may use at most 960 MiB of HBM per device.

v0:
```python
import functools
import math

import jax
import jax.numpy as jnp
from jax import lax
from jax.sharding import PartitionSpec as P

D = 2048
HEADS = 32
HEAD_DIM = 64
ROT = 32
FF = 8192
LAYERS = 2


EPS = 1e-05
NEG = -1e30


def place_tokens(token_index, lengths):
    bounds = jnp.cumsum(lengths)
    starts = bounds - lengths
    segment = jnp.sum((token_index[:, None] >= bounds[None, :]).astype(jnp.int32), axis=1)
    chosen = segment[:, None] == jnp.arange(lengths.shape[0], dtype=jnp.int32)[None, :]
    position = token_index - jnp.sum(jnp.where(chosen, starts[None, :], 0), axis=1)
    return (segment, position)


def angles(position):
    indices = jnp.arange(0, ROT, 2, dtype=jnp.float32) / ROT
    inverse = 1.0 / 10000.0**indices
    turned = position.astype(jnp.float32)[:, None] * inverse[None, :]
    turned = jnp.concatenate([turned, turned], axis=1)
    return (jnp.cos(turned), jnp.sin(turned))


def rotate(values, cosine, sine):
    rotary = values[..., :ROT]
    middle = ROT // 2
    turned = jnp.concatenate([-rotary[..., middle:], rotary[..., :middle]], axis=-1)
    mixed = rotary * cosine[:, None, :] + turned * sine[:, None, :]
    return jnp.concatenate([mixed, values[..., ROT:]], axis=-1)


def normalize(hidden, gain_row, shift_row):
    average = jnp.mean(hidden, axis=1, keepdims=True)
    centred = hidden - average
    spread = jnp.mean(centred * centred, axis=1, keepdims=True)
    return centred * lax.rsqrt(spread + EPS) * gain_row + shift_row


def block_scores(queries, travelling, start, query_index, query_segment, lengths):
    key_flat, value_flat, key_keep = travelling
    count = key_flat.shape[0]
    key_index = start + jnp.arange(count, dtype=jnp.int32)
    key_segment = place_tokens(key_index, lengths)[0]
    allowed = (
        (query_segment[:, None] == key_segment[None, :])
        & (key_index[None, :] <= query_index[:, None])
        & ((key_keep[None, :] > 0) | (key_index[None, :] == query_index[:, None]))
    )
    key_rows = key_flat.reshape(count, HEADS, HEAD_DIM)
    value_rows = value_flat.reshape(count, HEADS, HEAD_DIM)
    scores = jnp.einsum("qhd,khd->hqk", queries, key_rows, preferred_element_type=jnp.float32) * (
        1.0 / math.sqrt(HEAD_DIM)
    )
    return (scores, allowed, key_rows, value_rows)


def attend(running, travelling, start, queries, query_index, query_segment, lengths):
    maxima, totals, weighted = running
    scores, allowed, key_rows, value_rows = block_scores(
        queries, travelling, start, query_index, query_segment, lengths
    )
    masked = jnp.where(allowed[None], scores, NEG)
    new_max = jnp.maximum(maxima, jnp.max(masked, axis=2))
    probs = jnp.where(allowed[None], jnp.exp(masked - new_max[:, :, None]), 0.0)
    totals = jnp.sum(probs, axis=2)
    weighted = jnp.einsum(
        "hqk,khd->hqd", probs.astype(jnp.bfloat16), value_rows, preferred_element_type=jnp.float32
    )
    return (new_max, totals, weighted)


def attend_back(
    travelling, start, queries, maxima, grad_numer, drift, query_index, query_segment, lengths
):
    scores, allowed, key_rows, value_rows = block_scores(
        queries, travelling, start, query_index, query_segment, lengths
    )
    count = key_rows.shape[0]
    scale = 1.0 / math.sqrt(HEAD_DIM)
    probs = jnp.where(allowed[None], jnp.exp(scores - maxima[:, :, None]), 0.0)
    grad_probs = jnp.einsum(
        "hqd,khd->hqk", grad_numer, value_rows, preferred_element_type=jnp.float32
    )
    grad_scores = (probs * (grad_probs - drift[:, :, None])).astype(jnp.bfloat16)
    grad_query = (
        jnp.einsum("hqk,khd->qhd", grad_scores, key_rows, preferred_element_type=jnp.float32)
        * scale
    )
    grad_key = (
        jnp.einsum("hqk,qhd->khd", grad_scores, queries, preferred_element_type=jnp.float32) * scale
    )
    grad_value = jnp.einsum(
        "hqk,hqd->khd", probs.astype(jnp.bfloat16), grad_numer, preferred_element_type=jnp.float32
    )
    return (
        grad_query,
        grad_key.reshape(count, HEADS * HEAD_DIM),
        grad_value.reshape(count, HEADS * HEAD_DIM),
    )


def attention_forward(queries, key_flat, value_flat, key_keep, query_index, query_segment, lengths):
    row_count = key_flat.shape[0]
    initial = (
        jnp.full((HEADS, row_count), NEG, jnp.float32),
        jnp.zeros((HEADS, row_count), jnp.float32),
        jnp.zeros((HEADS, row_count, HEAD_DIM), jnp.float32),
    )
    return attend(
        initial,
        (
            lax.all_gather(key_flat, "ctx", axis=0, tiled=True),
            lax.all_gather(value_flat, "ctx", axis=0, tiled=True),
            lax.all_gather(key_keep, "ctx", axis=0, tiled=True),
        ),
        jnp.int32(0),
        queries,
        query_index,
        query_segment,
        lengths,
    )


def attention_backward(
    queries,
    key_flat,
    value_flat,
    key_keep,
    maxima,
    grad_numer,
    drift,
    query_index,
    query_segment,
    lengths,
):
    whole = (
        lax.all_gather(key_flat, "ctx", axis=0, tiled=True),
        lax.all_gather(value_flat, "ctx", axis=0, tiled=True),
        lax.all_gather(key_keep, "ctx", axis=0, tiled=True),
    )
    grad_query, every_key, every_value = attend_back(
        whole, 0, queries, maxima, grad_numer, drift, query_index, query_segment, lengths
    )
    grad_key, grad_value = (
        lax.psum_scatter(
            every_key.astype(jnp.bfloat16), "ctx", scatter_dimension=0, tiled=True
        ).astype(jnp.float32),
        lax.psum_scatter(
            every_value.astype(jnp.bfloat16), "ctx", scatter_dimension=0, tiled=True
        ).astype(jnp.float32),
    )
    return (grad_query, grad_key, grad_value)


def layer_forward(hidden, weights, cosine, sine, key_keep, query_index, query_segment, lengths):
    (
        norm_gain,
        norm_shift,
        joint_weight,
        joint_bias,
        output_weight,
        output_bias,
        upper_weight,
        upper_bias,
        lower_weight,
        lower_bias,
    ) = weights
    row_count = hidden.shape[0]
    width = HEADS * HEAD_DIM
    normed = normalize(
        hidden, norm_gain.astype(jnp.float32), norm_shift.astype(jnp.float32)
    ).astype(jnp.bfloat16)
    joint = jnp.dot(normed, joint_weight, preferred_element_type=jnp.float32) + joint_bias.astype(
        jnp.float32
    )
    queries = rotate(joint[:, :width].reshape(row_count, HEADS, HEAD_DIM), cosine, sine).astype(
        jnp.bfloat16
    )
    key_flat = (
        rotate(joint[:, width : 2 * width].reshape(row_count, HEADS, HEAD_DIM), cosine, sine)
        .astype(jnp.bfloat16)
        .reshape(row_count, width)
    )
    value_flat = joint[:, 2 * width :].astype(jnp.bfloat16)
    maxima, totals, weighted = attention_forward(
        queries, key_flat, value_flat, key_keep, query_index, query_segment, lengths
    )
    mixed = (weighted / totals[:, :, None]).transpose(1, 0, 2).reshape(row_count, width)
    attention_out = jnp.dot(
        mixed.astype(jnp.bfloat16), output_weight, preferred_element_type=jnp.float32
    ) + output_bias.astype(jnp.float32)
    inner = jnp.dot(normed, upper_weight, preferred_element_type=jnp.float32) + upper_bias.astype(
        jnp.float32
    )
    activated = jax.nn.gelu(inner, approximate=True).astype(jnp.bfloat16)
    feed_out = jnp.dot(
        activated, lower_weight, preferred_element_type=jnp.float32
    ) + lower_bias.astype(jnp.float32)
    saved = (hidden, normed, queries, key_flat, value_flat, maxima, totals, mixed, inner, activated)
    return (hidden + (attention_out + feed_out), saved)


def layer_backward(
    grad_out, saved, weights, cosine, sine, key_keep, query_index, query_segment, lengths
):
    hidden, normed, queries, key_flat, value_flat, maxima, totals, mixed, inner, activated = saved
    (
        norm_gain,
        norm_shift,
        joint_weight,
        joint_bias,
        output_weight,
        output_bias,
        upper_weight,
        upper_bias,
        lower_weight,
        lower_bias,
    ) = weights
    row_count = hidden.shape[0]
    width = HEADS * HEAD_DIM
    ratio = FF // D
    grad_branch = grad_out.astype(jnp.bfloat16)
    mixed_low = mixed.astype(jnp.bfloat16)
    branch_bias = jnp.sum(grad_branch, axis=0, dtype=jnp.float32)
    grad_activated = jnp.einsum(
        "td,fd->tf", grad_branch, lower_weight, preferred_element_type=jnp.float32
    )
    gelu_pull = jax.vjp(functools.partial(jax.nn.gelu, approximate=True), inner)[1]
    grad_inner = gelu_pull(grad_activated)[0].astype(jnp.bfloat16)
    upper_bias_grad = jnp.sum(grad_inner, axis=0, dtype=jnp.float32)
    grad_normed = jnp.einsum(
        "tf,df->td", grad_inner, upper_weight, preferred_element_type=jnp.float32
    )
    upper_bias_rows = upper_bias_grad.reshape(D, ratio)
    normed_cols = normed
    upper_part = jnp.einsum(
        "tc,tf->cf", normed_cols, grad_inner, preferred_element_type=jnp.float32
    )
    lower_part = jnp.einsum(
        "tc,td->cd", activated, grad_branch, preferred_element_type=jnp.float32
    ).reshape(lax.axis_size(("ctx", "fsdp")) * (D // lax.axis_size(("ctx", "fsdp"))), ratio * width)
    bias_part = upper_bias_rows
    branch_part = branch_bias[:, None]
    feed_share = lax.psum_scatter(
        jnp.concatenate([upper_part, lower_part, bias_part, branch_part], axis=1),
        ("ctx", "fsdp"),
        scatter_dimension=0,
        tiled=True,
    )
    share_rows = feed_share.shape[0]
    upper_share = feed_share[:, :FF]
    lower_share = feed_share[:, FF : FF + ratio * width].reshape(share_rows * ratio, width)
    upper_bias_share = feed_share[:, FF + ratio * width : FF + ratio * width + ratio].reshape(
        share_rows * ratio
    )
    branch_share = feed_share[:, FF + ratio * width + ratio]
    feed_parts = (upper_share, upper_bias_share, lower_share, branch_share)
    output_share = None
    grad_mixed = jnp.einsum(
        "te,de->td", grad_branch, output_weight, preferred_element_type=jnp.float32
    )
    head_mixed = mixed.reshape(row_count, HEADS, HEAD_DIM).transpose(1, 0, 2)
    head_grad = grad_mixed.reshape(row_count, HEADS, HEAD_DIM).transpose(1, 0, 2)
    drift = jnp.sum(head_grad * head_mixed, axis=2) / totals
    grad_numer = (head_grad / totals[:, :, None]).astype(jnp.bfloat16)
    grad_query, grad_key, grad_value = attention_backward(
        queries,
        key_flat,
        value_flat,
        key_keep,
        maxima,
        grad_numer,
        drift,
        query_index,
        query_segment,
        lengths,
    )
    grad_query = rotate(grad_query, cosine, -sine).reshape(row_count, width)
    grad_key = rotate(grad_key.reshape(row_count, HEADS, HEAD_DIM), cosine, -sine).reshape(
        row_count, width
    )
    grad_joint = jnp.concatenate([grad_query, grad_key, grad_value], axis=1).astype(jnp.bfloat16)
    joint_bias_grad = jnp.sum(grad_joint, axis=0, dtype=jnp.float32)
    grad_normed = grad_normed + jnp.einsum(
        "te,de->td", grad_joint, joint_weight, preferred_element_type=jnp.float32
    )
    norm_pull = jax.vjp(
        normalize, hidden, norm_gain.astype(jnp.float32), norm_shift.astype(jnp.float32)
    )[1]
    grad_hidden, gain_grad, shift_grad = norm_pull(grad_normed)
    joint_bias_rows = joint_bias_grad.reshape(D, 3)
    normed_cols = normed
    joint_part = jnp.einsum(
        "tc,te->ce", normed_cols, grad_joint, preferred_element_type=jnp.float32
    )
    output_part = jnp.einsum(
        "tc,te->ce", mixed_low, grad_branch, preferred_element_type=jnp.float32
    )
    bias_part = joint_bias_rows
    gain_part = gain_grad[:, None]
    shift_part = shift_grad[:, None]
    attn_share = lax.psum_scatter(
        jnp.concatenate([joint_part, output_part, bias_part, gain_part, shift_part], axis=1),
        ("ctx", "fsdp"),
        scatter_dimension=0,
        tiled=True,
    )
    share_rows = attn_share.shape[0]
    joint_share = attn_share[:, : 3 * width]
    output_share = attn_share[:, 3 * width : 4 * width]
    joint_bias_share = attn_share[:, 4 * width : 4 * width + 3].reshape(share_rows * 3)
    gain_share = attn_share[:, 4 * width + 3]
    shift_share = attn_share[:, 4 * width + 4]
    attention_parts = (gain_share, shift_share, joint_share, joint_bias_share, output_share)
    return (grad_out + grad_hidden, attention_parts, feed_parts)


def on_device(
    tokens,
    doc_lengths,
    keep_mask,
    ln_gain,
    ln_bias,
    qkv_weight,
    qkv_bias,
    out_weight,
    out_bias,
    up_weight,
    up_bias,
    down_weight,
    down_bias,
    cotangent,
):
    row_count = tokens.shape[1]
    position = lax.axis_index("ctx")
    query_index = position * row_count + jnp.arange(row_count, dtype=jnp.int32)
    lengths = doc_lengths[0]
    query_segment, query_position = place_tokens(query_index, lengths)
    cosine, sine = angles(query_position)
    key_keep = keep_mask[0].astype(jnp.bfloat16)
    shards = (
        ln_gain,
        ln_bias,
        qkv_weight,
        qkv_bias,
        out_weight,
        out_bias,
        up_weight,
        up_bias,
        down_weight,
        down_bias,
    )

    def fetch(layer_index):
        return (
            lax.all_gather(shards[0][layer_index], ("ctx", "fsdp"), axis=0, tiled=True),
            lax.all_gather(shards[1][layer_index], ("ctx", "fsdp"), axis=0, tiled=True),
            lax.all_gather(shards[2][layer_index], ("ctx", "fsdp"), axis=0, tiled=True),
            lax.all_gather(shards[3][layer_index], ("ctx", "fsdp"), axis=0, tiled=True),
            lax.all_gather(shards[4][layer_index], ("ctx", "fsdp"), axis=0, tiled=True),
            lax.all_gather(shards[5][layer_index], ("ctx", "fsdp"), axis=0, tiled=True),
            lax.all_gather(shards[6][layer_index], ("ctx", "fsdp"), axis=0, tiled=True),
            lax.all_gather(shards[7][layer_index], ("ctx", "fsdp"), axis=0, tiled=True),
            lax.all_gather(shards[8][layer_index], ("ctx", "fsdp"), axis=0, tiled=True),
            lax.all_gather(shards[9][layer_index], ("ctx", "fsdp"), axis=0, tiled=True),
        )

    hidden = tokens[0].astype(jnp.float32)
    saved_layers = []
    weights = None
    for layer_index in range(LAYERS):
        weights = fetch(layer_index)
        hidden, saved = layer_forward(
            hidden, weights, cosine, sine, key_keep, query_index, query_segment, lengths
        )
        saved_layers.append(saved)
    result = hidden.astype(jnp.bfloat16)[None]
    grad_hidden = cotangent[0].astype(jnp.float32) * keep_mask[0].astype(jnp.float32)[:, None]
    attention_list = [None] * LAYERS
    feed_list = [None] * LAYERS
    for layer_index in reversed(range(LAYERS)):
        weights = weights if layer_index == LAYERS - 1 else fetch(layer_index)
        grad_hidden, attention_parts, feed_parts = layer_backward(
            grad_hidden,
            saved_layers[layer_index],
            weights,
            cosine,
            sine,
            key_keep,
            query_index,
            query_segment,
            lengths,
        )
        attention_list[layer_index] = attention_parts
        feed_list[layer_index] = feed_parts
    gain_stack = jnp.stack([attention_list[layer_index][0] for layer_index in range(LAYERS)])
    shift_stack = jnp.stack([attention_list[layer_index][1] for layer_index in range(LAYERS)])
    joint_stack = jnp.stack([attention_list[layer_index][2] for layer_index in range(LAYERS)])
    joint_bias_stack = jnp.stack([attention_list[layer_index][3] for layer_index in range(LAYERS)])
    output_stack = jnp.stack([attention_list[layer_index][4] for layer_index in range(LAYERS)])
    upper_stack = jnp.stack([feed_list[layer_index][0] for layer_index in range(LAYERS)])
    upper_bias_stack = jnp.stack([feed_list[layer_index][1] for layer_index in range(LAYERS)])
    lower_stack = jnp.stack([feed_list[layer_index][2] for layer_index in range(LAYERS)])
    branch_stack = jnp.stack([feed_list[layer_index][3] for layer_index in range(LAYERS)])
    summed = (
        lax.psum(gain_stack.astype(jnp.bfloat16), "seq").astype(jnp.float32),
        lax.psum(shift_stack.astype(jnp.bfloat16), "seq").astype(jnp.float32),
        lax.psum(joint_stack.astype(jnp.bfloat16), "seq").astype(jnp.float32),
        lax.psum(joint_bias_stack.astype(jnp.bfloat16), "seq").astype(jnp.float32),
        lax.psum(output_stack.astype(jnp.bfloat16), "seq").astype(jnp.float32),
        lax.psum(upper_stack.astype(jnp.bfloat16), "seq").astype(jnp.float32),
        lax.psum(upper_bias_stack.astype(jnp.bfloat16), "seq").astype(jnp.float32),
        lax.psum(lower_stack.astype(jnp.bfloat16), "seq").astype(jnp.float32),
        lax.psum(branch_stack.astype(jnp.bfloat16), "seq").astype(jnp.float32),
    )
    return (
        result,
        grad_hidden[None],
        summed[0],
        summed[1],
        summed[2],
        summed[3],
        summed[4],
        summed[8],
        summed[5],
        summed[6],
        summed[7],
        summed[8],
    )


def solution(mesh):
    return jax.shard_map(
        on_device,
        mesh=mesh,
        in_specs=(
            P(("seq", "fsdp"), "ctx", None),
            P(("seq", "fsdp"), None),
            P(("seq", "fsdp"), "ctx"),
            P(None, ("ctx", "fsdp")),
            P(None, ("ctx", "fsdp")),
            P(None, ("ctx", "fsdp"), None),
            P(None, ("ctx", "fsdp")),
            P(None, ("ctx", "fsdp"), None),
            P(None, ("ctx", "fsdp")),
            P(None, ("ctx", "fsdp"), None),
            P(None, ("ctx", "fsdp")),
            P(None, ("ctx", "fsdp"), None),
            P(None, ("ctx", "fsdp")),
            P(("seq", "fsdp"), "ctx", None),
        ),
        out_specs=(
            P(("seq", "fsdp"), "ctx", None),
            P(("seq", "fsdp"), "ctx", None),
            P(None, ("ctx", "fsdp")),
            P(None, ("ctx", "fsdp")),
            P(None, ("ctx", "fsdp"), None),
            P(None, ("ctx", "fsdp")),
            P(None, ("ctx", "fsdp"), None),
            P(None, ("ctx", "fsdp")),
            P(None, ("ctx", "fsdp"), None),
            P(None, ("ctx", "fsdp")),
            P(None, ("ctx", "fsdp"), None),
            P(None, ("ctx", "fsdp")),
        ),
        check_vma=False,
    )
```

profile of v0, /device:TPU:0, one launch (start us, length us, event | category | flops | bytes accessed | tf_op | source)
XLA Modules:
  0.0 5768.3 jit_solution(15558921635551212047)
XLA Ops:
  11.3 34.6 all-gather.4
  74.4 30.5 all-gather.1
  105.6 45.0 all-gather.42.cloned.1.call-done
  196.1 31.4 all-gather.6
  257.5 31.6 all-gather.8
  317.6 30.5 all-gather.11
  450.6 44.3 all-gather.46.cloned.1.call-done
  513.0 161.7 %all-gather.48.cloned.1.call-done = bf16[1,8192,2048]{2,1,0:T(8,128)(2,1)} async-done(((bf16[1,512,2048]{2,1,0:T(8,128)(2,1)}), bf16[1,8192,2048]{2,1,0:T(8,128)(2,1)}) %all-gather.48.cloned.1.call-update) | async-done | bytes 33554448 | tf_op jit(solution)/shard_map/all_gather | solution.py:378
  695.2 116.9 %all-gather.50.cloned.1.call-done = bf16[1,2048,6144]{2,1,0:T(8,128)(2,1)} async-done(((bf16[1,128,6144]{2,1,0:T(8,128)(2,1)}), bf16[1,2048,6144]{2,1,0:T(8,128)(2,1)}) %all-gather.50.cloned.1.call-update) | async-done | bytes 25165840 | tf_op jit(solution)/shard_map/all_gather | solution.py:372
  868.7 30.8 all-gather.38.cloned.1.call-done
  1017.6 31.2 all-gather.18
  1066.1 89.3 %all-gather.54.cloned.1.call-done = bf16[1,2048,8192]{2,1,0:T(8,128)(2,1)} async-done(((bf16[1,128,8192]{2,1,0:T(8,128)(2,1)}), bf16[1,2048,8192]{2,1,0:T(8,128)(2,1)}) %all-gather.54.cloned.1.call-update) | async-done | bytes 33554448 | tf_op jit(solution)/shard_map/all_gather | solution.py:376
  1173.4 161.4 %all-gather.56.cloned.1.call-done = bf16[1,8192,2048]{2,1,0:T(8,128)(2,1)} async-done(((bf16[1,512,2048]{2,1,0:T(8,128)(2,1)}), bf16[1,8192,2048]{2,1,0:T(8,128)(2,1)}) %all-gather.56.cloned.1.call-update) | async-done | bytes 33554448 | tf_op jit(solution)/shard_map/all_gather | solution.py:378
  1397.8 31.2 reduce-scatter.11.cloned.1.call-done
  1541.8 68.5 %concatenate.110 = f32[2048,8197]{1,0:T(8,128)} concatenate(f32[2048,6144]{1,0:T(8,128)} %fusion.192, f32[2048,2048]{1,0:T(8,128)} %fusion.159, f32[2048,3]{1,0:T(8,128)} %reshape.431, f32[2048,1]{1,0:T(8,128)} %copy.69, f32[2048,1]{1,0:T(8,128)} %copy.70), dimensions={1} | concatenate | bytes 134299648 | tf_op jit(solution)/shard_map/concatenate | solution.py:317
  1743.3 78.1 %concatenate.109 = f32[2048,8197]{1,0:T(8,128)} concatenate(f32[2048,6144]{1,0:T(8,128)} %fusion.191, f32[2048,2048]{1,0:T(8,128)} %fusion.221, f32[2048,3]{1,0:T(8,128)} %reshape.430, f32[2048,1]{1,0:T(8,128)} %copy.66, f32[2048,1]{1,0:T(8,128)} %copy.67), dimensions={1} | concatenate | bytes 134299648 | tf_op jit(solution)/shard_map/concatenate | solution.py:317
  1850.9 79.8 %reshape.434 = f32[2048,8192]{1,0:T(8,128)} reshape(f32[8192,2048]{1,0:T(8,128)} %fusion.188) | data formatting | bytes 134217728 | tf_op jit(solution)/shard_map/reshape | solution.py:255
  1958.3 176.4 %concatenate.112 = f32[2048,16389]{1,0:T(8,128)} concatenate(f32[2048,8192]{1,0:T(8,128)} %fusion.222, f32[2048,8192]{1,0:T(8,128)} %reshape.434, f32[2048,4]{1,0:T(8,128)S(1)} %reshape.435, f32[2048,1]{1,0:T(8,128)S(1)} %copy.72), dimensions={1} | concatenate | bytes 268517376 | tf_op jit(solution)/shard_map/concatenate | solution.py:259
  2164.8 79.9 %reshape.432 = f32[2048,8192]{1,0:T(8,128)} reshape(f32[8192,2048]{1,0:T(8,128)} %fusion.196) | data formatting | bytes 134217728 | tf_op jit(solution)/shard_map/reshape | solution.py:255
  2272.0 182.4 %concatenate.111 = f32[2048,16389]{1,0:T(8,128)} concatenate(f32[2048,8192]{1,0:T(8,128)} %fusion.197, f32[2048,8192]{1,0:T(8,128)} %reshape.432, f32[2048,4]{1,0:T(8,128)S(1)} %reshape.433, f32[2048,1]{1,0:T(8,128)S(1)} %copy.71), dimensions={1} | concatenate | bytes 268517376 | tf_op jit(solution)/shard_map/concatenate | solution.py:259
  2458.4 460.6 %reduce-scatter.17.cloned.1.call-done = f32[128,8197]{1,0:T(8,128)} async-done(((f32[2048,8197]{1,0:T(8,128)}), f32[128,8197]{1,0:T(8,128)}) %reduce-scatter.17.cloned.1.call-update) | async-done | bytes 4196880 | tf_op jit(solution)/shard_map/reduce_scatter | solution.py:316
  2925.1 1252.2 %reduce-scatter.23.cloned.1.call-done = f32[128,16389]{1,0:T(8,128)} async-done(((f32[2048,16389]{1,0:T(8,128)}), f32[128,16389]{1,0:T(8,128)}) %reduce-scatter.23.cloned.1.call-update) | async-done | bytes 8391184 | tf_op jit(solution)/shard_map/reduce_scatter | solution.py:258
  4185.0 1249.6 %reduce-scatter.21.cloned.1.call-done = f32[128,16389]{1,0:T(8,128)} async-done(((f32[2048,16389]{1,0:T(8,128)}), f32[128,16389]{1,0:T(8,128)}) %reduce-scatter.21.cloned.1.call-update) | async-done | bytes 8391184 | tf_op jit(solution)/shard_map/reduce_scatter | solution.py:258
  5559.5 185.1 %all-reduce.4.cloned.1.call-done = (bf16[2,128,6144]{2,1,0:T(8,128)(2,1)}, bf16[2,128,2048]{2,1,0:T(8,128)(2,1)}, bf16[2,128,8192]{2,1,0:T(8,128)(2,1)}, bf16[2,512,2048]{2,1,0:T(8,128)(2,1)}) async-done(((bf16[2,128,6144]{2,1,0:T(8,128)(2,1)}, bf16[2,128,2048]{2,1,0:T(8,128)(2,1)}, bf16[2,128,8192]{2,1,0:T(8,128)(2,1)}, bf16[2,512,2048]{2,1,0:T(8,128)(2,1)}), (bf16[2,128,6144]{2,1,0:T(8,128)(2,1)}, ...) | async-done | bytes 12582928 | tf_op jit(solution)/shard_map/psum | solution.py:422
  (490 shorter events, 1068.8 us)
Async XLA Ops:
  7.2 143.4 %all-gather.42.cloned.1.call-start = ((), (), s32[]{:S(2)}) async-start(), calls=%async_computation.20 | async-start | bytes 26738688 | tf_op jit(solution)/shard_map/all_gather | solution.py:372
  11.2 374.7 %all-gather.36.cloned.1.call-start = ((), (), s32[]{:S(2)}) async-start(), calls=%async_computation.9 | async-start | bytes 5242880 | tf_op jit(solution)/shard_map/all_gather | solution.py:127
  74.3 420.5 %copy-start.60 = (f32[1,2048]{1,0:T(1,128)}, f32[1,2048]{1,0:T(1,128)S(1)}, u32[]{:S(2)}) copy-start(f32[1,2048]{1,0:T(1,128)S(1)} %convert_element_type.346) | copy-start | bytes 24580
  104.9 389.9 %copy-start.47 = (f32[1,2048]{1,0:T(1,128)}, f32[1,2048]{1,0:T(1,128)S(1)}, u32[]{:S(2)}) copy-start(f32[1,2048]{1,0:T(1,128)S(1)} %convert_element_type.345) | copy-start | bytes 24580
  166.3 226.2 %all-gather.34.cloned.1.call-start = ((), (), s32[]{:S(2)}) async-start(), calls=%async_computation.8 | async-start | bytes 5242880 | tf_op jit(solution)/shard_map/all_gather | solution.py:126
  168.0 672.0 %copy-start.64 = (f32[256,32]{0,1:T(8,128)}, f32[256,32]{0,1:T(8,128)S(1)}, u32[]{:S(2)}) copy-start(f32[256,32]{0,1:T(8,128)S(1)} %get-tuple-element.75) | copy-start | bytes 98308
  182.6 260.4 %all-gather.44.cloned.1.call-start = ((), (), s32[]{:S(2)}) async-start(), calls=%async_computation.21 | async-start | bytes 8912896 | tf_op jit(solution)/shard_map/all_gather | solution.py:374
  185.0 309.9 %all-gather.46.cloned.1.call-start = ((), (), s32[]{:S(2)}) async-start(), calls=%async_computation.22 | async-start | bytes 35651584 | tf_op jit(solution)/shard_map/all_gather | solution.py:376
  189.8 484.9 %all-gather.48.cloned.1.call-start = ((), (), s32[]{:S(2)}) async-start(), calls=%async_computation.23 | async-start | bytes 35651584 | tf_op jit(solution)/shard_map/all_gather | solution.py:378
  194.7 617.4 %all-gather.50.cloned.1.call-start = ((), (), s32[]{:S(2)}) async-start(), calls=%async_computation.24 | async-start | bytes 26738688 | tf_op jit(solution)/shard_map/all_gather | solution.py:372
  195.5 666.8 %all-gather.40.cloned.1.call-start = ((), (), s32[]{:S(2)}) async-start(), calls=%async_computation.11 | async-start | bytes 5242880 | tf_op jit(solution)/shard_map/all_gather | solution.py:127
  827.6 71.8 %all-gather.38.cloned.1.call-start = ((), (), s32[]{:S(2)}) async-start(), calls=%async_computation.10 | async-start | bytes 5242880 | tf_op jit(solution)/shard_map/all_gather | solution.py:126
  842.1 134.4 %all-gather.52.cloned.1.call-start = ((), (), s32[]{:S(2)}) async-start(), calls=%async_computation.25 | async-start | bytes 8912896 | tf_op jit(solution)/shard_map/all_gather | solution.py:374
  842.7 312.8 %all-gather.54.cloned.1.call-start = ((), (), s32[]{:S(2)}) async-start(), calls=%async_computation.26 | async-start | bytes 35651584 | tf_op jit(solution)/shard_map/all_gather | solution.py:376
  843.4 491.4 %all-gather.56.cloned.1.call-start = ((), (), s32[]{:S(2)}) async-start(), calls=%async_computation.27 | async-start | bytes 35651584 | tf_op jit(solution)/shard_map/all_gather | solution.py:378
  844.0 545.5 %reduce-scatter.9.cloned.1.call-start = ((), (), s32[]{:S(2)}) async-start(), calls=%async_computation.12 | async-start | bytes 5242880 | tf_op jit(solution)/shard_map/reduce_scatter | solution.py:159
  1016.9 412.0 %reduce-scatter.11.cloned.1.call-start = ((), (), s32[]{:S(2)}) async-start(), calls=%async_computation.13 | async-start | bytes 5242880 | tf_op jit(solution)/shard_map/reduce_scatter | solution.py:162
  1066.1 623.1 %reduce-scatter.13.cloned.1.call-start = ((), (), s32[]{:S(2)}) async-start(), calls=%async_computation.14 | async-start | bytes 5242880 | tf_op jit(solution)/shard_map/reduce_scatter | solution.py:159
  1487.9 206.6 %reduce-scatter.15.cloned.1.call-start = ((), (), s32[]{:S(2)}) async-start(), calls=%async_computation.15 | async-start | bytes 5242880 | tf_op jit(solution)/shard_map/reduce_scatter | solution.py:162
  1506.6 947.9 %reduce-scatter.19.cloned.1.call-start = ((), (), s32[]{:S(2)}) async-start(), calls=%async_computation.17 | async-start | bytes 72417280 | tf_op jit(solution)/shard_map/reduce_scatter | solution.py:316
  1610.4 1308.5 %reduce-scatter.17.cloned.1.call-start = ((), (), s32[]{:S(2)}) async-start(), calls=%async_computation.16 | async-start | bytes 72417280 | tf_op jit(solution)/shard_map/reduce_scatter | solution.py:316
  1821.4 2355.9 %reduce-scatter.23.cloned.1.call-start = ((), (), s32[]{:S(2)}) async-start(), calls=%async_computation.19 | async-start | bytes 143720448 | tf_op jit(solution)/shard_map/reduce_scatter | solution.py:258
  2134.7 3299.9 %reduce-scatter.21.cloned.1.call-start = ((), (), s32[]{:S(2)}) async-start(), calls=%async_computation.18 | async-start | bytes 143720448 | tf_op jit(solution)/shard_map/reduce_scatter | solution.py:258
  2454.4 3290.2 %all-reduce.4.cloned.1.call-start = ((), (), s32[]{:S(2)}) async-start(), calls=%async_computation.28 | async-start | bytes 25165824 | tf_op jit(solution)/shard_map/psum | solution.py:422
  (121 other events, 4964.2 us)
Sparse Core Ops, SparseCore 0:
  11.4 139.2 all-gather.41
  166.4 34.4 all-gather.35
  203.0 35.0 all-gather.33
  240.7 75.1 all-gather.43
  317.9 176.8 all-gather.45
  496.8 177.8 all-gather.47
  676.3 135.7 all-gather.49
  827.8 34.4 all-gather.39
  864.4 35.0 all-gather.37
  901.5 74.8 all-gather.51
  978.6 176.8 all-gather.53
  1156.9 177.8 all-gather.55
  1337.3 44.4 reduce-scatter.8
  1384.4 44.4 reduce-scatter.10
  1488.0 44.4 reduce-scatter.12
  1535.1 44.4 reduce-scatter.14
  1610.5 656.7 reduce-scatter.18
  2272.0 646.9 reduce-scatter.16
  2923.2 1254.0 reduce-scatter.22
  4182.0 1252.6 reduce-scatter.20
  5455.3 289.2 all-reduce.3
where the time goes:
time: 5800 us; the launch traced here: 5770 us
  waiting for transfers between devices  3880 us (67%)
  local copies, waits for them, and re-layouts  773 us (13%)
  matrix products  619 us (11%)
  blocking collectives  373 us (6%)
  other arithmetic  111 us (2%)
    reduce_scatter x2, waiting for transfers between devices, layer_backward(): lax.psum_scatter(jnp.concatenate([upper_part, lower_part, bias_part, bran...  2500 us
    reduce_scatter x2, waiting for transfers between devices, layer_backward(): lax.psum_scatter(jnp.concatenate([joint_part, output_part, bias_part, gai...  461 us
    concatenate x2, local copies, waits for them, and re-layouts, layer_backward(): jnp.concatenate([upper_part, lower_part, bias_part, branch_part], axis=1)  359 us
    all_gather x2, waiting for transfers between devices, fetch(): lax.all_gather(shards[8][layer_index], ('ctx', 'fsdp'), axis=0, tiled=True)  323 us
    psum x1, waiting for transfers between devices, on_device(): lax.psum(joint_stack.astype(jnp.bfloat16), 'seq').astype(jnp.float32)  185 us
    all_gather x2, waiting for transfers between devices, fetch(): lax.all_gather(shards[2][layer_index], ('ctx', 'fsdp'), axis=0, tiled=True)  162 us
    reshape x2, local copies, waits for them, and re-layouts, layer_backward(): lower_part = jnp.einsum('tc,td->cd', activated, grad_branch, preferred_el...  160 us
    concatenate x2, local copies, waits for them, and re-layouts, layer_backward(): jnp.concatenate([joint_part, output_part, bias_part, gain_part, shift_par...  147 us
  transfers between devices with their start and end apart: 21, of which 14 were waited for; matrix products, arithmetic and copies ran while one was open for 24% of the time, Pallas kernels for 0%

commit v1 on v0

--- a/solution.py
+++ b/solution.py
@@ -3,7 +3,10 @@
 
 import jax
 import jax.numpy as jnp
+import numpy as np
 from jax import lax
+from jax.experimental import pallas as pl
+from jax.experimental.pallas import tpu as pltpu
 from jax.sharding import PartitionSpec as P
 
 D = 2048
@@ -329,7 +332,7 @@
     return (grad_out + grad_hidden, attention_parts, feed_parts)
 
 
-def on_device(
+def on_device_gathered(
     tokens,
     doc_lengths,
     keep_mask,
@@ -443,7 +446,1625 @@
     )
 
 
+SIDE = 4
+GROUP = SIDE * SIDE
+OWN = HEADS // GROUP
+HEAD_COLS = OWN * HEAD_DIM
+JOINT_COLS = 3 * HEAD_COLS
+FEED_COLS = FF // GROUP
+COLS = JOINT_COLS + FEED_COLS
+BACK_COLS = HEAD_COLS + FEED_COLS
+SHARE = D // GROUP
+VMEM = pl.BlockSpec(memory_space=pltpu.VMEM)
+HBM = pl.BlockSpec(memory_space=pl.ANY)
+MESH = pl.DeviceIdType.MESH
+ROOM = 60 * 2**20
+
+
+def dot(left, right, left_dim=1, right_dim=0):
+    return lax.dot_general(
+        left, right, (((left_dim,), (right_dim,)), ((), ())), preferred_element_type=jnp.float32
+    )
+
+
+def digit(entries, index):
+    words = [
+        sum(entry << (2 * place) for place, entry in enumerate(entries[start : start + 8]))
+        for start in range(0, len(entries), 8)
+    ]
+    word = jnp.int32(words[0])
+    for number in range(1, len(words)):
+        word = jnp.where(index >= 8 * number, jnp.int32(words[number]), word)
+    return lax.rem(lax.shift_right_logical(word, 2 * lax.rem(index, 8)), 4)
+
+
+def digit_of_row(table, row, index):
+    value = digit(table[0], index)
+    for number in range(1, len(table)):
+        value = jnp.where(row == number, digit(table[number], index), value)
+    return value
+
+
+NEAR = ((0, 1, 2, 3), (1, 0, 2, 3), (2, 3, 1, 0), (3, 2, 1, 0))
+FAR = ((3, 2, 1, 0), (3, 0, 2, 1), (0, 3, 1, 2), (0, 1, 2, 3))
+
+
+def neighbours():
+    ctx, place = lax.axis_index("ctx"), lax.axis_index("fsdp")
+    twin = ctx + 1 - 2 * lax.rem(ctx, 2)
+    across = lax.rem(ctx + 2, 4)
+    return ctx, place, twin, across, lax.rem(twin + 2, 4)
+
+
+def greet_neighbours():
+    ctx, place, twin, across, _ = neighbours()
+    barrier = pltpu.get_barrier_semaphore()
+    pl.semaphore_signal(barrier, inc=1, device_id={"ctx": twin}, device_id_type=MESH)
+    pl.semaphore_signal(barrier, inc=1, device_id={"ctx": across}, device_id_type=MESH)
+
+    @pl.when(place > 0)
+    def _():
+        pl.semaphore_signal(barrier, inc=1, device_id={"fsdp": place - 1}, device_id_type=MESH)
+
+    @pl.when(place < SIDE - 1)
+    def _():
+        pl.semaphore_signal(barrier, inc=1, device_id={"fsdp": place + 1}, device_id_type=MESH)
+
+    inner = jnp.int32(2) + jnp.where(place > 0, 1, 0) + jnp.where(place < SIDE - 1, 1, 0)
+    pl.semaphore_wait(barrier, inner)
+
+
+def greet_plane(steps, cross=True):
+    ctx, place = lax.axis_index("ctx"), lax.axis_index("fsdp")
+    me = ctx * SIDE + place
+    barrier = pltpu.get_barrier_semaphore()
+    for step in range(1, steps):
+        peer = lax.rem(me + step, GROUP)
+        pl.semaphore_signal(
+            barrier,
+            inc=1,
+            device_id={"ctx": peer // SIDE, "fsdp": lax.rem(peer, SIDE)},
+            device_id_type=MESH,
+        )
+    if cross:
+        pl.semaphore_signal(
+            barrier, inc=1, device_id={"seq": 1 - lax.axis_index("seq")}, device_id_type=MESH
+        )
+    pl.semaphore_wait(barrier, steps if cross else steps - 1)
+
+
+def to_peer(source, target, send, recv, peer):
+    return pltpu.make_async_remote_copy(
+        src_ref=source,
+        dst_ref=target,
+        send_sem=send,
+        recv_sem=recv,
+        device_id={"ctx": peer // SIDE, "fsdp": lax.rem(peer, SIDE)},
+        device_id_type=MESH,
+    )
+
+
+def to_axis(source, target, send, recv, axis, index):
+    return pltpu.make_async_remote_copy(
+        src_ref=source,
+        dst_ref=target,
+        send_sem=send,
+        recv_sem=recv,
+        device_id={axis: index},
+        device_id_type=MESH,
+    )
+
+
+PARTS = ((0, 112), (112, 96), (208, 48))
+LAST = len(PARTS) - 1
+GATHER_KIND = (
+    (0, 0, 0, 0, 0, 1, 0, 0, 1, 0, 2, 0, 1, 1, 1, 2, 0, 0, 1, 0, 1, 3, 2, 1, 0, 3, 1, 1, 1, 1, 0, 3, 0, 0, 1, 1, 1, 1, 2, 3),
+    (0, 0, 0, 1, 0, 0, 0, 0, 0, 0, 0, 0, 1, 0, 2, 1, 2, 1, 0, 1, 1, 2, 0, 3, 1, 1, 0, 1, 1, 1, 3, 1, 1, 0, 1, 3, 1, 1, 2, 3),
+)
+GATHER_STEP = (
+    (0, 0, 1, 0, 0, 0, 1, 1, 0, 1, 0, 2, 0, 0, 1, 1, 2, 2, 1, 2, 1, 0, 2, 1, 3, 1, 2, 2, 2, 2, 3, 2, 3, 3, 3, 3, 3, 3, 3, 3),
+    (0, 0, 0, 0, 2, 2, 1, 0, 1, 2, 1, 1, 0, 2, 0, 0, 2, 0, 3, 2, 2, 1, 3, 0, 2, 1, 3, 1, 2, 1, 2, 3, 1, 3, 3, 1, 3, 3, 3, 3),
+)
+GATHER_PART = (
+    (1, 0, 1, 2, 3, 1, 2, 0, 0, 3, 3, 2, 2, 3, 0, 3, 1, 0, 1, 3, 2, 3, 3, 3, 0, 3, 1, 2, 0, 3, 1, 3, 2, 3, 1, 0, 2, 3, 3, 3),
+    (1, 0, 2, 0, 2, 0, 2, 3, 1, 1, 0, 3, 2, 3, 3, 1, 3, 3, 0, 0, 2, 3, 1, 3, 1, 1, 2, 2, 3, 0, 3, 2, 3, 3, 0, 3, 1, 3, 3, 3),
+)
+OPS = len(GATHER_KIND[0])
+WORKS = tuple(
+    tuple(
+        number for number in range(OPS) if parts[number] == 3
+    )
+    for parts in GATHER_PART
+)
+
+
+def by_place(tables, index):
+    place = lax.axis_index("fsdp")
+    at_end = (place == 0) | (place == SIDE - 1)
+    return jnp.where(at_end, digit(tables[0], index), digit(tables[1], index))
+
+
+def gather_slot(kind, step):
+    ctx, place, twin, across, twin_across = neighbours()
+    line = digit_of_row(NEAR, place, step)
+    owner = jnp.where(
+        kind == 0, ctx, jnp.where(kind == 1, across, jnp.where(kind == 2, twin, twin_across))
+    )
+    return line, owner * SIDE + line
+
+
+def work_slot(number):
+    kind = by_place(
+        tuple(tuple(row[at] for at in places) for row, places in zip(GATHER_KIND, WORKS)), number
+    )
+    step = by_place(
+        tuple(tuple(row[at] for at in places) for row, places in zip(GATHER_STEP, WORKS)), number
+    )
+    return gather_slot(kind, step)[1]
+
+
+def gather_blocks(land, every, up, down, side, core, arrived, core_arrived, kept, work):
+    ctx, place, twin, across, _ = neighbours()
+
+    def copies(kind, line, slot, part):
+        start, size = PARTS[part]
+        block = land.at[slot, pl.ds(start, size)]
+        row, met = kind * SIDE + line, arrived.at[slot, part]
+        return (
+            lambda: to_axis(block, block, up.at[row, part], met, "fsdp", place + 1),
+            lambda: to_axis(block, block, down.at[row, part], met, "fsdp", place - 1),
+            lambda: to_axis(block, block, side.at[line, part], met, "ctx", across),
+        )
+
+    def routes(kind, line, part):
+        goes_up = (line <= place) & (place < SIDE - 1)
+        goes_down = (line >= place) & (place > 0)
+        if part == LAST:
+            return goes_up, goes_down, (kind == 0) & (line == place)
+        return goes_up & (kind == 0), goes_down & (kind == 0), kind == 0
+
+    def core_copy(kind, line, slot):
+        block = land.at[slot]
+        return to_axis(
+            block, block, core.at[kind * SIDE + line], core_arrived.at[slot], "ctx", twin
+        )
+
+    def step_op(number, worked):
+        kind, step = by_place(GATHER_KIND, number), by_place(GATHER_STEP, number)
+        part = by_place(GATHER_PART, number)
+        line, slot = gather_slot(kind, step)
+        for which in range(len(PARTS)):
+
+            @pl.when(part == which)
+            def _(which=which):
+                @pl.when((kind == 1) | (line != place))
+                def _():
+                    copies(kind, line, slot, which)[2]().wait_recv()
+
+                for copy, goes in zip(
+                    copies(kind, line, slot, which), routes(kind, line, which)
+                ):
+
+                    @pl.when(goes)
+                    def _(copy=copy):
+                        copy().start()
+
+        @pl.when(part == 3)
+        def _():
+            @pl.when(kind <= 1)
+            def _():
+                core_copy(kind, line, slot).start()
+
+            @pl.when(kind >= 2)
+            def _():
+                core_copy(kind - 2, line, slot).wait_recv()
+
+            if every is not None:
+                pltpu.make_async_copy(land.at[slot], every.at[slot], kept.at[slot]).start()
+            work(worked, slot)
+
+        return worked + jnp.where(part == 3, 1, 0)
+
+    lax.fori_loop(0, OPS, step_op, jnp.int32(0))
+
+    def finish(number, carry):
+        kind, line = number // SIDE, lax.rem(number, SIDE)
+        slot = jnp.where(kind == 0, ctx, across) * SIDE + line
+        for which in range(len(PARTS)):
+            for copy, goes in zip(copies(kind, line, slot, which), routes(kind, line, which)):
+
+                @pl.when(goes)
+                def _(copy=copy):
+                    copy().wait_send()
+
+        core_copy(kind, line, slot).wait_send()
+        return carry
+
+    lax.fori_loop(0, 2 * SIDE, finish, 0)
+
+    def finish_kept(slot, carry):
+        pltpu.make_async_copy(land.at[slot], every.at[slot], kept.at[slot]).wait()
+        return carry
+
+    if every is not None:
+        lax.fori_loop(0, GROUP, finish_kept, 0)
+
+
+def gather_scratch(rows):
+    parts = len(PARTS)
+    return [
+        pltpu.VMEM((GROUP, rows, D), jnp.bfloat16),
+        pltpu.SemaphoreType.DMA((2 * SIDE, parts)),
+        pltpu.SemaphoreType.DMA((2 * SIDE, parts)),
+        pltpu.SemaphoreType.DMA((SIDE, parts)),
+        pltpu.SemaphoreType.DMA((2 * SIDE,)),
+        pltpu.SemaphoreType.DMA((GROUP, parts)),
+        pltpu.SemaphoreType.DMA((GROUP,)),
+        pltpu.SemaphoreType.DMA((GROUP,)),
+    ]
+
+
+def spin(values, cosine, sine, sign):
+    lane = lax.rem(lax.broadcasted_iota(jnp.int32, values.shape, 1), HEAD_DIM)
+    partner = jnp.where(
+        lane < ROT // 2,
+        -pltpu.roll(values, HEAD_COLS - ROT // 2, 1),
+        pltpu.roll(values, ROT // 2, 1),
+    )
+    return values * cosine + sign * (partner * sine)
+
+
+STRIP = 32
+
+
+def each_strip(rows, body, start):
+    def step(number, carry):
+        return body(pl.ds(pl.multiple_of(number * STRIP, STRIP), STRIP), carry)
+
+    return lax.fori_loop(0, rows // STRIP, step, start)
+
+
+def column_places(block):
+    return [
+        (0, pl.multiple_of(part * D + block * HEAD_COLS, HEAD_COLS), part * HEAD_COLS, HEAD_COLS)
+        for part in range(3)
+    ] + [(1, pl.multiple_of(block * FEED_COLS, FEED_COLS), JOINT_COLS, FEED_COLS)]
+
+
+PLACES = 4
+
+
+def forward_gather(hidden, gain, shift, bias, turns, sources, layer):
+    rows = hidden.shape[0]
+    half = SHARE // 2
+    first = layer == 0
+
+    def kernel(hidden, gain, shift, bias, turn_a, turn_b, source_a, source_b, *refs):
+        every, columns_out, query, key, value, inner, active = refs[:7]
+        refs = refs[7:]
+        if first:
+            cosine, sine = refs[:2]
+            refs = refs[2:]
+        else:
+            cosine, sine = turn_a, turn_b
+        columns, plane_send, plane_recv, cross_send, cross_recv, own_sem, saved = refs[:7]
+        land = refs[7]
+        ctx, place, seq = lax.axis_index("ctx"), lax.axis_index("fsdp"), lax.axis_index("seq")
+        me = ctx * SIDE + place
+        part_rows = pl.ds(pl.multiple_of(seq * half, half), half)
+        other_rows = pl.ds(pl.multiple_of((1 - seq) * half, half), half)
+        if first:
+            greet_plane(GROUP)
+        else:
+            greet_neighbours()
+        sources = (source_a, source_b)
+        halves = ()
+        if not first:
+            halves = (
+                pltpu.make_async_copy(source_a, columns.at[:, part_rows], own_sem.at[0]),
+                pltpu.make_async_copy(source_b, columns.at[:, other_rows], own_sem.at[1]),
+            )
+
+        def piece(step, number):
+            peer = lax.rem(me + step, GROUP)
+            which, start, at, width = column_places(peer)[number]
+            return (
+                peer,
+                sources[which].at[layer, part_rows, pl.ds(start, width)],
+                columns.at[me, part_rows, pl.ds(at, width)],
+            )
+
+        def send_piece(step, number):
+            peer, source, target = piece(step, number)
+            return to_peer(
+                source, target, plane_send.at[step, number], plane_recv.at[me, number], peer
+            )
+
+        def own_piece(number):
+            _, source, target = piece(0, number)
+            return pltpu.make_async_copy(source, target, own_sem.at[number])
+
+        def cross(source):
+            block = columns.at[source, part_rows]
+            return to_axis(
+                block, block, cross_send.at[source], cross_recv.at[source], "seq", 1 - seq
+            )
+
+        if first:
+            for number in range(PLACES):
+                own_piece(number).start()
+        else:
+            for copy in halves:
+                copy.start()
+
+        def send_columns(step, carry):
+            for number in range(PLACES):
+                send_piece(step, number).start()
+            return carry
+
+        def strip(part, carry):
+            values = hidden[part].astype(jnp.float32)
+            centred = values - jnp.mean(values, axis=1, keepdims=True)
+            spread = jnp.mean(centred * centred, axis=1, keepdims=True)
+            normed = centred * lax.rsqrt(spread + EPS) * gain[...] + shift[...]
+            land[me, part] = normed.astype(jnp.bfloat16)
+            return carry
+
+        each_strip(rows, strip, 0)
+
+        def pass_on(step):
+            source = lax.rem(me + GROUP - step, GROUP)
+
+            @pl.when(step == 0)
+            def _():
+                for number in range(PLACES):
+                    own_piece(number).wait()
+
+            @pl.when(step > 0)
+            def _():
+                for number in range(PLACES):
+                    _, _, at, width = column_places(0)[number]
+                    target = columns.at[source, part_rows, pl.ds(at, width)]
+                    to_peer(
+                        target, target, plane_send.at[0, number], plane_recv.at[source, number], source
+                    ).wait_recv()
+
+            cross(source).start()
+
+        def product(slot):
+            whole = dot(land[slot], columns[...].reshape(D, COLS)) + bias[...]
+            one, two = HEAD_COLS, 2 * HEAD_COLS
+            query[slot] = spin(whole[:, :one], cosine[slot], sine[slot], 1.0).astype(jnp.bfloat16)
+            key[slot] = spin(whole[:, one:two], cosine[slot], sine[slot], 1.0).astype(jnp.bfloat16)
+            value[slot] = whole[:, two:JOINT_COLS].astype(jnp.bfloat16)
+            units = whole[:, JOINT_COLS:]
+            inner[slot] = units
+            active[slot] = jax.nn.gelu(units, approximate=True).astype(jnp.bfloat16)
+
+        save = pltpu.make_async_copy(columns, columns_out, saved)
+
+        def work_as_columns_come(number, slot):
+            @pl.when(number == 0)
+            def _():
+                lax.fori_loop(1, GROUP, send_columns, 0)
+
+            angle = turn_a[slot] * turn_b[...]
+            cosine[slot] = jnp.cos(angle)
+            sine[slot] = jnp.sin(angle)
+
+            @pl.when(number < GROUP // 2)
+            def _():
+                pass_on(2 * number)
+                pass_on(2 * number + 1)
+
+            @pl.when(number == GROUP // 2)
+            def _():
+                def arrive(source, carry):
+                    block = columns.at[source, part_rows]
+                    to_axis(
+                        block, block, cross_send.at[source], cross_recv.at[source], "seq", 1 - seq
+                    ).wait_recv()
+                    return carry
+
+                lax.fori_loop(0, GROUP, arrive, 0)
+                save.start()
+
+            @pl.when(number >= GROUP // 2)
+            def _():
+                def two_products(more, carry):
+                    product(work_slot(2 * number - GROUP + more))
+                    return carry
+
+                lax.fori_loop(0, 2, two_products, 0)
+
+        def work(number, slot):
+            @pl.when(number == 0)
+            def _():
+                for copy in halves:
+                    copy.wait()
+                save.start()
+
+            product(slot)
+
+        gather_blocks(land, every, *refs[8:], work_as_columns_come if first else work)
+        save.wait()
+
+        def end(step, carry):
+            cross(step).wait_send()
+
+            @pl.when(step > 0)
+            def _():
+                for number in range(PLACES):
+                    send_piece(step, number).wait_send()
+
+            return carry
+
+        if first:
+            lax.fori_loop(0, GROUP, end, 0)
+
+    def out(width, dtype):
+        return jax.ShapeDtypeStruct((GROUP, rows, width), dtype)
+
+    out_shape = [
+        out(D, jnp.bfloat16),
+        jax.ShapeDtypeStruct((GROUP, SHARE, COLS), jnp.bfloat16),
+        out(HEAD_COLS, jnp.bfloat16),
+        out(HEAD_COLS, jnp.bfloat16),
+        out(HEAD_COLS, jnp.bfloat16),
+        out(FEED_COLS, jnp.float32),
+        out(FEED_COLS, jnp.bfloat16),
+    ] + [out(HEAD_COLS, jnp.float32)] * (2 if first else 0)
+    return pl.pallas_call(
+        kernel,
+        out_shape=out_shape,
+        in_specs=[VMEM] * 6 + [HBM] * 2,
+        out_specs=[HBM, HBM] + [VMEM] * (len(out_shape) - 2),
+        scratch_shapes=[
+            pltpu.VMEM((GROUP, SHARE, COLS), jnp.bfloat16),
+            pltpu.SemaphoreType.DMA((GROUP, PLACES)),
+            pltpu.SemaphoreType.DMA((GROUP, PLACES)),
+            pltpu.SemaphoreType.DMA((GROUP,)),
+            pltpu.SemaphoreType.DMA((GROUP,)),
+            pltpu.SemaphoreType.DMA((PLACES,)),
+            pltpu.SemaphoreType.DMA,
+        ]
+        + gather_scratch(rows),
+        compiler_params=pltpu.CompilerParams(
+            collective_id=30 + layer, has_side_effects=True, vmem_limit_bytes=ROOM
+        ),
+    )(hidden, gain, shift, bias, *turns, *sources)
+
+
+def backward_gather(grad, out_weight, down_weight, inner, mixed, active):
+    rows = grad.shape[0]
+
+    def kernel(
+        own,
+        out_weight,
+        down_weight,
+        inner,
+        mixed,
+        active,
+        grad_mixed,
+        grad_inner,
+        branch,
+        total,
+        land,
+        *sems,
+    ):
+        ctx, place, _, _, _ = neighbours()
+        greet_neighbours()
+        land[ctx * SIDE + place] = own[...]
+        total[...] = jnp.zeros_like(total)
+
+        def work(number, slot):
+            block = land[slot]
+            grad_mixed[slot] = dot(block, out_weight[...], 1, 1)
+            value = inner[slot]
+            factor = math.sqrt(2.0 / math.pi)
+            square = value * value
+            bend = jnp.tanh(factor * value * (1.0 + 0.044715 * square))
+            slope = 0.5 * (1.0 + bend) + 0.5 * value * (1.0 - bend * bend) * (
+                factor * (1.0 + 3 * 0.044715 * square)
+            )
+            grad_inner[slot] = (dot(block, down_weight[...], 1, 1) * slope).astype(jnp.bfloat16)
+            total[:HEAD_COLS] += dot(mixed[slot], block, 0, 0)
+            total[HEAD_COLS:] += dot(active[slot], block, 0, 0)
+
+        gather_blocks(land, None, *sems, work)
+        branch[...] = total[...].astype(jnp.bfloat16)
+
+    return pl.pallas_call(
+        kernel,
+        out_shape=(
+            jax.ShapeDtypeStruct((GROUP, rows, HEAD_COLS), jnp.float32),
+            jax.ShapeDtypeStruct((GROUP, rows, FEED_COLS), jnp.bfloat16),
+            jax.ShapeDtypeStruct((BACK_COLS, D), jnp.bfloat16),
+        ),
+        in_specs=[VMEM] * 6,
+        out_specs=(VMEM, VMEM, VMEM),
+        scratch_shapes=[pltpu.VMEM((BACK_COLS, D), jnp.float32)] + gather_scratch(rows),
+        compiler_params=pltpu.CompilerParams(
+            collective_id=4, has_side_effects=True, vmem_limit_bytes=ROOM
+        ),
+    )(grad, out_weight, down_weight, inner, mixed, active)
+
+
+SCATTER_OPS = (
+    ((0, 0), (0, 1), (1, 0), (2, 0), (1, 1), (0, 2), (2, 1), (3, 0), (1, 2), (2, 2), (4, 0), (6, 0), (5, 0), (0, 3), (3, 1), (3, 2), (1, 3), (3, 3), (4, 1), (5, 1), (6, 1), (4, 2), (5, 2), (6, 2), (2, 3), (4, 3), (5, 3), (6, 3)),
+    ((0, 0), (0, 2), (3, 2), (1, 0), (3, 0), (0, 1), (0, 3), (1, 1), (2, 0), (1, 2), (3, 1), (1, 3), (4, 0), (6, 0), (5, 0), (3, 3), (2, 1), (2, 2), (4, 1), (6, 1), (5, 1), (4, 2), (5, 2), (6, 2), (2, 3), (4, 3), (5, 3), (6, 3)),
+)
+SCATTER_OPS_WORK = (
+    ((0, 0), (0, 1), (1, 0), (2, 0), (1, 1), (0, 2), (2, 1), (3, 0), (1, 2), (2, 2), (4, 0), (6, 0), (7, 0), (5, 0), (0, 3), (3, 1), (3, 2), (1, 3), (3, 3), (4, 1), (7, 0), (5, 1), (7, 0), (7, 0), (7, 0), (7, 0), (7, 0), (6, 1), (4, 2), (7, 0), (5, 2), (7, 0), (7, 0), (7, 0), (6, 2), (2, 3), (7, 0), (7, 0), (7, 0), (7, 0), (7, 0), (4, 3), (5, 3), (6, 3)),
+    ((0, 0), (0, 2), (3, 2), (1, 0), (3, 0), (7, 0), (0, 1), (0, 3), (1, 1), (2, 0), (1, 2), (3, 1), (7, 0), (7, 0), (1, 3), (4, 0), (6, 0), (7, 0), (5, 0), (7, 0), (7, 0), (3, 3), (2, 1), (7, 0), (2, 2), (7, 0), (7, 0), (4, 1), (6, 1), (5, 1), (4, 2), (5, 2), (7, 0), (7, 0), (7, 0), (6, 2), (7, 0), (7, 0), (7, 0), (2, 3), (7, 0), (4, 3), (5, 3), (6, 3)),
+)
+SCATTER_OPS_EARLY = (
+    ((0, 0), (0, 1), (1, 0), (2, 0), (0, 2), (1, 1), (2, 1), (3, 0), (1, 2), (2, 2), (4, 0), (6, 0), (7, 0), (5, 0), (0, 3), (7, 0), (7, 0), (3, 1), (3, 2), (3, 3), (4, 1), (7, 0), (5, 1), (7, 0), (7, 0), (6, 1), (1, 3), (7, 0), (4, 2), (7, 0), (7, 0), (5, 2), (7, 0), (7, 0), (7, 0), (6, 2), (7, 0), (7, 0), (7, 0), (7, 0), (2, 3), (4, 3), (5, 3), (6, 3)),
+    ((0, 1), (0, 0), (1, 1), (0, 3), (1, 0), (0, 2), (3, 0), (1, 2), (2, 0), (7, 0), (1, 3), (3, 3), (2, 2), (3, 1), (3, 2), (4, 0), (7, 0), (6, 0), (7, 0), (2, 1), (2, 3), (7, 0), (5, 0), (7, 0), (7, 0), (4, 1), (7, 0), (7, 0), (6, 1), (7, 0), (7, 0), (5, 1), (4, 2), (5, 2), (7, 0), (7, 0), (7, 0), (7, 0), (7, 0), (7, 0), (6, 2), (4, 3), (5, 3), (6, 3)),
+)
+SPLIT = ((0, 208), (208, 48))
+
+
+def nibble(entries, index):
+    word = jnp.int32(0)
+    for start in range(0, len(entries), 7):
+        packed = sum(entry << (4 * place) for place, entry in enumerate(entries[start : start + 7]))
+        word = jnp.where(index >= start, jnp.int32(packed), word)
+    return lax.rem(lax.shift_right_logical(word, 4 * lax.rem(index, 7)), 16)
+
+
+def scatter_events(partial, other_work, ops, scratch):
+    total, give, take, side_take, line_take, other_take = scratch[:6]
+    core_send, core_recv, side_send, side_recv, line_send, line_recv = scratch[6:12]
+    other_send, other_recv = scratch[12:]
+    ctx, place, twin, across, twin_across = neighbours()
+    below, above = place - 1, place + 1
+    has_below, has_above = place > 0, place < SIDE - 1
+    at_end = (place == 0) | (place == SIDE - 1)
+
+    def rows_of(part):
+        return pl.ds(*SPLIT[part])
+
+    def core_copy(step, store):
+        return to_axis(
+            give.at[step], take.at[store], core_send.at[store], core_recv.at[store], "ctx", twin
+        )
+
+    def side_copy(step, part):
+        return to_axis(
+            take.at[step, rows_of(part)],
+            side_take.at[step, rows_of(part)],
+            side_send.at[step, part],
+            side_recv.at[step, part],
+            "ctx",
+            across,
+        )
+
+    def line_copy(step, line, slot, target, part):
+        return to_axis(
+            take.at[SIDE + step, rows_of(part)],
+            line_take.at[slot, rows_of(part)],
+            line_send.at[line, part],
+            line_recv.at[slot, part],
+            "fsdp",
+            target,
+        )
+
+    def other_copy(step, line, slot, target):
+        return to_axis(
+            take.at[step, rows_of(1)],
+            other_take.at[slot],
+            other_send.at[line],
+            other_recv.at[slot],
+            "fsdp",
+            target,
+        )
+
+    def from_above(line):
+        return jnp.where(line == place, SIDE, line)
+
+    def to_below(line):
+        return jnp.where(line == place - 1, SIDE, line)
+
+    def one(number, turn):
+        def by_end(field):
+            ends, middle = (tuple(entry[field] for entry in table) for table in ops)
+            return jnp.where(at_end, nibble(ends, number), nibble(middle, number))
+
+        what, step = by_end(0), by_end(1)
+        line = digit_of_row(FAR, place, step)
+
+        @pl.when((what <= 1) | (what == 3) | (what == 4))
+        def _():
+            owner = jnp.where(
+                what == 0,
+                twin_across,
+                jnp.where(what == 1, across, jnp.where(what == 3, twin, ctx)),
+            )
+            total[...] = partial(owner * SIDE + line)
+
+        @pl.when(what == 0)
+        def _():
+            give[step] = total[...].astype(jnp.bfloat16)
+            core_copy(step, step).start()
+
+        @pl.when(what == 1)
+        def _():
+            core_copy(step, step).wait_recv()
+            take[step] = (total[...] + take[step].astype(jnp.float32)).astype(jnp.bfloat16)
+            side_copy(step, 0).start()
+
+        @pl.when(what == 2)
+        def _():
+            rows = rows_of(1)
+
+            @pl.when((line >= place) & has_below)
+            def _():
+                other_copy(step, line, line, below).wait_recv()
+                take[step, rows] = (
+                    take[step, rows].astype(jnp.float32) + other_take[line].astype(jnp.float32)
+                ).astype(jnp.bfloat16)
+
+            @pl.when((line <= place) & has_above)
+            def _():
+                other_copy(step, line, from_above(line), above).wait_recv()
+                take[step, rows] = (
+                    take[step, rows].astype(jnp.float32)
+                    + other_take[from_above(line)].astype(jnp.float32)
+                ).astype(jnp.bfloat16)
+
+            @pl.when(line > place)
+            def _():
+                other_copy(step, line, line, above).start()
+
+            @pl.when(line < place)
+            def _():
+                other_copy(step, line, to_below(line), below).start()
+
+            @pl.when(line == place)
+            def _():
+                side_copy(step, 1).start()
+
+        @pl.when(what == 3)
+        def _():
+            core_copy(step, step).wait_send()
+            give[step] = total[...].astype(jnp.bfloat16)
+            core_copy(step, SIDE + step).start()
+
+        @pl.when(what == 4)
+        def _():
+            core_copy(step, SIDE + step).wait_recv()
+            total[...] += take[SIDE + step].astype(jnp.float32)
+
+        for part in range(2):
+            rows = rows_of(part)
+
+            @pl.when(what == 5 + part)
+            def _(rows=rows, part=part):
+                crossed = line == place if part == 1 else line >= 0
+
+                @pl.when(crossed)
+                def _():
+                    side_copy(step, part).wait_recv()
+                    total[rows] += side_take[step, rows].astype(jnp.float32)
+
+                @pl.when((line >= place) & has_below)
+                def _():
+                    line_copy(step, line, line, below, part).wait_recv()
+                    total[rows] += line_take[line, rows].astype(jnp.float32)
+
+                @pl.when((line <= place) & has_above)
+                def _():
+                    line_copy(step, line, from_above(line), above, part).wait_recv()
+                    total[rows] += line_take[from_above(line), rows].astype(jnp.float32)
+
+                @pl.when(line > place)
+                def _():
+                    take[SIDE + step, rows] = total[rows].astype(jnp.bfloat16)
+                    line_copy(step, line, line, above, part).start()
+
+                @pl.when(line < place)
+                def _():
+                    take[SIDE + step, rows] = total[rows].astype(jnp.bfloat16)
+                    line_copy(step, line, to_below(line), below, part).start()
+
+        if other_work is not None:
+
+            @pl.when(what == 7)
+            def _():
+                other_work(turn)
+
+        return turn + jnp.where(what == 7, 1, 0)
+
+    lax.fori_loop(0, len(ops[0]), one, jnp.int32(0))
+
+    def finish(step, carry):
+        line = digit_of_row(FAR, place, step)
+        core_copy(step, SIDE + step).wait_send()
+        side_copy(step, 0).wait_send()
+
+        @pl.when(line == place)
+        def _():
+            side_copy(step, 1).wait_send()
+
+        @pl.when(line != place)
+        def _():
+            for part in range(2):
+                line_copy(step, line, line, place, part).wait_send()
+            other_copy(step, line, line, place).wait_send()
+
+        return carry
+
+    lax.fori_loop(0, SIDE, finish, 0)
+
+
+def scatter_scratch(rows):
+    return [
+        pltpu.VMEM((rows, D), jnp.float32),
+        pltpu.VMEM((SIDE, rows, D), jnp.bfloat16),
+        pltpu.VMEM((2 * SIDE, rows, D), jnp.bfloat16),
+        pltpu.VMEM((SIDE, rows, D), jnp.bfloat16),
+        pltpu.VMEM((SIDE + 1, rows, D), jnp.bfloat16),
+        pltpu.VMEM((SIDE + 1, SPLIT[1][1], D), jnp.bfloat16),
+        pltpu.SemaphoreType.DMA((2 * SIDE,)),
+        pltpu.SemaphoreType.DMA((2 * SIDE,)),
+        pltpu.SemaphoreType.DMA((SIDE, 2)),
+        pltpu.SemaphoreType.DMA((SIDE, 2)),
+        pltpu.SemaphoreType.DMA((SIDE, 2)),
+        pltpu.SemaphoreType.DMA((SIDE + 1, 2)),
+        pltpu.SemaphoreType.DMA((SIDE,)),
+        pltpu.SemaphoreType.DMA((SIDE + 1,)),
+    ]
+
+
+def forward_scatter(hidden, bias, mixed, active, out_weight, down_weight, layer):
+    rows = hidden.shape[0]
+
+    def kernel(hidden, bias, mixed, active, out_weight, down_weight, out, *scratch):
+        greet_neighbours()
+
+        def partial(slot):
+            return dot(mixed[slot], out_weight[...]) + dot(active[slot], down_weight[...])
+
+        scatter_events(partial, None, SCATTER_OPS, scratch)
+        out[...] = hidden[...].astype(jnp.float32) + (scratch[0][...] + bias[...])
+
+    return pl.pallas_call(
+        kernel,
+        out_shape=jax.ShapeDtypeStruct((rows, D), jnp.float32),
+        in_specs=[VMEM] * 6,
+        out_specs=VMEM,
+        scratch_shapes=scatter_scratch(rows),
+        compiler_params=pltpu.CompilerParams(
+            collective_id=10 + layer, has_side_effects=True, vmem_limit_bytes=ROOM
+        ),
+    )(hidden, bias, mixed, active, out_weight, down_weight)
+
+
+SMALL_ROWS = 16
+
+
+def backward_scatter(hidden, grad, gain, grad_joint, grad_inner, columns, every, layer):
+    rows = hidden.shape[0]
+    half = SHARE // 2
+    collects = layer == 0
+
+    def kernel(
+        hidden,
+        grad,
+        gain,
+        grad_joint,
+        grad_inner,
+        columns,
+        every,
+        out,
+        small_out,
+        *refs,
+    ):
+        if collects:
+            joint_out, upper_out, mine, strips, other, summed, arrived = refs[:7]
+            refs = refs[7:]
+        else:
+            mine, strips = refs[:2]
+            joint_out = upper_out = other = summed = arrived = mine
+            refs = refs[2:]
+        (
+        shares,
+        small_land,
+        small_mine,
+        small_other,
+        load,
+        cross_send,
+        cross_recv,
+        plane_send,
+        plane_recv,
+        back_send,
+        back_recv,
+        keep,
+        small_send,
+        small_recv,
+        swap_send,
+        swap_recv,
+        *scratch,
+        ) = refs
+        total = scratch[0]
+        ctx, place, seq = lax.axis_index("ctx"), lax.axis_index("fsdp"), lax.axis_index("seq")
+        me = ctx * SIDE + place
+        part_rows = pl.ds(pl.multiple_of(seq * half, half), half)
+        other_rows = pl.ds(pl.multiple_of((1 - seq) * half, half), half)
+        outputs = (joint_out, upper_out)
+        greet_plane(GROUP)
+
+        def block_of(turn):
+            return lax.rem(me + 1 + turn, GROUP)
+
+        def load_strip(turn):
+            start = pl.multiple_of(block_of(turn) * SHARE, SHARE)
+            buffer = lax.rem(turn, 2)
+            return pltpu.make_async_copy(
+                every.at[:, :, pl.ds(start, SHARE)], strips.at[buffer], load.at[buffer]
+            )
+
+        def cross_copy(block):
+            return to_axis(
+                mine.at[block, other_rows],
+                other.at[block],
+                cross_send.at[block],
+                cross_recv.at[block],
+                "seq",
+                1 - seq,
+            )
+
+        def plane_copy(block):
+            return to_peer(
+                summed.at[block], arrived.at[me], plane_send.at[block], plane_recv.at[me], block
+            )
+
+        def final_pieces(source):
+            return [
+                (
+                    number,
+                    arrived.at[source, :, pl.ds(at, width)],
+                    outputs[which].at[part_rows, pl.ds(start, width)],
+                )
+                for number, (which, start, at, width) in enumerate(column_places(source))
+            ]
+
+        def back_copies(source):
+            return [
+                to_axis(
+                    piece,
+                    target,
+                    back_send.at[source, number],
+                    back_recv.at[source, number],
+                    "seq",
+                    1 - seq,
+                )
+                for number, piece, target in final_pieces(source)
+            ]
+
+        def keep_copies(source):
+            return [
+                pltpu.make_async_copy(piece, target, keep.at[source, number])
+                for number, piece, target in final_pieces(source)
+            ]
+
+        def partial(slot):
+            return dot(grad_joint[slot], columns[:, :JOINT_COLS], 1, 1) + dot(
+                grad_inner[slot], columns[:, JOINT_COLS:], 1, 1
+            )
+
+        def product(turn):
+            block = block_of(turn)
+            load_strip(turn).wait()
+
+            @pl.when(turn + 1 < GROUP)
+            def _():
+                load_strip(turn + 1).start()
+
+            strip = strips[lax.rem(turn, 2)].reshape(GROUP * rows, SHARE)
+            mine[block, :, :JOINT_COLS] = dot(
+                strip, grad_joint[...].reshape(GROUP * rows, JOINT_COLS), 0, 0
+            ).astype(jnp.bfloat16)
+            mine[block, :, JOINT_COLS:] = dot(
+                strip, grad_inner[...].reshape(GROUP * rows, FEED_COLS), 0, 0
+            ).astype(jnp.bfloat16)
+            if collects:
+                cross_copy(block).start()
+
+        def add(turn):
+            block = block_of(turn)
+            cross_copy(block).wait_recv()
+            summed[block] = (
+                mine[block, part_rows].astype(jnp.float32) + other[block].astype(jnp.float32)
+            ).astype(jnp.bfloat16)
+
+            @pl.when(turn < GROUP - 1)
+            def _():
+                plane_copy(block).start()
+
+        def other_work(turn):
+            product(turn)
+            if collects:
+
+                @pl.when(turn >= SIDE)
+                def _():
+                    add(turn - SIDE)
+
+        def last_adds(turn, carry):
+            add(turn)
+            return carry
+
+        load_strip(0).start()
+        scatter_events(
+            partial, other_work, SCATTER_OPS_EARLY if collects else SCATTER_OPS_WORK, scratch
+        )
+        if collects:
+            lax.fori_loop(GROUP - SIDE, GROUP, last_adds, 0)
+            arrived[me] = summed[me]
+
+        def norm_back(part, sums):
+            values = hidden[part].astype(jnp.float32)
+            centred = values - jnp.mean(values, axis=1, keepdims=True)
+            spread = jnp.mean(centred * centred, axis=1, keepdims=True)
+            root = lax.rsqrt(spread + EPS)
+            normed = centred * root
+            above = total[part]
+            scaled = above * gain[...]
+            down = jnp.mean(scaled, axis=1, keepdims=True)
+            along = jnp.mean(scaled * normed, axis=1, keepdims=True)
+            passing = grad[part]
+            out[part] = passing + root * (scaled - down - normed * along)
+            low = passing.astype(jnp.bfloat16).astype(jnp.float32)
+
+            def fold(values):
+                return jnp.sum(values.reshape(STRIP // 8, 8, D), axis=0)
+
+            return (sums[0] + fold(above * normed), sums[1] + fold(above), sums[2] + fold(low))
+
+        zeros = jnp.zeros((8, D), jnp.float32)
+        sums = each_strip(rows, norm_back, (zeros, zeros, zeros))
+        shares[...] = jnp.zeros_like(shares)
+        for number, folded in enumerate(sums):
+            row = jnp.sum(folded, axis=0, keepdims=True)
+            for block in range(GROUP):
+                shares[block, number : number + 1] = row[:, block * SHARE : (block + 1) * SHARE]
+        ones = jnp.ones((16, GROUP * rows), jnp.bfloat16)
+        joint_bias = dot(ones, grad_joint[...].reshape(GROUP * rows, JOINT_COLS))[:1]
+        upper_bias = dot(ones, grad_inner[...].reshape(GROUP * rows, FEED_COLS))[:1]
+        for part in range(3):
+            at = part * GROUP + me
+            shares[at // 3, pl.ds(3 + lax.rem(at, 3), 1)] = joint_bias[
+                :, part * HEAD_COLS : (part + 1) * HEAD_COLS
+            ]
+        for part in range(FEED_COLS // SHARE):
+            shares[me, 6 + part : 7 + part] = upper_bias[:, part * SHARE : (part + 1) * SHARE]
+
+        def small_copy(step):
+            peer = lax.rem(me + step, GROUP)
+            return to_peer(
+                shares.at[peer], small_land.at[me], small_send.at[step], small_recv.at[me], peer
+            )
+
+        def small_begin(step, carry):
+            small_copy(step).start()
+            return carry
+
+        lax.fori_loop(1, GROUP, small_begin, 0)
+        small_land[me] = shares[me]
+
+        def pass_on(step, carry):
+            source = lax.rem(me + GROUP - step, GROUP)
+
+            @pl.when(step > 0)
+            def _():
+                to_peer(
+                    summed.at[source],
+                    arrived.at[source],
+                    plane_send.at[source],
+                    plane_recv.at[source],
+                    source,
+                ).wait_recv()
+
+            for copy in back_copies(source) + keep_copies(source):
+                copy.start()
+            return carry
+
+        if collects:
+            lax.fori_loop(0, GROUP, pass_on, 0)
+
+        def small_end(step, carry):
+            source = lax.rem(me + GROUP - step, GROUP)
+            to_peer(
+                shares.at[source],
+                small_land.at[source],
+                small_send.at[step],
+                small_recv.at[source],
+                source,
+            ).wait_recv()
+            small_copy(step).wait_send()
+            return carry
+
+        lax.fori_loop(1, GROUP, small_end, 0)
+        small_mine[...] = jnp.sum(small_land[...], axis=0)
+        swap = to_axis(small_mine, small_other, swap_send, swap_recv, "seq", 1 - seq)
+        swap.start()
+        swap.wait()
+        small_out[...] = small_mine[...] + small_other[...]
+
+        def end(block, carry):
+            cross_copy(block).wait_send()
+
+            @pl.when(block != me)
+            def _():
+                plane_copy(block).wait_send()
+
+            for copy in back_copies(block) + keep_copies(block):
+                copy.wait()
+            return carry
+
+        if collects:
+            lax.fori_loop(0, GROUP, end, 0)
+
+    part = pltpu.VMEM((GROUP, half, COLS), jnp.bfloat16)
+    whole = (GROUP, SHARE, COLS)
+    small = (SMALL_ROWS, SHARE)
+    return pl.pallas_call(
+        kernel,
+        out_shape=(
+            jax.ShapeDtypeStruct((rows, D), jnp.float32),
+            jax.ShapeDtypeStruct(small, jnp.float32),
+        )
+        + (
+            (
+                jax.ShapeDtypeStruct((SHARE, 3 * D), jnp.bfloat16),
+                jax.ShapeDtypeStruct((SHARE, FF), jnp.bfloat16),
+            )
+            if collects
+            else (jax.ShapeDtypeStruct(whole, jnp.bfloat16),)
+        ),
+        in_specs=[VMEM] * 6 + [HBM],
+        out_specs=(VMEM, VMEM) + ((HBM, HBM) if collects else (VMEM,)),
+        scratch_shapes=([pltpu.VMEM(whole, jnp.bfloat16)] if collects else [])
+        + [pltpu.VMEM((2, GROUP, rows, SHARE), jnp.bfloat16)]
+        + ([part] * 3 if collects else [])
+        + [
+            pltpu.VMEM((GROUP,) + small, jnp.float32),
+            pltpu.VMEM((GROUP,) + small, jnp.float32),
+            pltpu.VMEM(small, jnp.float32),
+            pltpu.VMEM(small, jnp.float32),
+            pltpu.SemaphoreType.DMA((2,)),
+        ]
+        + [pltpu.SemaphoreType.DMA((GROUP,))] * 4
+        + [pltpu.SemaphoreType.DMA((GROUP, PLACES))] * 3
+        + [pltpu.SemaphoreType.DMA((GROUP,))] * 2
+        + [pltpu.SemaphoreType.DMA] * 2
+        + scatter_scratch(rows),
+        compiler_params=pltpu.CompilerParams(
+            collective_id=20 + layer, has_side_effects=True, vmem_limit_bytes=ROOM
+        ),
+    )(hidden, grad, gain, grad_joint, grad_inner, columns, every)
+
+
+def gather_small(packed):
+    def kernel(packed, out, send, recv):
+        ctx, place = lax.axis_index("ctx"), lax.axis_index("fsdp")
+        me = ctx * SIDE + place
+        greet_plane(GROUP, False)
+        out[me] = packed[...]
+
+        def copy(step):
+            return to_peer(
+                packed, out.at[me], send.at[step], recv.at[me], lax.rem(me + step, GROUP)
+            )
+
+        def begin(step, carry):
+            copy(step).start()
+            return carry
+
+        lax.fori_loop(1, GROUP, begin, 0)
+
+        def end(step, carry):
+            source = lax.rem(me + GROUP - step, GROUP)
+            to_peer(packed, out.at[source], send.at[step], recv.at[source], source).wait_recv()
+            copy(step).wait_send()
+            return carry
+
+        lax.fori_loop(1, GROUP, end, 0)
+
+    return pl.pallas_call(
+        kernel,
+        out_shape=jax.ShapeDtypeStruct((GROUP,) + packed.shape, packed.dtype),
+        in_specs=[VMEM],
+        out_specs=VMEM,
+        scratch_shapes=[pltpu.SemaphoreType.DMA((GROUP,))] * 2,
+        compiler_params=pltpu.CompilerParams(
+            collective_id=6, has_side_effects=True, vmem_limit_bytes=ROOM
+        ),
+    )(packed)
+
+
+def mask_rest(rows, begin, spot, first, lead):
+    if lead:
+        old = jnp.where(spot[:lead] >= begin, rows[:lead], NEG)
+    key_at = lax.broadcasted_iota(jnp.int32, (first, first), 0) + lead
+    query_at = lax.broadcasted_iota(jnp.int32, (first, first), 1) + lead
+    near = spot[lead:]
+    seen = ((near >= begin) & (near <= query_at)) | (key_at == query_at)
+    new = jnp.where(seen, rows[lead:], NEG)
+    return jnp.concatenate([old, new], axis=0) if lead else new
+
+
+def head_lanes(head, rows):
+    lane = lax.broadcasted_iota(jnp.int32, (rows, HEAD_COLS), 1)
+    return (lane >= head * HEAD_DIM) & (lane < (head + 1) * HEAD_DIM)
+
+
+def column_exchange(sources, land, sems, layer):
+    plane_send, plane_recv, own_sem = sems
+    ctx, place, seq = lax.axis_index("ctx"), lax.axis_index("fsdp"), lax.axis_index("seq")
+    me = ctx * SIDE + place
+    half = SHARE // 2
+    part_rows = pl.ds(pl.multiple_of(seq * half, half), half)
+
+    def piece(peer, number):
+        which, start, at, width = column_places(peer)[number]
+        return (
+            sources[which].at[layer, part_rows, pl.ds(start, width)],
+            land.at[me, :, pl.ds(at, width)],
+        )
+
+    def send_piece(step, number):
+        peer = lax.rem(me + step, GROUP)
+        source, target = piece(peer, number)
+        return to_peer(source, target, plane_send.at[step, number], plane_recv.at[me, number], peer)
+
+    def own_piece(number):
+        return pltpu.make_async_copy(*piece(me, number), own_sem.at[number])
+
+    def begin():
+        greet_plane(GROUP, False)
+
+        def send(step, carry):
+            for number in range(PLACES):
+                send_piece(step, number).start()
+            return carry
+
+        lax.fori_loop(1, GROUP, send, 0)
+        for number in range(PLACES):
+            own_piece(number).start()
+
+    def end():
+        def arrive(step, carry):
+            source = lax.rem(me + GROUP - step, GROUP)
+            for number in range(PLACES):
+                _, _, at, width = column_places(0)[number]
+                target = land.at[source, :, pl.ds(at, width)]
+                to_peer(
+                    target, target, plane_send.at[0, number], plane_recv.at[source, number], source
+                ).wait_recv()
+                send_piece(step, number).wait_send()
+            return carry
+
+        lax.fori_loop(1, GROUP, arrive, 0)
+        for number in range(PLACES):
+            own_piece(number).wait()
+
+    return begin, end
+
+
+def row_exchange(summed, outputs, sems):
+    plane_send, plane_recv, own_sem = sems
+    me = lax.axis_index("ctx") * SIDE + lax.axis_index("fsdp")
+
+    def piece(peer, number):
+        which, start, at, width = column_places(me)[number]
+        return summed.at[peer, :, pl.ds(at, width)], outputs[which].at[:, pl.ds(start, width)]
+
+    def send_piece(step, number):
+        peer = lax.rem(me + step, GROUP)
+        source, target = piece(peer, number)
+        return to_peer(source, target, plane_send.at[step, number], plane_recv.at[me, number], peer)
+
+    def own_piece(number):
+        return pltpu.make_async_copy(*piece(me, number), own_sem.at[number])
+
+    def begin():
+        greet_plane(GROUP, False)
+
+        def send(step, carry):
+            for number in range(PLACES):
+                send_piece(step, number).start()
+            return carry
+
+        lax.fori_loop(1, GROUP, send, 0)
+        for number in range(PLACES):
+            own_piece(number).start()
+
+    def end():
+        def arrive(step, carry):
+            source = lax.rem(me + GROUP - step, GROUP)
+            for number in range(PLACES):
+                which, start, _, width = column_places(source)[number]
+                target = outputs[which].at[:, pl.ds(start, width)]
+                to_peer(
+                    target, target, plane_send.at[0, number], plane_recv.at[source, number], source
+                ).wait_recv()
+                send_piece(step, number).wait_send()
+            return carry
+
+        lax.fori_loop(1, GROUP, arrive, 0)
+        for number in range(PLACES):
+            own_piece(number).wait()
+
+    return begin, end
+
+
+EXCHANGE_SEMS = [
+    pltpu.SemaphoreType.DMA((GROUP, PLACES)),
+    pltpu.SemaphoreType.DMA((GROUP, PLACES)),
+    pltpu.SemaphoreType.DMA((PLACES,)),
+]
+
+
+def attend_plane(query, key, value, begin, spot, weights=None, layer=0):
+    rows = query.shape[1]
+    length = SIDE * rows
+    scale = 1.0 / math.sqrt(HEAD_DIM)
+
+    def kernel(query, key, value, begin, spot, *refs):
+        if weights is None:
+            mixed, turned, stats = refs
+        else:
+            mixed, turned, stats, land = refs[2:6]
+            begin_exchange, end_exchange = column_exchange(refs[:2], land, refs[6:], layer)
+            pl.when(pl.program_id(0) == 0)(begin_exchange)
+        keys = key[:, 0].reshape(length, HEAD_COLS)
+        values = value[:, 0].reshape(length, HEAD_COLS)
+        for chunk in range(SIDE):
+            lead = chunk * rows
+            seen = lead + rows
+            scaled = query[chunk, 0] * jnp.bfloat16(scale)
+            start = begin[0, :, lead:seen]
+            outs = []
+            for head in range(OWN):
+                own = jnp.where(head_lanes(head, rows), scaled, jnp.bfloat16(0))
+                scores = mask_rest(
+                    dot(keys[:seen], own, 1, 1), start, spot[0, :seen], rows, lead
+                )
+                peak = jnp.max(scores, axis=0, keepdims=True)
+                probs = jnp.exp(scores - peak)
+                norm = jnp.sum(probs, axis=0, keepdims=True)
+                stats[0, head : head + 1, lead:seen] = peak
+                stats[0, OWN + head : OWN + head + 1, lead:seen] = norm
+                whole = dot(values[:seen], probs.astype(jnp.bfloat16), 0, 0)
+                outs.append(whole[head * HEAD_DIM : (head + 1) * HEAD_DIM] / norm)
+            joined = jnp.concatenate(outs, axis=0)
+            turned[chunk, 0] = joined
+            mixed[chunk, 0] = joined.T.astype(jnp.bfloat16)
+        if weights is not None:
+            pl.when(pl.program_id(0) == SIDE - 1)(end_exchange)
+
+    def spec(height, width):
+        return pl.BlockSpec((SIDE, 1, height, width), lambda step: (0, step, 0, 0))
+
+    def shape(height, width, dtype):
+        return jax.ShapeDtypeStruct((SIDE, SIDE, height, width), dtype)
+
+    extra = weights is not None
+    land = (jax.ShapeDtypeStruct((GROUP, SHARE // 2, COLS), jnp.bfloat16),) if extra else ()
+    mixed, turned, stats, *land = pl.pallas_call(
+        kernel,
+        grid=(SIDE,),
+        out_shape=(
+            shape(rows, HEAD_COLS, jnp.bfloat16),
+            shape(HEAD_COLS, rows, jnp.float32),
+            jax.ShapeDtypeStruct((SIDE, 2 * OWN, length), jnp.float32),
+        )
+        + land,
+        in_specs=[spec(rows, HEAD_COLS)] * 3
+        + [
+            pl.BlockSpec((1, 1, length), lambda step: (step, 0, 0)),
+            pl.BlockSpec((1, length, 1), lambda step: (step, 0, 0)),
+        ]
+        + [HBM] * (2 if extra else 0),
+        out_specs=(
+            spec(rows, HEAD_COLS),
+            spec(HEAD_COLS, rows),
+            pl.BlockSpec((1, 2 * OWN, length), lambda step: (step, 0, 0)),
+        )
+        + ((HBM,) if extra else ()),
+        scratch_shapes=EXCHANGE_SEMS if extra else [],
+        compiler_params=pltpu.CompilerParams(
+            collective_id=40, has_side_effects=True, vmem_limit_bytes=ROOM
+        )
+        if extra
+        else pltpu.CompilerParams(vmem_limit_bytes=ROOM),
+    )(
+        *(array.reshape(SIDE, SIDE, rows, HEAD_COLS) for array in (query, key, value)),
+        begin,
+        spot,
+        *(weights or ()),
+    )
+    return mixed.reshape(GROUP, rows, HEAD_COLS), turned, stats, *land
+
+
+def attend_plane_back(query, key, value, begin, spot, turned, stats, grad, tables, summed=None):
+    rows = query.shape[1]
+    length = SIDE * rows
+    scale = 1.0 / math.sqrt(HEAD_DIM)
+
+    extra = summed is not None
+
+    def kernel(query, key, value, grad, cosine, sine, begin, spot, turned, stats, *refs):
+        if extra:
+            out, grad_k, grad_v = refs[1], refs[4], refs[5]
+            begin_exchange, end_exchange = row_exchange(refs[0], refs[2:4], refs[6:])
+            pl.when(pl.program_id(0) == 0)(begin_exchange)
+        else:
+            out, grad_k, grad_v = refs
+        keys = key[:, 0].reshape(length, HEAD_COLS)
+        values = value[:, 0].reshape(length, HEAD_COLS)
+        for chunk in range(SIDE):
+            lead = chunk * rows
+            seen = lead + rows
+            if chunk == 0:
+                grad_k[...] = jnp.zeros_like(grad_k)
+                grad_v[...] = jnp.zeros_like(grad_v)
+            scaled = query[chunk, 0] * jnp.bfloat16(scale)
+            start = begin[0, :, lead:seen]
+            flipped = grad[chunk, 0].T
+            grad_q, drifts, numers = [], [], []
+            for head in range(OWN):
+                part = slice(head * HEAD_DIM, (head + 1) * HEAD_DIM)
+                norm = stats[0, OWN + head : OWN + head + 1, lead:seen]
+                drifts.append(
+                    jnp.sum(flipped[part] * turned[chunk, 0, part], axis=0, keepdims=True) / norm
+                )
+                numers.append(flipped[part] / norm)
+            numer = jnp.concatenate(numers, axis=0).T.astype(jnp.bfloat16)
+            for head in range(OWN):
+                part = slice(head * HEAD_DIM, (head + 1) * HEAD_DIM)
+                lanes = head_lanes(head, rows)
+                own = jnp.where(lanes, scaled, jnp.bfloat16(0))
+                own_numer = jnp.where(lanes, numer, jnp.bfloat16(0))
+                scores = mask_rest(
+                    dot(keys[:seen], own, 1, 1), start, spot[0, :seen], rows, lead
+                )
+                probs = jnp.exp(scores - stats[0, head : head + 1, lead:seen])
+                grad_probs = dot(values[:seen], own_numer, 1, 1)
+                grad_scores = (probs * (grad_probs - drifts[head])).astype(jnp.bfloat16)
+                grad_q.append(dot(keys[:seen], grad_scores, 0, 0)[part])
+                grad_k[:seen] += dot(grad_scores, own)
+                grad_v[:seen] += dot(probs.astype(jnp.bfloat16), own_numer)
+            turns = (cosine[chunk, 0], sine[chunk, 0])
+            whole = jnp.concatenate(grad_q, axis=0).T * scale
+            out[chunk, 0, :, :HEAD_COLS] = spin(whole, *turns, -1.0).astype(jnp.bfloat16)
+        for chunk in range(SIDE):
+            place = slice(chunk * rows, (chunk + 1) * rows)
+            turns = (cosine[chunk, 0], sine[chunk, 0])
+            out[chunk, 0, :, HEAD_COLS : 2 * HEAD_COLS] = spin(grad_k[place], *turns, -1.0).astype(
+                jnp.bfloat16
+            )
+            out[chunk, 0, :, 2 * HEAD_COLS :] = grad_v[place].astype(jnp.bfloat16)
+        if extra:
+            pl.when(pl.program_id(0) == SIDE - 1)(end_exchange)
+
+    def spec(height, width):
+        return pl.BlockSpec((SIDE, 1, height, width), lambda step: (0, step, 0, 0))
+
+    half = SHARE // 2
+    halves = (
+        jax.ShapeDtypeStruct((half, 3 * D), jnp.bfloat16),
+        jax.ShapeDtypeStruct((half, FF), jnp.bfloat16),
+    )
+    out, *halves = pl.pallas_call(
+        kernel,
+        grid=(SIDE,),
+        out_shape=(jax.ShapeDtypeStruct((SIDE, SIDE, rows, JOINT_COLS), jnp.bfloat16),)
+        + (halves if extra else ()),
+        in_specs=[spec(rows, HEAD_COLS)] * 6
+        + [
+            pl.BlockSpec((1, 1, length), lambda step: (step, 0, 0)),
+            pl.BlockSpec((1, length, 1), lambda step: (step, 0, 0)),
+            spec(HEAD_COLS, rows),
+            pl.BlockSpec((1, 2 * OWN, length), lambda step: (step, 0, 0)),
+        ]
+        + [HBM] * (1 if extra else 0),
+        out_specs=(spec(rows, JOINT_COLS),) + ((HBM, HBM) if extra else ()),
+        scratch_shapes=[pltpu.VMEM((length, HEAD_COLS), jnp.float32)] * 2
+        + (EXCHANGE_SEMS if extra else []),
+        compiler_params=pltpu.CompilerParams(
+            collective_id=41, has_side_effects=True, vmem_limit_bytes=ROOM
+        )
+        if extra
+        else pltpu.CompilerParams(vmem_limit_bytes=ROOM),
+    )(
+        *(
+            array.reshape(SIDE, SIDE, rows, HEAD_COLS)
+            for array in (query, key, value, grad) + tuple(tables)
+        ),
+        begin,
+        spot,
+        turned,
+        stats,
+        *((summed,) if extra else ()),
+    )
+    return out.reshape(GROUP, rows, JOINT_COLS), *halves
+
+
+def on_device_split(
+    tokens,
+    doc_lengths,
+    keep_mask,
+    ln_gain,
+    ln_bias,
+    qkv_weight,
+    qkv_bias,
+    out_weight,
+    out_bias,
+    up_weight,
+    up_bias,
+    down_weight,
+    down_bias,
+    cotangent,
+):
+    rows = tokens.shape[1]
+    length = SIDE * rows
+    docs = doc_lengths.shape[1]
+    me = lax.axis_index("ctx") * SIDE + lax.axis_index("fsdp")
+
+    high = (doc_lengths[0] // 32).astype(jnp.bfloat16)
+    low = (doc_lengths[0] % 32).astype(jnp.bfloat16)
+    fields = [ln_gain, ln_bias, qkv_bias, out_bias, down_bias]
+    packed = jnp.concatenate(
+        [field.reshape(-1) for field in fields]
+        + [keep_mask[0].astype(jnp.bfloat16), high, low]
+    )
+    tile = 16 * 128
+    packed = jnp.pad(packed, (0, -packed.shape[0] % tile)).reshape(-1, 128)
+    everyone = gather_small(packed).reshape(GROUP, -1)
+    at = 0
+    whole = []
+    for field in fields:
+        width = field.shape[1]
+        part = everyone[:, at : at + LAYERS * width].reshape(GROUP, LAYERS, width)
+        whole.append(part.transpose(1, 0, 2).reshape(LAYERS, 1, GROUP * width).astype(jnp.float32))
+        at += LAYERS * width
+    gain, shift, joint_bias, output_bias, lower_bias = whole
+    keep = everyone[:, at : at + rows].reshape(SIDE, SIDE, rows)
+    keep = keep.transpose(1, 0, 2).reshape(SIDE, length)
+    at += rows
+    lengths = (
+        everyone[:SIDE, at : at + docs].astype(jnp.int32) * 32
+        + everyone[:SIDE, at + docs : at + 2 * docs].astype(jnp.int32)
+    )
+    own_bias = lax.dynamic_slice_in_dim(
+        joint_bias.reshape(LAYERS, 3, GROUP, HEAD_COLS), me, 1, axis=2
+    ).reshape(LAYERS, JOINT_COLS)
+    column_bias = jnp.concatenate([own_bias, up_bias.astype(jnp.float32)], axis=1)
+
+    index = jnp.arange(length, dtype=jnp.int32)
+    ends = jnp.cumsum(lengths, axis=1)
+    passed = jnp.where(index[None, None, :] >= ends[:, :, None], ends[:, :, None], 0)
+    begin = jnp.max(passed, axis=1)[:, None, :]
+    spot = jnp.where(keep > 0, index[None, :], -1)[:, :, None]
+    position = (index[None, None, :] - begin).astype(jnp.float32)
+    position = position.reshape(SIDE, SIDE, rows).transpose(1, 0, 2).reshape(GROUP, rows, 1)
+    lane = np.arange(HEAD_COLS) % HEAD_DIM
+    inverse = 1.0 / 10000.0 ** (np.arange(0, ROT, 2, dtype=np.float32) / np.float32(ROT))
+    inverse = np.where(lane < ROT, inverse[lane % (ROT // 2)], 0.0).astype(np.float32)
+    inverse = jnp.asarray(inverse)[None, :]
+
+    seq = lax.axis_index("seq")
+    half = SHARE // 2
+    swap = [(0, 1), (1, 0)]
+
+    def swapped(values):
+        return lax.ppermute(values, "seq", swap)
+
+    hidden = tokens[0]
+    saved, tables = [], None
+    sources = (qkv_weight, up_weight)
+    for layer in range(LAYERS):
+        out = forward_gather(
+            hidden,
+            gain[layer],
+            shift[layer],
+            column_bias[layer][None, :],
+            tables or (position, inverse),
+            sources,
+            layer,
+        )
+        every, columns, query, key, value, inner, active = out[:7]
+        tables = tables or tuple(out[7:])
+        if layer + 1 < LAYERS:
+            mixed, turned, stats, arrived = attend_plane(
+                query, key, value, begin, spot, (qkv_weight, up_weight), layer + 1
+            )
+            sources = (arrived, swapped(arrived))
+        else:
+            mixed, turned, stats = attend_plane(query, key, value, begin, spot)
+        saved.append(
+            (hidden, every, columns, query, key, value, inner, active, mixed, turned, stats)
+        )
+        hidden = forward_scatter(
+            hidden,
+            output_bias[layer] + lower_bias[layer],
+            mixed,
+            active,
+            out_weight[layer],
+            down_weight[layer],
+            layer,
+        )
+    result = hidden.astype(jnp.bfloat16)[None]
+
+    grad_hidden = cotangent[0].astype(jnp.float32) * keep_mask[0].astype(jnp.float32)[:, None]
+    joint_grads, upper_grads, branch_grads, small_grads = [], [], [], []
+    summed = None
+    for layer in reversed(range(LAYERS)):
+        before, every, columns, query, key, value, inner, active, mixed, turned, stats = saved[layer]
+        grad_mixed, grad_inner, branch = backward_gather(
+            grad_hidden.astype(jnp.bfloat16),
+            out_weight[layer],
+            down_weight[layer],
+            inner,
+            mixed,
+            active,
+        )
+        branch_grads.insert(
+            0, branch.astype(jnp.float32) + swapped(branch).astype(jnp.float32)
+        )
+        grad_joint, *halves = attend_plane_back(
+            query, key, value, begin, spot, turned, stats, grad_mixed, tables, summed
+        )
+        for grads, own in zip((joint_grads, upper_grads), halves):
+            other = swapped(own)
+            grads.insert(
+                0,
+                jnp.concatenate(
+                    [jnp.where(seq == 0, own, other), jnp.where(seq == 0, other, own)], axis=0
+                ),
+            )
+        grad_hidden, small, *grads = backward_scatter(
+            before,
+            grad_hidden,
+            gain[layer],
+            grad_joint,
+            grad_inner,
+            columns.reshape(D, COLS),
+            every,
+            layer,
+        )
+        small_grads.insert(0, small)
+        if layer > 0:
+            own = lax.dynamic_slice_in_dim(grads[0], seq * half, half, axis=1)
+            other = swapped(lax.dynamic_slice_in_dim(grads[0], (1 - seq) * half, half, axis=1))
+            summed = (own.astype(jnp.float32) + other.astype(jnp.float32)).astype(jnp.bfloat16)
+        else:
+            joint_grads.insert(0, grads[0])
+            upper_grads.insert(0, grads[1])
+    branch_grad = jnp.stack(branch_grads)
+    small = jnp.stack(small_grads)
+    return (
+        result,
+        grad_hidden[None],
+        small[:, 0],
+        small[:, 1],
+        jnp.stack(joint_grads).astype(jnp.float32),
+        small[:, 3:6].reshape(LAYERS, JOINT_COLS),
+        branch_grad[:, :HEAD_COLS],
+        small[:, 2],
+        jnp.stack(upper_grads).astype(jnp.float32),
+        small[:, 6:10].reshape(LAYERS, FEED_COLS),
+        branch_grad[:, HEAD_COLS:],
+        small[:, 2],
+    )
+
+
 def solution(mesh):
+    small = mesh.shape["ctx"] == SIDE and mesh.shape["fsdp"] == SIDE and mesh.shape["seq"] == 2
+    on_device = on_device_split if small else on_device_gathered
     return jax.shard_map(
         on_device,
         mesh=mesh,

time: 5800 us -> 1180 us (0.20)
  waiting for transfers between devices: 3880 us -> 23.2 us
  Pallas kernels: 0 us -> 1070 us
  local copies, waits for them, and re-layouts: 773 us -> 24.2 us
  matrix products: 619 us -> 0 us
  blocking collectives: 373 us -> 0 us
  other arithmetic: 111 us -> 38.1 us
    reduce_scatter x8 -> x0, waiting for transfers between devices: 2990 us -> none  [the longest x2 2500 us: layer_backward(): lax.psum_scatter(jnp.concatenate([upper_part, lower_part, bias_part, bran...]
    pallas_call x0 -> x13, Pallas kernels: none -> 1070 us  [the longest x2 276 us: backward_scatter(): pl.pallas_call(kernel, out_shape=(jax.ShapeDtypeStruct((rows, D), jnp.flo...]
    all_gather x12 -> x0, waiting for transfers between devices: 694 us -> none  [the longest x2 323 us: fetch(): lax.all_gather(shards[8][layer_index], ('ctx', 'fsdp'), axis=0, tiled=True)]
    dot_general x36 -> x0, matrix products: 619 us -> none  [the longest x2 57.1 us: layer_backward(): jnp.einsum('tc,td->cd', activated, grad_branch, preferred_element_type=jn...]
    concatenate x4 -> x1, local copies, waits for them, and re-layouts: 505 us -> 2.75 us  [on_device_split(): jnp.concatenate([field.reshape(-1) for field in fields] + [keep_mask[0].a...]
    all_gather x13 -> x0, blocking collectives: 368 us -> none  [the longest x2 63.8 us: fetch(): lax.all_gather(shards[3][layer_index], ('ctx', 'fsdp'), axis=0, tiled=True)]
    psum x1 -> x0, waiting for transfers between devices: 185 us -> none  [on_device(): lax.psum(joint_stack.astype(jnp.bfloat16), 'seq').astype(jnp.float32)]
    reshape x6 -> x3, local copies, waits for them, and re-layouts: 166 us -> 4.59 us  [the longest x1 3.29 us: on_device_split(): position.reshape(SIDE, SIDE, rows).transpose(1, 0, 2)]
  transfers between devices with their start and end apart: 21 -> 6, of which waited for: 14 -> 1; matrix products, arithmetic and copies ran while one was open for 24% -> 3% of each run, Pallas kernels for 0% -> 35%
where the time goes in v1:
time: 1180 us; the launch traced here: 1160 us
  Pallas kernels  1070 us (91%)
  other arithmetic  38.1 us (3%)
  local copies, waits for them, and re-layouts  24.2 us (2%)
  waiting for transfers between devices  23.2 us (2%)
    pallas_call x2, Pallas kernels, backward_scatter(): pl.pallas_call(kernel, out_shape=(jax.ShapeDtypeStruct((rows, D), jnp.flo...  276 us
    pallas_call x2, Pallas kernels, forward_gather(): pl.pallas_call(kernel, out_shape=out_shape, in_specs=[VMEM] * 6 + [HBM] *...  252 us
    pallas_call x2, Pallas kernels, backward_gather(): pl.pallas_call(kernel, out_shape=(jax.ShapeDtypeStruct((GROUP, rows, HEAD...  202 us
    pallas_call x2, Pallas kernels, forward_scatter(): pl.pallas_call(kernel, out_shape=jax.ShapeDtypeStruct((rows, D), jnp.floa...  192 us
    pallas_call x2, Pallas kernels, attend_plane_back(): pl.pallas_call(kernel, grid=(SIDE,), out_shape=(jax.ShapeDtypeStruct((SID...  70.9 us
    pallas_call x2, Pallas kernels, attend_plane(): pl.pallas_call(kernel, grid=(SIDE,), out_shape=(shape(rows, HEAD_COLS, jn...  65.4 us
  transfers between devices with their start and end apart: 6, of which 1 were waited for; matrix products, arithmetic and copies ran while one was open for 3% of the time, Pallas kernels for 35%

profile of v1, /device:TPU:0, one launch (start us, length us, event | category | flops | bytes accessed | tf_op | source)
XLA Modules:
  0.0 1164.3 jit_solution(3037366901863311481)
XLA Ops:
  2.7 2.7 concatenate.12
  6.1 11.9 %shard_map.238 = bf16[16,32,128]{2,1,0:T(8,128)(2,1)} custom-call(bf16[32,128]{1,0:T(8,128)(2,1)} %pad_bitcast_fusion.packed), custom_call_target="tpu_custom_call" | custom-call | tf_op jit(solution)/shard_map/pallas_call | solution.py:1575
  20.8 3.3 reshape.331.turn_a
  27.7 147.4 %shard_map.239 = (bf16[16,256,2048]{2,1,0:T(8,128)(2,1)}, bf16[16,128,896]{2,1,0:T(8,128)(2,1)}, bf16[16,256,128]{2,1,0:T(8,128)(2,1)}, bf16[16,256,128]{2,1,0:T...) custom-call(bf16[256,2048]{1,0:T(8,128)(2,1)} %bitcast.124, ...), custom_call_target="tpu_custom_call" | custom-call | tf_op jit(solution)/shard_map/pallas_call | solution.py:917
  175.2 46.0 %shard_map.240 = (bf16[4,4,256,128]{3,2,1,0:T(8,128)(2,1)}, f32[4,4,128,256]{3,2,1,0:T(8,128)}, f32[4,4,1024]{2,1,0:T(4,128)}, bf16[16,64,896]{2,1,0:T(8,128)(2,1)}) custom-call(bf16[4,4,256,128]{3,2,1,0:T(8,128)(2,1)} %bitcast.127, bf16[4,4,256,128]{3,2,1,0:T(8,128)(2,1)} %bitcast.129, bf16[4,4,256,128]{3,2,1,0:T(8,128)(2,1)} %bitcast.131, ...), custom_call_target="tpu_custom_call" | custom-call | tf_op jit(solution)/shard_map/pallas_call | solution.py:1756
  224.4 4.8 slice_bitcast_fusion
  229.3 96.7 %shard_map.241.hidden = f32[256,2048]{1,0:T(8,128)} custom-call(bf16[256,2048]{1,0:T(8,128)(2,1)} %bitcast.125, f32[1,2048]{1,0:T(1,128)} %get-tuple-element.105.bias, bf16[16,256,128]{2,1,0:T(8,128)(2,1)} %bitcast.133, bf16[16,256,512]{2,1,0:T(8,128)(2,1)} %get-tuple-element.55.active, bf16[128,2048]{1,0:T(8,128)(2,1)} %get-tuple-element.99.out_weight, ...), custom_call_target="tpu_custom_call" | custom-call | tf_op jit(solution)/shard_map/pallas_call | solution.py:1232
  329.2 105.0 %shard_map.242 = (bf16[16,256,2048]{2,1,0:T(8,128)(2,1)}, bf16[16,128,896]{2,1,0:T(8,128)(2,1)}, bf16[16,256,128]{2,1,0:T(8,128)(2,1)}, bf16[16,256,128]{2,1,0:T...) custom-call(f32[256,2048]{1,0:T(8,128)} %shard_map.241.hidden, ...), custom_call_target="tpu_custom_call" | custom-call | tf_op jit(solution)/shard_map/pallas_call | solution.py:917
  434.2 19.3 %shard_map.243 = (bf16[4,4,256,128]{3,2,1,0:T(8,128)(2,1)}, f32[4,4,128,256]{3,2,1,0:T(8,128)}, f32[4,4,1024]{2,1,0:T(4,128)}) custom-call(bf16[4,4,256,128]{3,2,1,0:T(8,128)(2,1)} %bitcast.137, bf16[4,4,256,128]{3,2,1,0:T(8,128)(2,1)} %bitcast.139, bf16[4,4,256,128]{3,2,1,0:T(8,128)(2,1)} %bitcast.141, s32[4,1,1024]{2,1,0:T(1,128)} %broadcast_in_dim.43.begin, ...), custom_call_target="tpu_custom_call" | custom-call | tf_op jit(solution)/shard_map/pallas_call | solution.py:1756
  453.5 102.2 %shard_map.245 = (f32[16,256,128]{2,1,0:T(8,128)}, bf16[16,256,512]{2,1,0:T(8,128)(2,1)}, bf16[640,2048]{1,0:T(8,128)(2,1)}) custom-call(bf16[256,2048]{1,0:T(8,128)(2,1)} %get-tuple-element.96.own, bf16[128,2048]{1,0:T(8,128)(2,1)} %get-tuple-element.98.out_weight, bf16[512,2048]{1,0:T(8,128)(2,1)} %get-tuple-element.90.down_weight, ...), custom_call_target="tpu_custom_call" | custom-call | tf_op jit(solution)/shard_map/pallas_call | solution.py:977
  555.7 21.6 %shard_map.246 = bf16[4,4,256,384]{3,2,1,0:T(8,128)(2,1)} custom-call(bf16[4,4,256,128]{3,2,1,0:T(8,128)(2,1)} %bitcast.138, bf16[4,4,256,128]{3,2,1,0:T(8,128)(2,1)} %bitcast.140, bf16[4,4,256,128]{3,2,1,0:T(8,128)(2,1)} %bitcast.142, f32[4,4,256,128]{3,2,1,0:T(8,128)} %bitcast.147, f32[4,4,256,128]{3,2,1,0:T(8,128)} %bitcast.119, ...), custom_call_target="tpu_custom_call" | custom-call | tf_op jit(solution)/shard_map/pallas_call | solution.py:1861
  577.3 115.1 %shard_map.247 = (f32[256,2048]{1,0:T(8,128)}, f32[16,128]{1,0:T(8,128)}, bf16[16,128,896]{2,1,0:T(8,128)(2,1)}) custom-call(f32[256,2048]{1,0:T(8,128)} %shard_map.241.hidden, f32[256,2048]{1,0:T(8,128)} %get-tuple-element.97.grad, f32[1,2048]{1,0:T(1,128)} %get-tuple-element.118.gain, bf16[16,256,384]{2,1,0:T(8,128)(2,1)} %bitcast.123, ...), custom_call_target="tpu_custom_call" | custom-call | tf_op jit(solution)/shard_map/pallas_call | solution.py:1512
  692.4 2.7 convert_element_type.198.own
  695.2 99.8 %shard_map.248 = (f32[16,256,128]{2,1,0:T(8,128)}, bf16[16,256,512]{2,1,0:T(8,128)(2,1)}, bf16[640,2048]{1,0:T(8,128)(2,1)}) custom-call(bf16[256,2048]{1,0:T(8,128)(2,1)} %convert_element_type.198.own, bf16[128,2048]{1,0:T(8,128)(2,1)} %get-tuple-element.99.out_weight, bf16[512,2048]{1,0:T(8,128)(2,1)} %get-tuple-element.91.down_weight, ...), custom_call_target="tpu_custom_call" | custom-call | tf_op jit(solution)/shard_map/pallas_call | solution.py:977
  800.0 95.1 %shard_map.244 = f32[256,2048]{1,0:T(8,128)} custom-call(f32[256,2048]{1,0:T(8,128)} %shard_map.241.hidden, f32[1,2048]{1,0:T(1,128)} %get-tuple-element.104.bias, bf16[16,256,128]{2,1,0:T(8,128)(2,1)} %bitcast.136, bf16[16,256,512]{2,1,0:T(8,128)(2,1)} %get-tuple-element.63.active, bf16[128,2048]{1,0:T(8,128)(2,1)} %get-tuple-element.98.out_weight, ...), custom_call_target="tpu_custom_call" | custom-call | tf_op jit(solution)/shard_map/pallas_call | solution.py:1232
  897.8 3.3 add_convert_fusion.refs_0_
  901.1 49.3 %shard_map.249 = (bf16[4,4,256,384]{3,2,1,0:T(8,128)(2,1)}, bf16[64,6144]{1,0:T(8,128)(2,1)}, bf16[64,8192]{1,0:T(8,128)(2,1)}) custom-call(bf16[4,4,256,128]{3,2,1,0:T(8,128)(2,1)} %bitcast.128, bf16[4,4,256,128]{3,2,1,0:T(8,128)(2,1)} %bitcast.130, bf16[4,4,256,128]{3,2,1,0:T(8,128)(2,1)} %bitcast.132, f32[4,4,256,128]{3,2,1,0:T(8,128)} %bitcast.146, ...), custom_call_target="tpu_custom_call" | custom-call | tf_op jit(solution)/shard_map/pallas_call | solution.py:1861
  950.5 160.7 %shard_map.250 = (f32[256,2048]{1,0:T(8,128)}, f32[16,128]{1,0:T(8,128)}, bf16[128,6144]{1,0:T(8,128)(2,1)}, bf16[128,8192]{1,0:T(8,128)(2,1)}) custom-call(bf16[256,2048]{1,0:T(8,128)(2,1)} %bitcast.126, f32[256,2048]{1,0:T(8,128)} %get-tuple-element.71.grad, f32[1,2048]{1,0:T(1,128)} %get-tuple-element.117.gain, bf16[16,256,384]{2,1,0:T(8,128)(2,1)} %bitcast.145, ...), custom_call_target="tpu_custom_call" | custom-call | tf_op jit(solution)/shard_map/pallas_call | solution.py:1512
  1117.2 2.8 add_bitcast_fusion.1
  1120.0 3.6 add_bitcast_fusion
  1123.6 4.0 pad_maximum_fusion
  1127.6 23.2 %collective-permute-done.2 = bf16[64,6144]{1,0:T(8,128)(2,1)S(1)} collective-permute-done((bf16[64,6144]{1,0:T(8,128)(2,1)}, bf16[64,6144]{1,0:T(8,128)(2,1)S(1)}, u32[]{:S(2)}, u32[]{:S(2)}) %collective-permute-start.2) | collective-permute-done | bytes 786464 | tf_op jit(solution)/shard_map/ppermute | solution.py:1964
  1153.2 3.1 maximum_convert_fusion.1
  1158.0 3.9 maximum_convert_fusion
  (85 shorter events, 35.2 us)
Async XLA Ops:
  175.1 48.3 %copy-start.13 = (s32[1,256]{1,0:T(1,128)S(1)}, s32[1,256]{1,0:T(1,128)}, u32[]{:S(2)}) copy-start(s32[1,256]{1,0:T(1,128)} %param.17) | copy-start | bytes 3076
  175.1 48.3 %copy-start.9 = (bf16[2,128,2048]{2,1,0:T(8,128)(2,1)S(1)}, bf16[2,128,2048]{2,1,0:T(8,128)(2,1)}, u32[]{:S(2)}) copy-start(bf16[2,128,2048]{2,1,0:T(8,128)(2,1)} %param.22) | copy-start | bytes 3145732
  221.2 106.8 %collective-permute-start = (bf16[16,64,896]{2,1,0:T(8,128)(2,1)}, bf16[16,64,896]{2,1,0:T(8,128)(2,1)S(1)}, u32[]{:S(2)}, u32[]{:S(2)}) collective-permute-start(bf16[16,64,896]{2,1,0:T(8,128)(2,1)} %get-tuple-element.58.source_a), channel_id=1, source_target_pairs={{0,16},{16,0},{1,17},{17,1},{2,18},{18,2},{3,19},{19,3},{4,20},{20... | collective-permute-start | bytes 5505032 | tf_op jit(solution)/shard_map/ppermute | solution.py:1964
  229.3 96.7 %copy-start.7 = (bf16[1,256,2048]{2,1,0:T(8,128)(2,1)S(1)}, bf16[1,256,2048]{2,1,0:T(8,128)(2,1)}, u32[]{:S(2)}) copy-start(bf16[1,256,2048]{2,1,0:T(8,128)(2,1)} %param.28) | copy-start | bytes 3145732
  328.0 1.2 copy-start.5
  695.2 101.4 %copy-start = (bf16[16,128,896]{2,1,0:T(8,128)(2,1)S(1)}, bf16[16,128,896]{2,1,0:T(8,128)(2,1)}, u32[]{:S(2)}) copy-start(bf16[16,128,896]{2,1,0:T(8,128)(2,1)} %get-tuple-element.76) | copy-start | bytes 11010052
  795.0 322.2 %collective-permute-start.3 = (bf16[640,2048]{1,0:T(8,128)(2,1)}, bf16[640,2048]{1,0:T(8,128)(2,1)}, u32[]{:S(2)}, u32[]{:S(2)}) collective-permute-start(bf16[640,2048]{1,0:T(8,128)(2,1)} %get-tuple-element.86), channel_id=1, source_target_pairs={{0,16},{16,0},{1,17},{17,1},{2,18},{18,2},{3,19},{19,3},{4,20},{20... | collective-permute-start | bytes 7864328 | tf_op jit(solution)/shard_map/ppermute | solution.py:1964
  798.0 99.8 %collective-permute-start.1 = (bf16[16,64,896]{2,1,0:T(8,128)(2,1)}, bf16[16,64,896]{2,1,0:T(8,128)(2,1)}, u32[]{:S(2)}, u32[]{:S(2)}) collective-permute-start(bf16[16,64,896]{2,1,0:T(8,128)(2,1)} %constant_dynamic-slice_fusion), channel_id=1, source_target_pairs={{0,16},{16,0},{1,17},{17,1},{2,18},{18,2},{3,19},{19,3},{4,20},{20... | collective-permute-start | bytes 5505032 | tf_op jit(solution)/shard_map/ppermute | solution.py:1964
  798.5 321.5 %collective-permute-start.4 = (bf16[640,2048]{1,0:T(8,128)(2,1)}, bf16[640,2048]{1,0:T(8,128)(2,1)}, u32[]{:S(2)}, u32[]{:S(2)}) collective-permute-start(bf16[640,2048]{1,0:T(8,128)(2,1)} %get-tuple-element.87), channel_id=1, source_target_pairs={{0,16},{16,0},{1,17},{17,1},{2,18},{18,2},{3,19},{19,3},{4,20},{20... | collective-permute-start | bytes 7864328 | tf_op jit(solution)/shard_map/ppermute | solution.py:1964
  800.0 97.8 %copy-start.1 = (bf16[16,128,896]{2,1,0:T(8,128)(2,1)S(1)}, bf16[16,128,896]{2,1,0:T(8,128)(2,1)}, u32[]{:S(2)}) copy-start(bf16[16,128,896]{2,1,0:T(8,128)(2,1)} %get-tuple-element.76) | copy-start | bytes 11010052
  950.4 160.8 %copy-start.11 = (f32[16,128]{1,0:T(8,128)S(1)}, f32[16,128]{1,0:T(8,128)}, u32[]{:S(2)}) copy-start(f32[16,128]{1,0:T(8,128)} %get-tuple-element.83) | copy-start | bytes 24580
  950.4 162.1 %copy-start.8 = (bf16[64,8192]{1,0:T(8,128)(2,1)S(1)}, bf16[64,8192]{1,0:T(8,128)(2,1)}, u32[]{:S(2)}) copy-start(bf16[64,8192]{1,0:T(8,128)(2,1)} %get-tuple-element.89) | copy-start | bytes 3145732
  950.4 166.7 %copy-start.2 = (bf16[640,2048]{1,0:T(8,128)(2,1)S(1)}, bf16[640,2048]{1,0:T(8,128)(2,1)}, u32[]{:S(2)}) copy-start(bf16[640,2048]{1,0:T(8,128)(2,1)} %get-tuple-element.86) | copy-start | bytes 7864324
  1112.5 43.8 %collective-permute-start.5 = (bf16[64,8192]{1,0:T(8,128)(2,1)S(1)}, bf16[64,8192]{1,0:T(8,128)(2,1)S(1)}, u32[]{:S(2)}, u32[]{:S(2)}) collective-permute-start(bf16[64,8192]{1,0:T(8,128)(2,1)S(1)} %copy-done.8), channel_id=1, source_target_pairs={{0,16},{16,0},{1,17},{17,1},{2,18},{18,2},{3,19},{19,3},{4,20},{20... | collective-permute-start | bytes 3145736 | tf_op jit(solution)/shard_map/ppermute | solution.py:1964
  1115.2 35.5 %collective-permute-start.2 = (bf16[64,6144]{1,0:T(8,128)(2,1)}, bf16[64,6144]{1,0:T(8,128)(2,1)S(1)}, u32[]{:S(2)}, u32[]{:S(2)}) collective-permute-start(bf16[64,6144]{1,0:T(8,128)(2,1)} %get-tuple-element.85), channel_id=1, source_target_pairs={{0,16},{16,0},{1,17},{17,1},{2,18},{18,2},{3,19},{19,3},{4,20},{20... | collective-permute-start | bytes 2359304 | tf_op jit(solution)/shard_map/ppermute | solution.py:1964
  1117.2 44.8 %copy-start.12 = (f32[2,1,128]{2,1,0:T(1,128)}, f32[2,1,128]{2,1,0:T(1,128)S(1)}, u32[]{:S(2)}) copy-start(f32[2,1,128]{2,1,0:T(1,128)S(1)} %get-tuple-element.106) | copy-start | bytes 3076
  1123.6 27.2 %copy-start.10 = (bf16[64,6144]{1,0:T(8,128)(2,1)S(1)}, bf16[64,6144]{1,0:T(8,128)(2,1)}, u32[]{:S(2)}) copy-start(bf16[64,6144]{1,0:T(8,128)(2,1)} %get-tuple-element.85) | copy-start | bytes 2359300
  1151.0 2.2 copy-start.6
  1156.4 1.6 copy-start.4
  1158.0 4.5 copy-start.3

commit v2 on v1

--- a/solution.py
+++ b/solution.py
@@ -734,21 +734,33 @@
 PLACES = 4
 
 
+def load_all(pairs, sems):
+    copies = [
+        pltpu.make_async_copy(source, target, sems.at[number])
+        for number, (source, target) in enumerate(pairs)
+    ]
+    for copy in copies:
+        copy.start()
+    return copies
+
+
+def wait_all(copies):
+    for copy in copies:
+        copy.wait()
+
+
 def forward_gather(hidden, gain, shift, bias, turns, sources, layer):
     rows = hidden.shape[0]
     half = SHARE // 2
     first = layer == 0
 
     def kernel(hidden, gain, shift, bias, turn_a, turn_b, source_a, source_b, *refs):
-        every, columns_out, query, key, value, inner, active = refs[:7]
-        refs = refs[7:]
-        if first:
-            cosine, sine = refs[:2]
-            refs = refs[2:]
-        else:
-            cosine, sine = turn_a, turn_b
+        every, columns_out, results, refs = refs[0], refs[1], refs[2:7], refs[7:]
+        rings, ring_sem, refs = refs[-6:-1], refs[-1], refs[:-6]
+        cosine, sine, refs = refs[0], refs[1], refs[2:]
         columns, plane_send, plane_recv, cross_send, cross_recv, own_sem, saved = refs[:7]
         land = refs[7]
+        query, key, value, inner, active = rings
         ctx, place, seq = lax.axis_index("ctx"), lax.axis_index("fsdp"), lax.axis_index("seq")
         me = ctx * SIDE + place
         part_rows = pl.ds(pl.multiple_of(seq * half, half), half)
@@ -758,12 +770,6 @@
         else:
             greet_neighbours()
         sources = (source_a, source_b)
-        halves = ()
-        if not first:
-            halves = (
-                pltpu.make_async_copy(source_a, columns.at[:, part_rows], own_sem.at[0]),
-                pltpu.make_async_copy(source_b, columns.at[:, other_rows], own_sem.at[1]),
-            )
 
         def piece(step, number):
             peer = lax.rem(me + step, GROUP)
@@ -794,8 +800,15 @@
             for number in range(PLACES):
                 own_piece(number).start()
         else:
-            for copy in halves:
-                copy.start()
+            halves = load_all(
+                (
+                    (source_a, columns.at[:, part_rows]),
+                    (source_b, columns.at[:, other_rows]),
+                    (turn_a, cosine),
+                    (turn_b, sine),
+                ),
+                own_sem,
+            )
 
         def send_columns(step, carry):
             for number in range(PLACES):
@@ -831,15 +844,32 @@
 
             cross(source).start()
 
-        def product(slot):
+        def leave(number):
+            at = lax.rem(number, 2)
+            return [
+                pltpu.make_async_copy(
+                    ring.at[at], result.at[work_slot(number)], ring_sem.at[at, which]
+                )
+                for which, (ring, result) in enumerate(zip(rings, results))
+            ]
+
+        def product(number, slot):
             whole = dot(land[slot], columns[...].reshape(D, COLS)) + bias[...]
             one, two = HEAD_COLS, 2 * HEAD_COLS
-            query[slot] = spin(whole[:, :one], cosine[slot], sine[slot], 1.0).astype(jnp.bfloat16)
-            key[slot] = spin(whole[:, one:two], cosine[slot], sine[slot], 1.0).astype(jnp.bfloat16)
-            value[slot] = whole[:, two:JOINT_COLS].astype(jnp.bfloat16)
+            at = lax.rem(number, 2)
+
+            @pl.when(number >= 2)
+            def _():
+                wait_all(leave(number - 2))
+
+            query[at] = spin(whole[:, :one], cosine[slot], sine[slot], 1.0).astype(jnp.bfloat16)
+            key[at] = spin(whole[:, one:two], cosine[slot], sine[slot], 1.0).astype(jnp.bfloat16)
+            value[at] = whole[:, two:JOINT_COLS].astype(jnp.bfloat16)
             units = whole[:, JOINT_COLS:]
-            inner[slot] = units
-            active[slot] = jax.nn.gelu(units, approximate=True).astype(jnp.bfloat16)
+            inner[at] = units
+            active[at] = jax.nn.gelu(units, approximate=True).astype(jnp.bfloat16)
+            for copy in leave(number):
+                copy.start()
 
         save = pltpu.make_async_copy(columns, columns_out, saved)
 
@@ -872,7 +902,8 @@
             @pl.when(number >= GROUP // 2)
             def _():
                 def two_products(more, carry):
-                    product(work_slot(2 * number - GROUP + more))
+                    which = 2 * number - GROUP + more
+                    product(which, work_slot(which))
                     return carry
 
                 lax.fori_loop(0, 2, two_products, 0)
@@ -880,14 +911,15 @@
         def work(number, slot):
             @pl.when(number == 0)
             def _():
-                for copy in halves:
-                    copy.wait()
+                wait_all(halves)
                 save.start()
 
-            product(slot)
+            product(number, slot)
 
         gather_blocks(land, every, *refs[8:], work_as_columns_come if first else work)
         save.wait()
+        for number in (GROUP - 2, GROUP - 1):
+            wait_all(leave(jnp.int32(number)))
 
         def end(step, carry):
             cross(step).wait_send()
@@ -917,9 +949,10 @@
     return pl.pallas_call(
         kernel,
         out_shape=out_shape,
-        in_specs=[VMEM] * 6 + [HBM] * 2,
-        out_specs=[HBM, HBM] + [VMEM] * (len(out_shape) - 2),
-        scratch_shapes=[
+        in_specs=[VMEM] * 4 + [VMEM if first else HBM] * 2 + [HBM] * 2,
+        out_specs=[HBM] * 7 + [VMEM] * (len(out_shape) - 7),
+        scratch_shapes=([] if first else [pltpu.VMEM((GROUP, rows, HEAD_COLS), jnp.float32)] * 2)
+        + [
             pltpu.VMEM((GROUP, SHARE, COLS), jnp.bfloat16),
             pltpu.SemaphoreType.DMA((GROUP, PLACES)),
             pltpu.SemaphoreType.DMA((GROUP, PLACES)),
@@ -928,7 +961,15 @@
             pltpu.SemaphoreType.DMA((PLACES,)),
             pltpu.SemaphoreType.DMA,
         ]
-        + gather_scratch(rows),
+        + gather_scratch(rows)
+        + [
+            pltpu.VMEM((2, rows, HEAD_COLS), jnp.bfloat16),
+            pltpu.VMEM((2, rows, HEAD_COLS), jnp.bfloat16),
+            pltpu.VMEM((2, rows, HEAD_COLS), jnp.bfloat16),
+            pltpu.VMEM((2, rows, FEED_COLS), jnp.float32),
+            pltpu.VMEM((2, rows, FEED_COLS), jnp.bfloat16),
+            pltpu.SemaphoreType.DMA((2, 5)),
+        ],
         compiler_params=pltpu.CompilerParams(
             collective_id=30 + layer, has_side_effects=True, vmem_limit_bytes=ROOM
         ),
@@ -938,41 +979,70 @@
 def backward_gather(grad, out_weight, down_weight, inner, mixed, active):
     rows = grad.shape[0]
 
-    def kernel(
-        own,
-        out_weight,
-        down_weight,
-        inner,
-        mixed,
-        active,
-        grad_mixed,
-        grad_inner,
-        branch,
-        total,
-        land,
-        *sems,
-    ):
+    def kernel(own, out_weight, down_weight, inner, mixed, active, grad_mixed, grad_inner, branch, *refs):
+        out_part, down_part, weight_sem, total = refs[:4]
+        fetched, fetch_sem, rings, ring_sem = refs[4:7], refs[7], refs[8:10], refs[10]
+        land, sems = refs[11], refs[12:]
+        inner_part, mixed_part, active_part = fetched
         ctx, place, _, _, _ = neighbours()
+
+        def fetch(number):
+            at, slot = lax.rem(number, 2), work_slot(number)
+            return [
+                pltpu.make_async_copy(source.at[slot], target.at[at], fetch_sem.at[at, which])
+                for which, (source, target) in enumerate(zip((inner, mixed, active), fetched))
+            ]
+
+        def leave(number):
+            at, slot = lax.rem(number, 2), work_slot(number)
+            return [
+                pltpu.make_async_copy(ring.at[at], result.at[slot], ring_sem.at[at, which])
+                for which, (ring, result) in enumerate(zip(rings, (grad_mixed, grad_inner)))
+            ]
+
+        weights = load_all(((out_weight, out_part), (down_weight, down_part)), weight_sem)
+        for copy in fetch(jnp.int32(0)):
+            copy.start()
         greet_neighbours()
         land[ctx * SIDE + place] = own[...]
         total[...] = jnp.zeros_like(total)
 
         def work(number, slot):
+            at = lax.rem(number, 2)
+
+            @pl.when(number == 0)
+            def _():
+                wait_all(weights)
+
+            @pl.when(number + 1 < GROUP)
+            def _():
+                for copy in fetch(number + 1):
+                    copy.start()
+
+            @pl.when(number >= 2)
+            def _():
+                wait_all(leave(number - 2))
+
+            wait_all(fetch(number))
             block = land[slot]
-            grad_mixed[slot] = dot(block, out_weight[...], 1, 1)
-            value = inner[slot]
+            rings[0][at] = dot(block, out_part[...], 1, 1)
+            value = inner_part[at]
             factor = math.sqrt(2.0 / math.pi)
             square = value * value
             bend = jnp.tanh(factor * value * (1.0 + 0.044715 * square))
             slope = 0.5 * (1.0 + bend) + 0.5 * value * (1.0 - bend * bend) * (
                 factor * (1.0 + 3 * 0.044715 * square)
             )
-            grad_inner[slot] = (dot(block, down_weight[...], 1, 1) * slope).astype(jnp.bfloat16)
-            total[:HEAD_COLS] += dot(mixed[slot], block, 0, 0)
-            total[HEAD_COLS:] += dot(active[slot], block, 0, 0)
+            rings[1][at] = (dot(block, down_part[...], 1, 1) * slope).astype(jnp.bfloat16)
+            for copy in leave(number):
+                copy.start()
+            total[:HEAD_COLS] += dot(mixed_part[at], block, 0, 0)
+            total[HEAD_COLS:] += dot(active_part[at], block, 0, 0)
 
         gather_blocks(land, None, *sems, work)
         branch[...] = total[...].astype(jnp.bfloat16)
+        for number in (GROUP - 2, GROUP - 1):
+            wait_all(leave(jnp.int32(number)))
 
     return pl.pallas_call(
         kernel,
@@ -981,9 +1051,22 @@
             jax.ShapeDtypeStruct((GROUP, rows, FEED_COLS), jnp.bfloat16),
             jax.ShapeDtypeStruct((BACK_COLS, D), jnp.bfloat16),
         ),
-        in_specs=[VMEM] * 6,
-        out_specs=(VMEM, VMEM, VMEM),
-        scratch_shapes=[pltpu.VMEM((BACK_COLS, D), jnp.float32)] + gather_scratch(rows),
+        in_specs=[VMEM] + [HBM] * 5,
+        out_specs=(HBM, HBM, VMEM),
+        scratch_shapes=[
+            pltpu.VMEM(out_weight.shape, jnp.bfloat16),
+            pltpu.VMEM(down_weight.shape, jnp.bfloat16),
+            pltpu.SemaphoreType.DMA((2,)),
+            pltpu.VMEM((BACK_COLS, D), jnp.float32),
+            pltpu.VMEM((2, rows, FEED_COLS), jnp.float32),
+            pltpu.VMEM((2, rows, HEAD_COLS), jnp.bfloat16),
+            pltpu.VMEM((2, rows, FEED_COLS), jnp.bfloat16),
+            pltpu.SemaphoreType.DMA((2, 3)),
+            pltpu.VMEM((2, rows, HEAD_COLS), jnp.float32),
+            pltpu.VMEM((2, rows, FEED_COLS), jnp.bfloat16),
+            pltpu.SemaphoreType.DMA((2, 2)),
+        ]
+        + gather_scratch(rows),
         compiler_params=pltpu.CompilerParams(
             collective_id=4, has_side_effects=True, vmem_limit_bytes=ROOM
         ),
@@ -999,8 +1082,8 @@
     ((0, 0), (0, 2), (3, 2), (1, 0), (3, 0), (7, 0), (0, 1), (0, 3), (1, 1), (2, 0), (1, 2), (3, 1), (7, 0), (7, 0), (1, 3), (4, 0), (6, 0), (7, 0), (5, 0), (7, 0), (7, 0), (3, 3), (2, 1), (7, 0), (2, 2), (7, 0), (7, 0), (4, 1), (6, 1), (5, 1), (4, 2), (5, 2), (7, 0), (7, 0), (7, 0), (6, 2), (7, 0), (7, 0), (7, 0), (2, 3), (7, 0), (4, 3), (5, 3), (6, 3)),
 )
 SCATTER_OPS_EARLY = (
-    ((0, 0), (0, 1), (1, 0), (2, 0), (0, 2), (1, 1), (2, 1), (3, 0), (1, 2), (2, 2), (4, 0), (6, 0), (7, 0), (5, 0), (0, 3), (7, 0), (7, 0), (3, 1), (3, 2), (3, 3), (4, 1), (7, 0), (5, 1), (7, 0), (7, 0), (6, 1), (1, 3), (7, 0), (4, 2), (7, 0), (7, 0), (5, 2), (7, 0), (7, 0), (7, 0), (6, 2), (7, 0), (7, 0), (7, 0), (7, 0), (2, 3), (4, 3), (5, 3), (6, 3)),
-    ((0, 1), (0, 0), (1, 1), (0, 3), (1, 0), (0, 2), (3, 0), (1, 2), (2, 0), (7, 0), (1, 3), (3, 3), (2, 2), (3, 1), (3, 2), (4, 0), (7, 0), (6, 0), (7, 0), (2, 1), (2, 3), (7, 0), (5, 0), (7, 0), (7, 0), (4, 1), (7, 0), (7, 0), (6, 1), (7, 0), (7, 0), (5, 1), (4, 2), (5, 2), (7, 0), (7, 0), (7, 0), (7, 0), (7, 0), (7, 0), (6, 2), (4, 3), (5, 3), (6, 3)),
+    ((0, 0), (0, 1), (1, 0), (3, 0), (2, 0), (0, 2), (1, 1), (2, 1), (1, 2), (2, 2), (0, 3), (4, 0), (6, 0), (7, 0), (7, 0), (7, 0), (5, 0), (7, 0), (3, 1), (1, 3), (7, 0), (7, 0), (7, 0), (4, 1), (7, 0), (7, 0), (7, 0), (6, 1), (7, 0), (5, 1), (7, 0), (7, 0), (7, 0), (7, 0), (7, 0), (3, 2), (3, 3), (2, 3), (4, 2), (5, 2), (6, 2), (8, 0), (8, 1), (8, 2), (8, 3), (4, 3), (5, 3), (6, 3)),
+    ((0, 2), (7, 0), (0, 0), (0, 1), (1, 0), (7, 0), (7, 0), (0, 3), (7, 0), (3, 3), (3, 0), (7, 0), (1, 1), (2, 0), (3, 2), (1, 2), (7, 0), (2, 2), (7, 0), (7, 0), (3, 1), (1, 3), (4, 0), (6, 0), (7, 0), (2, 1), (7, 0), (7, 0), (7, 0), (5, 0), (7, 0), (7, 0), (7, 0), (7, 0), (2, 3), (4, 1), (6, 1), (5, 1), (4, 2), (5, 2), (6, 2), (8, 0), (8, 1), (8, 2), (8, 3), (4, 3), (5, 3), (6, 3)),
 )
 SPLIT = ((0, 208), (208, 48))
 
@@ -1013,7 +1096,7 @@
     return lax.rem(lax.shift_right_logical(word, 4 * lax.rem(index, 7)), 16)
 
 
-def scatter_events(partial, other_work, ops, scratch):
+def scatter_events(partial, other_work, late_work, ops, scratch):
     total, give, take, side_take, line_take, other_take = scratch[:6]
     core_send, core_recv, side_send, side_recv, line_send, line_recv = scratch[6:12]
     other_send, other_recv = scratch[12:]
@@ -1173,6 +1256,12 @@
             @pl.when(what == 7)
             def _():
                 other_work(turn)
+
+        if late_work is not None:
+
+            @pl.when(what == 8)
+            def _():
+                late_work(step)
 
         return turn + jnp.where(what == 7, 1, 0)
 
@@ -1220,21 +1309,40 @@
 def forward_scatter(hidden, bias, mixed, active, out_weight, down_weight, layer):
     rows = hidden.shape[0]
 
-    def kernel(hidden, bias, mixed, active, out_weight, down_weight, out, *scratch):
+    def kernel(hidden, bias, mixed, active, out_weight, down_weight, out, *refs):
+        hidden_part, mixed_part, active_part, out_part, down_part, load_sem = refs[:6]
+        scratch = refs[6:]
+        loads = load_all(
+            (
+                (mixed, mixed_part),
+                (active, active_part),
+                (out_weight, out_part),
+                (down_weight, down_part),
+                (hidden, hidden_part),
+            ),
+            load_sem,
+        )
         greet_neighbours()
+        wait_all(loads[:4])
 
         def partial(slot):
-            return dot(mixed[slot], out_weight[...]) + dot(active[slot], down_weight[...])
-
-        scatter_events(partial, None, SCATTER_OPS, scratch)
-        out[...] = hidden[...].astype(jnp.float32) + (scratch[0][...] + bias[...])
+            return dot(mixed_part[slot], out_part[...]) + dot(active_part[slot], down_part[...])
+
+        scatter_events(partial, None, None, SCATTER_OPS, scratch)
+        loads[4].wait()
+        out[...] = hidden_part[...].astype(jnp.float32) + (scratch[0][...] + bias[...])
 
     return pl.pallas_call(
         kernel,
         out_shape=jax.ShapeDtypeStruct((rows, D), jnp.float32),
-        in_specs=[VMEM] * 6,
+        in_specs=[HBM, VMEM] + [HBM] * 4,
         out_specs=VMEM,
-        scratch_shapes=scatter_scratch(rows),
+        scratch_shapes=[
+            pltpu.VMEM(array.shape, array.dtype)
+            for array in (hidden, mixed, active, out_weight, down_weight)
+        ]
+        + [pltpu.SemaphoreType.DMA((5,))]
+        + scatter_scratch(rows),
         compiler_params=pltpu.CompilerParams(
             collective_id=10 + layer, has_side_effects=True, vmem_limit_bytes=ROOM
         ),
@@ -1244,56 +1352,37 @@
 SMALL_ROWS = 16
 
 
-def backward_scatter(hidden, grad, gain, grad_joint, grad_inner, columns, every, layer):
+def backward_scatter(hidden, grad, gain, grad_joint, grad_inner, columns, every, layer, up=None):
     rows = hidden.shape[0]
     half = SHARE // 2
-    collects = layer == 0
-
-    def kernel(
-        hidden,
-        grad,
-        gain,
-        grad_joint,
-        grad_inner,
-        columns,
-        every,
-        out,
-        small_out,
-        *refs,
-    ):
+    collects = up is not None
+    made = JOINT_COLS if collects else COLS
+    tokens = GROUP * rows
+
+    def kernel(*refs):
+        inputs, refs = refs[: 8 if collects else 7], refs[8 if collects else 7 :]
+        gain, every = inputs[2], inputs[6]
+        out, small_out, refs = refs[0], refs[1], refs[2:]
         if collects:
-            joint_out, upper_out, mine, strips, other, summed, arrived = refs[:7]
-            refs = refs[7:]
+            outputs, refs = refs[:2], refs[2:]
         else:
-            mine, strips = refs[:2]
-            joint_out = upper_out = other = summed = arrived = mine
-            refs = refs[2:]
-        (
-        shares,
-        small_land,
-        small_mine,
-        small_other,
-        load,
-        cross_send,
-        cross_recv,
-        plane_send,
-        plane_recv,
-        back_send,
-        back_recv,
-        keep,
-        small_send,
-        small_recv,
-        swap_send,
-        swap_recv,
-        *scratch,
-        ) = refs
+            mine, refs = refs[0], refs[1:]
+        hidden, grad, grad_joint, grad_inner, columns, load_sem, strips, load = refs[:8]
+        shares, small_land, small_mine, small_other = refs[8:12]
+        small_send, small_recv, swap_send, swap_recv = refs[12:16]
+        refs = refs[16:]
+        if collects:
+            mine, other, summed, arrived, arrived_up = refs[:5]
+            cross_send, cross_recv, plane_send, plane_recv = refs[5:9]
+            back_send, back_recv, keep = refs[9:12]
+            up_send, up_recv, up_own = refs[12:15]
+            refs = refs[15:]
+        scratch = refs
         total = scratch[0]
         ctx, place, seq = lax.axis_index("ctx"), lax.axis_index("fsdp"), lax.axis_index("seq")
         me = ctx * SIDE + place
         part_rows = pl.ds(pl.multiple_of(seq * half, half), half)
         other_rows = pl.ds(pl.multiple_of((1 - seq) * half, half), half)
-        outputs = (joint_out, upper_out)
-        greet_plane(GROUP)
 
         def block_of(turn):
             return lax.rem(me + 1 + turn, GROUP)
@@ -1304,6 +1393,41 @@
             return pltpu.make_async_copy(
                 every.at[:, :, pl.ds(start, SHARE)], strips.at[buffer], load.at[buffer]
             )
+
+        loads = load_all(
+            (
+                (inputs[3], grad_joint),
+                (inputs[4], grad_inner),
+                (inputs[5], columns),
+                (inputs[0], hidden),
+                (inputs[1], grad),
+            ),
+            load_sem,
+        )
+        load_strip(jnp.int32(0)).start()
+        greet_plane(GROUP)
+
+        def partial(slot):
+            return dot(grad_joint[slot], columns[:, :JOINT_COLS], 1, 1) + dot(
+                grad_inner[slot], columns[:, JOINT_COLS:], 1, 1
+            )
+
+        def product(turn):
+            block = block_of(turn)
+            load_strip(turn).wait()
+
+            @pl.when(turn + 1 < GROUP)
+            def _():
+                load_strip(turn + 1).start()
+
+            strip = strips[lax.rem(turn, 2)].reshape(tokens, SHARE)
+            mine[block, :, :JOINT_COLS] = dot(
+                strip, grad_joint[...].reshape(tokens, JOINT_COLS), 0, 0
+            ).astype(jnp.bfloat16)
+            if not collects:
+                mine[block, :, JOINT_COLS:] = dot(
+                    strip, grad_inner[...].reshape(tokens, FEED_COLS), 0, 0
+                ).astype(jnp.bfloat16)
 
         def cross_copy(block):
             return to_axis(
@@ -1320,57 +1444,35 @@
                 summed.at[block], arrived.at[me], plane_send.at[block], plane_recv.at[me], block
             )
 
+        def up_copy(step):
+            peer = lax.rem(me + step, GROUP)
+            return to_peer(inputs[7].at[peer], arrived_up.at[me], up_send.at[step], up_recv.at[me], peer)
+
         def final_pieces(source):
-            return [
-                (
-                    number,
-                    arrived.at[source, :, pl.ds(at, width)],
-                    outputs[which].at[part_rows, pl.ds(start, width)],
-                )
-                for number, (which, start, at, width) in enumerate(column_places(source))
-            ]
-
-        def back_copies(source):
-            return [
-                to_axis(
-                    piece,
-                    target,
-                    back_send.at[source, number],
-                    back_recv.at[source, number],
-                    "seq",
-                    1 - seq,
-                )
-                for number, piece, target in final_pieces(source)
-            ]
-
-        def keep_copies(source):
-            return [
-                pltpu.make_async_copy(piece, target, keep.at[source, number])
-                for number, piece, target in final_pieces(source)
-            ]
-
-        def partial(slot):
-            return dot(grad_joint[slot], columns[:, :JOINT_COLS], 1, 1) + dot(
-                grad_inner[slot], columns[:, JOINT_COLS:], 1, 1
+            pieces = []
+            for number, (which, start, at, width) in enumerate(column_places(source)):
+                piece = arrived_up.at[source] if which else arrived.at[source, :, pl.ds(at, width)]
+                pieces.append((number, piece, outputs[which].at[part_rows, pl.ds(start, width)]))
+            return pieces
+
+        def back_copy(number, piece, target, source):
+            return to_axis(
+                piece,
+                target,
+                back_send.at[source, number],
+                back_recv.at[source, number],
+                "seq",
+                1 - seq,
             )
 
-        def product(turn):
-            block = block_of(turn)
-            load_strip(turn).wait()
-
-            @pl.when(turn + 1 < GROUP)
-            def _():
-                load_strip(turn + 1).start()
-
-            strip = strips[lax.rem(turn, 2)].reshape(GROUP * rows, SHARE)
-            mine[block, :, :JOINT_COLS] = dot(
-                strip, grad_joint[...].reshape(GROUP * rows, JOINT_COLS), 0, 0
-            ).astype(jnp.bfloat16)
-            mine[block, :, JOINT_COLS:] = dot(
-                strip, grad_inner[...].reshape(GROUP * rows, FEED_COLS), 0, 0
-            ).astype(jnp.bfloat16)
-            if collects:
-                cross_copy(block).start()
+        def keep_copy(number, piece, target, source):
+            return pltpu.make_async_copy(piece, target, keep.at[source, number])
+
+        def pass_on(source, which):
+            for number, piece, target in final_pieces(source):
+                if (number == PLACES - 1) == (which == 1):
+                    back_copy(number, piece, target, source).start()
+                    keep_copy(number, piece, target, source).start()
 
         def add(turn):
             block = block_of(turn)
@@ -1386,22 +1488,55 @@
         def other_work(turn):
             product(turn)
             if collects:
+                cross_copy(block_of(turn)).start()
 
                 @pl.when(turn >= SIDE)
                 def _():
                     add(turn - SIDE)
 
+        def late_work(step):
+            def pass_up(more, carry):
+                number = SIDE * step + more
+                source = lax.rem(me + GROUP - number, GROUP)
+
+                @pl.when(number == 0)
+                def _():
+                    own_up.wait()
+
+                @pl.when(number > 0)
+                def _():
+                    block = arrived_up.at[source]
+                    to_peer(block, block, up_send.at[number], up_recv.at[source], source).wait_recv()
+
+                pass_on(source, 1)
+                return carry
+
+            lax.fori_loop(0, SIDE, pass_up, 0)
+
         def last_adds(turn, carry):
             add(turn)
             return carry
 
-        load_strip(0).start()
+        def send_up(step, carry):
+            up_copy(step).start()
+            return carry
+
+        wait_all(loads[:3])
+        if collects:
+            own_up = pltpu.make_async_copy(inputs[7].at[me], arrived_up.at[me], up_own)
+            own_up.start()
+            lax.fori_loop(1, GROUP, send_up, 0)
         scatter_events(
-            partial, other_work, SCATTER_OPS_EARLY if collects else SCATTER_OPS_WORK, scratch
+            partial,
+            other_work,
+            late_work if collects else None,
+            SCATTER_OPS_EARLY if collects else SCATTER_OPS_WORK,
+            scratch,
         )
         if collects:
             lax.fori_loop(GROUP - SIDE, GROUP, last_adds, 0)
             arrived[me] = summed[me]
+        wait_all(loads[3:])
 
         def norm_back(part, sums):
             values = hidden[part].astype(jnp.float32)
@@ -1429,9 +1564,9 @@
             row = jnp.sum(folded, axis=0, keepdims=True)
             for block in range(GROUP):
                 shares[block, number : number + 1] = row[:, block * SHARE : (block + 1) * SHARE]
-        ones = jnp.ones((16, GROUP * rows), jnp.bfloat16)
-        joint_bias = dot(ones, grad_joint[...].reshape(GROUP * rows, JOINT_COLS))[:1]
-        upper_bias = dot(ones, grad_inner[...].reshape(GROUP * rows, FEED_COLS))[:1]
+        ones = jnp.ones((16, tokens), jnp.bfloat16)
+        joint_bias = dot(ones, grad_joint[...].reshape(tokens, JOINT_COLS))[:1]
+        upper_bias = dot(ones, grad_inner[...].reshape(tokens, FEED_COLS))[:1]
         for part in range(3):
             at = part * GROUP + me
             shares[at // 3, pl.ds(3 + lax.rem(at, 3), 1)] = joint_bias[
@@ -1453,7 +1588,7 @@
         lax.fori_loop(1, GROUP, small_begin, 0)
         small_land[me] = shares[me]
 
-        def pass_on(step, carry):
+        def pass_joint(step, carry):
             source = lax.rem(me + GROUP - step, GROUP)
 
             @pl.when(step > 0)
@@ -1466,12 +1601,11 @@
                     source,
                 ).wait_recv()
 
-            for copy in back_copies(source) + keep_copies(source):
-                copy.start()
+            pass_on(source, 0)
             return carry
 
         if collects:
-            lax.fori_loop(0, GROUP, pass_on, 0)
+            lax.fori_loop(0, GROUP, pass_joint, 0)
 
         def small_end(step, carry):
             source = lax.rem(me + GROUP - step, GROUP)
@@ -1499,16 +1633,23 @@
             def _():
                 plane_copy(block).wait_send()
 
-            for copy in back_copies(block) + keep_copies(block):
-                copy.wait()
+            @pl.when(block > 0)
+            def _():
+                up_copy(block).wait_send()
+
+            for number, piece, target in final_pieces(block):
+                back_copy(number, piece, target, block).wait()
+                keep_copy(number, piece, target, block).wait()
             return carry
 
         if collects:
             lax.fori_loop(0, GROUP, end, 0)
 
-    part = pltpu.VMEM((GROUP, half, COLS), jnp.bfloat16)
-    whole = (GROUP, SHARE, COLS)
+    def part(width, height=half):
+        return pltpu.VMEM((GROUP, height, width), jnp.bfloat16)
+
     small = (SMALL_ROWS, SHARE)
+    sixteen, places = pltpu.SemaphoreType.DMA((GROUP,)), pltpu.SemaphoreType.DMA((GROUP, PLACES))
     return pl.pallas_call(
         kernel,
         out_shape=(
@@ -1521,29 +1662,43 @@
                 jax.ShapeDtypeStruct((SHARE, FF), jnp.bfloat16),
             )
             if collects
-            else (jax.ShapeDtypeStruct(whole, jnp.bfloat16),)
+            else (jax.ShapeDtypeStruct((GROUP, SHARE, COLS), jnp.bfloat16),)
         ),
-        in_specs=[VMEM] * 6 + [HBM],
+        in_specs=[HBM, HBM, VMEM] + [HBM] * (5 if collects else 4),
         out_specs=(VMEM, VMEM) + ((HBM, HBM) if collects else (VMEM,)),
-        scratch_shapes=([pltpu.VMEM(whole, jnp.bfloat16)] if collects else [])
-        + [pltpu.VMEM((2, GROUP, rows, SHARE), jnp.bfloat16)]
-        + ([part] * 3 if collects else [])
+        scratch_shapes=[
+            pltpu.VMEM(array.shape, array.dtype)
+            for array in (hidden, grad, grad_joint, grad_inner, columns)
+        ]
         + [
+            pltpu.SemaphoreType.DMA((5,)),
+            pltpu.VMEM((2, GROUP, rows, SHARE), jnp.bfloat16),
+            pltpu.SemaphoreType.DMA((2,)),
             pltpu.VMEM((GROUP,) + small, jnp.float32),
             pltpu.VMEM((GROUP,) + small, jnp.float32),
             pltpu.VMEM(small, jnp.float32),
             pltpu.VMEM(small, jnp.float32),
-            pltpu.SemaphoreType.DMA((2,)),
+            sixteen,
+            sixteen,
+            pltpu.SemaphoreType.DMA,
+            pltpu.SemaphoreType.DMA,
         ]
-        + [pltpu.SemaphoreType.DMA((GROUP,))] * 4
-        + [pltpu.SemaphoreType.DMA((GROUP, PLACES))] * 3
-        + [pltpu.SemaphoreType.DMA((GROUP,))] * 2
-        + [pltpu.SemaphoreType.DMA] * 2
+        + (
+            [part(JOINT_COLS, SHARE)]
+            + [part(JOINT_COLS)] * 3
+            + [part(FEED_COLS)]
+            + [sixteen] * 4
+            + [places] * 3
+            + [sixteen] * 2
+            + [pltpu.SemaphoreType.DMA]
+            if collects
+            else []
+        )
         + scatter_scratch(rows),
         compiler_params=pltpu.CompilerParams(
             collective_id=20 + layer, has_side_effects=True, vmem_limit_bytes=ROOM
         ),
-    )(hidden, grad, gain, grad_joint, grad_inner, columns, every)
+    )(hidden, grad, gain, grad_joint, grad_inner, columns, every, *((up,) if collects else ()))
 
 
 def gather_small(packed):
@@ -1653,6 +1808,77 @@
     return begin, end
 
 
+def up_products(every, feed, out, scratch):
+    feed_part, strips, mine, other, feed_sem, load, cross_send, cross_recv = scratch
+    rows = feed.shape[1]
+    tokens = GROUP * rows
+    half = SHARE // 2
+    seq = lax.axis_index("seq")
+    me = lax.axis_index("ctx") * SIDE + lax.axis_index("fsdp")
+    part_rows = pl.ds(pl.multiple_of(seq * half, half), half)
+    other_rows = pl.ds(pl.multiple_of((1 - seq) * half, half), half)
+
+    def load_strip(turn):
+        start = pl.multiple_of(lax.rem(me + 1 + turn, GROUP) * SHARE, SHARE)
+        buffer = lax.rem(turn, 2)
+        return pltpu.make_async_copy(
+            every.at[:, :, pl.ds(start, SHARE)], strips.at[buffer], load.at[buffer]
+        )
+
+    def cross_copy(block):
+        return to_axis(
+            mine.at[block, other_rows],
+            other.at[block],
+            cross_send.at[block],
+            cross_recv.at[block],
+            "seq",
+            1 - seq,
+        )
+
+    def feed_copy():
+        return pltpu.make_async_copy(feed, feed_part, feed_sem)
+
+    def begin():
+        feed_copy().start()
+        load_strip(jnp.int32(0)).start()
+
+    def product(turn, carry):
+        block = lax.rem(me + 1 + turn, GROUP)
+        load_strip(turn).wait()
+
+        @pl.when(turn == 0)
+        def _():
+            feed_copy().wait()
+
+        @pl.when(turn + 1 < GROUP)
+        def _():
+            load_strip(turn + 1).start()
+
+        strip = strips[lax.rem(turn, 2)].reshape(tokens, SHARE)
+        mine[block] = dot(strip, feed_part[...].reshape(tokens, FEED_COLS), 0, 0).astype(
+            jnp.bfloat16
+        )
+        cross_copy(block).start()
+        return carry
+
+    def add(turn, carry):
+        block = lax.rem(me + 1 + turn, GROUP)
+        cross_copy(block).wait()
+        out[block] = (
+            mine[block, part_rows].astype(jnp.float32) + other[block].astype(jnp.float32)
+        ).astype(jnp.bfloat16)
+        return carry
+
+    def make(step):
+        lax.fori_loop(SIDE * step, SIDE * step + SIDE, product, 0)
+        lax.fori_loop(SIDE * jnp.maximum(step - 1, 0), SIDE * step, add, 0)
+
+    def end():
+        lax.fori_loop(GROUP - SIDE, GROUP, add, 0)
+
+    return begin, make, end
+
+
 def row_exchange(summed, outputs, sems):
     plane_send, plane_recv, own_sem = sems
     me = lax.axis_index("ctx") * SIDE + lax.axis_index("fsdp")
@@ -1670,7 +1896,7 @@
         return pltpu.make_async_copy(*piece(me, number), own_sem.at[number])
 
     def begin():
-        greet_plane(GROUP, False)
+        greet_plane(GROUP)
 
         def send(step, carry):
             for number in range(PLACES):
@@ -1789,7 +2015,9 @@
     return mixed.reshape(GROUP, rows, HEAD_COLS), turned, stats, *land
 
 
-def attend_plane_back(query, key, value, begin, spot, turned, stats, grad, tables, summed=None):
+def attend_plane_back(
+    query, key, value, begin, spot, turned, stats, grad, tables, summed=None, every=None, feed=None
+):
     rows = query.shape[1]
     length = SIDE * rows
     scale = 1.0 / math.sqrt(HEAD_DIM)
@@ -1798,9 +2026,16 @@
 
     def kernel(query, key, value, grad, cosine, sine, begin, spot, turned, stats, *refs):
         if extra:
-            out, grad_k, grad_v = refs[1], refs[4], refs[5]
-            begin_exchange, end_exchange = row_exchange(refs[0], refs[2:4], refs[6:])
-            pl.when(pl.program_id(0) == 0)(begin_exchange)
+            summed, every, feed, out = refs[:4]
+            up_out, grad_k, grad_v = refs[6], refs[7], refs[8]
+            begin_exchange, end_exchange = row_exchange(summed, refs[4:6], refs[9:12])
+            begin_up, make_up, end_up = up_products(every, feed, up_out, refs[12:])
+
+            @pl.when(pl.program_id(0) == 0)
+            def _():
+                begin_up()
+                begin_exchange()
+
         else:
             out, grad_k, grad_v = refs
         keys = key[:, 0].reshape(length, HEAD_COLS)
@@ -1848,7 +2083,13 @@
             )
             out[chunk, 0, :, 2 * HEAD_COLS :] = grad_v[place].astype(jnp.bfloat16)
         if extra:
-            pl.when(pl.program_id(0) == SIDE - 1)(end_exchange)
+            make_up(pl.program_id(0))
+
+            @pl.when(pl.program_id(0) == SIDE - 1)
+            def _():
+                end_up()
+                end_exchange()
+
 
     def spec(height, width):
         return pl.BlockSpec((SIDE, 1, height, width), lambda step: (0, step, 0, 0))
@@ -1857,6 +2098,7 @@
     halves = (
         jax.ShapeDtypeStruct((half, 3 * D), jnp.bfloat16),
         jax.ShapeDtypeStruct((half, FF), jnp.bfloat16),
+        jax.ShapeDtypeStruct((GROUP, half, FEED_COLS), jnp.bfloat16),
     )
     out, *halves = pl.pallas_call(
         kernel,
@@ -1870,10 +2112,29 @@
             spec(HEAD_COLS, rows),
             pl.BlockSpec((1, 2 * OWN, length), lambda step: (step, 0, 0)),
         ]
-        + [HBM] * (1 if extra else 0),
-        out_specs=(spec(rows, JOINT_COLS),) + ((HBM, HBM) if extra else ()),
+        + [HBM] * (3 if extra else 0),
+        out_specs=(spec(rows, JOINT_COLS),)
+        + (
+            (HBM, HBM, pl.BlockSpec((GROUP, half, FEED_COLS), lambda step: (0, 0, 0)))
+            if extra
+            else ()
+        ),
         scratch_shapes=[pltpu.VMEM((length, HEAD_COLS), jnp.float32)] * 2
-        + (EXCHANGE_SEMS if extra else []),
+        + (
+            EXCHANGE_SEMS
+            + [
+                pltpu.VMEM((GROUP, rows, FEED_COLS), jnp.bfloat16),
+                pltpu.VMEM((2, GROUP, rows, SHARE), jnp.bfloat16),
+                pltpu.VMEM((GROUP, SHARE, FEED_COLS), jnp.bfloat16),
+                pltpu.VMEM((GROUP, half, FEED_COLS), jnp.bfloat16),
+                pltpu.SemaphoreType.DMA,
+                pltpu.SemaphoreType.DMA((2,)),
+                pltpu.SemaphoreType.DMA((GROUP,)),
+                pltpu.SemaphoreType.DMA((GROUP,)),
+            ]
+            if extra
+            else []
+        ),
         compiler_params=pltpu.CompilerParams(
             collective_id=41, has_side_effects=True, vmem_limit_bytes=ROOM
         )
@@ -1888,7 +2149,7 @@
         spot,
         turned,
         stats,
-        *((summed,) if extra else ()),
+        *((summed, every, feed) if extra else ()),
     )
     return out.reshape(GROUP, rows, JOINT_COLS), *halves
 
@@ -2015,10 +2276,21 @@
         branch_grads.insert(
             0, branch.astype(jnp.float32) + swapped(branch).astype(jnp.float32)
         )
-        grad_joint, *halves = attend_plane_back(
-            query, key, value, begin, spot, turned, stats, grad_mixed, tables, summed
-        )
-        for grads, own in zip((joint_grads, upper_grads), halves):
+        grad_joint, *rest = attend_plane_back(
+            query,
+            key,
+            value,
+            begin,
+            spot,
+            turned,
+            stats,
+            grad_mixed,
+            tables,
+            summed,
+            every,
+            grad_inner,
+        )
+        for grads, own in zip((joint_grads, upper_grads), rest[:2]):
             other = swapped(own)
             grads.insert(
                 0,
@@ -2035,6 +2307,7 @@
             columns.reshape(D, COLS),
             every,
             layer,
+            rest[2] if rest else None,
         )
         small_grads.insert(0, small)
         if layer > 0:

time: 1180 us -> 1160 us (0.983)
    pallas_call x2, Pallas kernels: 70.9 us -> 103 us  [attend_plane_back(): pl.pallas_call(kernel, grid=(SIDE,), out_shape=(jax.ShapeDtypeStruct((SID...]
    pallas_call x2, Pallas kernels: 276 us -> 248 us  [backward_scatter(): pl.pallas_call(kernel, out_shape=(jax.ShapeDtypeStruct((rows, D), jnp.flo...]
where the time goes in v2:
time: 1160 us; the launch traced here: 1150 us
  Pallas kernels  1060 us (91%)
  other arithmetic  38.1 us (3%)
  waiting for transfers between devices  24.5 us (2%)
  local copies, waits for them, and re-layouts  24.2 us (2%)
    pallas_call x2, Pallas kernels, backward_scatter(): pl.pallas_call(kernel, out_shape=(jax.ShapeDtypeStruct((rows, D), jnp.flo...  248 us
    pallas_call x2, Pallas kernels, forward_gather(): pl.pallas_call(kernel, out_shape=out_shape, in_specs=[VMEM] * 4 + [VMEM i...  246 us
    pallas_call x2, Pallas kernels, backward_gather(): pl.pallas_call(kernel, out_shape=(jax.ShapeDtypeStruct((GROUP, rows, HEAD...  191 us
    pallas_call x2, Pallas kernels, forward_scatter(): pl.pallas_call(kernel, out_shape=jax.ShapeDtypeStruct((rows, D), jnp.floa...  188 us
    pallas_call x2, Pallas kernels, attend_plane_back(): pl.pallas_call(kernel, grid=(SIDE,), out_shape=(jax.ShapeDtypeStruct((SID...  103 us
    pallas_call x2, Pallas kernels, attend_plane(): pl.pallas_call(kernel, grid=(SIDE,), out_shape=(shape(rows, HEAD_COLS, jn...  68.6 us
    ppermute x6, waiting for transfers between devices, swapped(): return lax.ppermute(values, 'seq', swap)  24.5 us
  transfers between devices with their start and end apart: 6, of which 1 were waited for; matrix products, arithmetic and copies ran while one was open for 3% of the time, Pallas kernels for 35%

profile of v2, /device:TPU:0, one launch (start us, length us, event | category | flops | bytes accessed | tf_op | source)
XLA Modules:
  0.0 1149.6 jit_solution(16266660842502422526)
XLA Ops:
  2.7 2.7 concatenate.12
  6.1 11.9 %shard_map.238 = bf16[16,32,128]{2,1,0:T(8,128)(2,1)} custom-call(bf16[32,128]{1,0:T(8,128)(2,1)} %pad_bitcast_fusion.packed), custom_call_target="tpu_custom_call" | custom-call | tf_op jit(solution)/shard_map/pallas_call | solution.py:1730
  20.8 3.3 reshape.331.turn_a
  27.7 145.7 %shard_map.239 = (bf16[16,256,2048]{2,1,0:T(8,128)(2,1)}, bf16[16,128,896]{2,1,0:T(8,128)(2,1)}, bf16[16,256,128]{2,1,0:T(8,128)(2,1)}, bf16[16,256,128]{2,1,0:T...) custom-call(bf16[256,2048]{1,0:T(8,128)(2,1)} %bitcast.124, ...), custom_call_target="tpu_custom_call" | custom-call | tf_op jit(solution)/shard_map/pallas_call | solution.py:949
  173.5 49.3 %shard_map.240 = (bf16[4,4,256,128]{3,2,1,0:T(8,128)(2,1)}, f32[4,4,128,256]{3,2,1,0:T(8,128)}, f32[4,4,1024]{2,1,0:T(4,128)}, bf16[16,64,896]{2,1,0:T(8,128)(2,1)}) custom-call(bf16[4,4,256,128]{3,2,1,0:T(8,128)(2,1)} %bitcast.127, bf16[4,4,256,128]{3,2,1,0:T(8,128)(2,1)} %bitcast.129, bf16[4,4,256,128]{3,2,1,0:T(8,128)(2,1)} %bitcast.131, ...), custom_call_target="tpu_custom_call" | custom-call | tf_op jit(solution)/shard_map/pallas_call | solution.py:1982
  225.1 4.8 slice_bitcast_fusion
  229.9 94.1 %shard_map.241.hidden.refs_0_ = f32[256,2048]{1,0:T(8,128)} custom-call(bf16[256,2048]{1,0:T(8,128)(2,1)} %bitcast.125, f32[1,2048]{1,0:T(1,128)} %get-tuple-element.107.bias, bf16[16,256,128]{2,1,0:T(8,128)(2,1)} %bitcast.133, bf16[16,256,512]{2,1,0:T(8,128)(2,1)} %get-tuple-element.56.active, bf16[128,2048]{1,0:T(8,128)(2,1)} %get-tuple-element.101.out_weight, ...), custom_call_target="tpu_custom_call" | custom-call | tf_op jit(solution)/shard_map/pallas_call | solution.py:1335
  327.2 99.9 %shard_map.242 = (bf16[16,256,2048]{2,1,0:T(8,128)(2,1)}, bf16[16,128,896]{2,1,0:T(8,128)(2,1)}, bf16[16,256,128]{2,1,0:T(8,128)(2,1)}, bf16[16,256,128]{2,1,0:T...) custom-call(f32[256,2048]{1,0:T(8,128)} %shard_map.241.hidden.refs_0_, ...), custom_call_target="tpu_custom_call" | custom-call | tf_op jit(solution)/shard_map/pallas_call | solution.py:949
  427.1 19.3 %shard_map.243 = (bf16[4,4,256,128]{3,2,1,0:T(8,128)(2,1)}, f32[4,4,128,256]{3,2,1,0:T(8,128)}, f32[4,4,1024]{2,1,0:T(4,128)}) custom-call(bf16[4,4,256,128]{3,2,1,0:T(8,128)(2,1)} %bitcast.137, bf16[4,4,256,128]{3,2,1,0:T(8,128)(2,1)} %bitcast.139, bf16[4,4,256,128]{3,2,1,0:T(8,128)(2,1)} %bitcast.141, s32[4,1,1024]{2,1,0:T(1,128)} %broadcast_in_dim.43.begin, ...), custom_call_target="tpu_custom_call" | custom-call | tf_op jit(solution)/shard_map/pallas_call | solution.py:1982
  446.4 96.9 %shard_map.245 = (f32[16,256,128]{2,1,0:T(8,128)}, bf16[16,256,512]{2,1,0:T(8,128)(2,1)}, bf16[640,2048]{1,0:T(8,128)(2,1)}) custom-call(bf16[256,2048]{1,0:T(8,128)(2,1)} %get-tuple-element.98.own, bf16[128,2048]{1,0:T(8,128)(2,1)} %get-tuple-element.100.out_weight, bf16[512,2048]{1,0:T(8,128)(2,1)} %get-tuple-element.92.down_weight, ...), custom_call_target="tpu_custom_call" | custom-call | tf_op jit(solution)/shard_map/pallas_call | solution.py:1047
  543.3 21.6 %shard_map.246 = bf16[4,4,256,384]{3,2,1,0:T(8,128)(2,1)} custom-call(bf16[4,4,256,128]{3,2,1,0:T(8,128)(2,1)} %bitcast.138, bf16[4,4,256,128]{3,2,1,0:T(8,128)(2,1)} %bitcast.140, bf16[4,4,256,128]{3,2,1,0:T(8,128)(2,1)} %bitcast.142, f32[4,4,256,128]{3,2,1,0:T(8,128)} %bitcast.147, f32[4,4,256,128]{3,2,1,0:T(8,128)} %bitcast.119, ...), custom_call_target="tpu_custom_call" | custom-call | tf_op jit(solution)/shard_map/pallas_call | solution.py:2103
  564.9 109.2 %shard_map.247 = (f32[256,2048]{1,0:T(8,128)}, f32[16,128]{1,0:T(8,128)}, bf16[16,128,896]{2,1,0:T(8,128)(2,1)}) custom-call(f32[256,2048]{1,0:T(8,128)} %shard_map.241.hidden.refs_0_, f32[256,2048]{1,0:T(8,128)} %get-tuple-element.99.refs_1_, f32[1,2048]{1,0:T(1,128)} %get-tuple-element.120.gain.refs_2_, bf16[16,256,384]{2,1,0:T(8,128)(2,1)} %bitcast.123, ...), custom_call_target="tpu_custom_call" | custom-call | tf_op jit(solution)/shard_map/pallas_call | solution.py:1653
  674.2 2.7 convert_element_type.198.own
  676.9 94.2 %shard_map.248 = (f32[16,256,128]{2,1,0:T(8,128)}, bf16[16,256,512]{2,1,0:T(8,128)(2,1)}, bf16[640,2048]{1,0:T(8,128)(2,1)}) custom-call(bf16[256,2048]{1,0:T(8,128)(2,1)} %convert_element_type.198.own, bf16[128,2048]{1,0:T(8,128)(2,1)} %get-tuple-element.101.out_weight, bf16[512,2048]{1,0:T(8,128)(2,1)} %get-tuple-element.93.down_weight, ...), custom_call_target="tpu_custom_call" | custom-call | tf_op jit(solution)/shard_map/pallas_call | solution.py:1047
  775.1 94.2 %shard_map.244 = f32[256,2048]{1,0:T(8,128)} custom-call(f32[256,2048]{1,0:T(8,128)} %shard_map.241.hidden.refs_0_, f32[1,2048]{1,0:T(1,128)} %get-tuple-element.106.bias, bf16[16,256,128]{2,1,0:T(8,128)(2,1)} %bitcast.136, bf16[16,256,512]{2,1,0:T(8,128)(2,1)} %get-tuple-element.64.active, bf16[128,2048]{1,0:T(8,128)(2,1)} %get-tuple-element.100.out_weight, ...), custom_call_target="tpu_custom_call" | custom-call | tf_op jit(solution)/shard_map/pallas_call | solution.py:1335
  872.0 3.3 add_convert_fusion.refs_0_
  875.3 81.4 %shard_map.249 = (bf16[4,4,256,384]{3,2,1,0:T(8,128)(2,1)}, bf16[64,6144]{1,0:T(8,128)(2,1)}, bf16[64,8192]{1,0:T(8,128)(2,1)}, bf16[16,64,512]{2,1,0:T(8,128)(2,1)}) custom-call(bf16[4,4,256,128]{3,2,1,0:T(8,128)(2,1)} %bitcast.128, bf16[4,4,256,128]{3,2,1,0:T(8,128)(2,1)} %bitcast.130, bf16[4,4,256,128]{3,2,1,0:T(8,128)(2,1)} %bitcast.132, ...), custom_call_target="tpu_custom_call" | custom-call | tf_op jit(solution)/shard_map/pallas_call | solution.py:2103
  956.7 138.5 %shard_map.250 = (f32[256,2048]{1,0:T(8,128)}, f32[16,128]{1,0:T(8,128)}, bf16[128,6144]{1,0:T(8,128)(2,1)}, bf16[128,8192]{1,0:T(8,128)(2,1)}) custom-call(bf16[256,2048]{1,0:T(8,128)(2,1)} %bitcast.126, f32[256,2048]{1,0:T(8,128)} %get-tuple-element.72.refs_1_, f32[1,2048]{1,0:T(1,128)} %get-tuple-element.119.gain.refs_2_, ...), custom_call_target="tpu_custom_call" | custom-call | tf_op jit(solution)/shard_map/pallas_call | solution.py:1653
  1101.2 2.8 add_bitcast_fusion.1
  1104.0 3.6 add_bitcast_fusion
  1107.6 4.0 pad_maximum_fusion
  1111.6 24.4 %collective-permute-done.2 = bf16[64,6144]{1,0:T(8,128)(2,1)S(1)} collective-permute-done((bf16[64,6144]{1,0:T(8,128)(2,1)}, bf16[64,6144]{1,0:T(8,128)(2,1)S(1)}, u32[]{:S(2)}, u32[]{:S(2)}) %collective-permute-start.2) | collective-permute-done | bytes 786464 | tf_op jit(solution)/shard_map/ppermute | solution.py:2225
  1138.5 3.1 maximum_convert_fusion.1
  1143.3 3.9 maximum_convert_fusion
  (85 shorter events, 33.3 us)
Async XLA Ops:
  173.5 50.6 %copy-start.13 = (s32[1,256]{1,0:T(1,128)S(1)}, s32[1,256]{1,0:T(1,128)}, u32[]{:S(2)}) copy-start(s32[1,256]{1,0:T(1,128)} %param.17) | copy-start | bytes 3076
  173.5 50.6 %copy-start.9 = (bf16[2,128,2048]{2,1,0:T(8,128)(2,1)S(1)}, bf16[2,128,2048]{2,1,0:T(8,128)(2,1)}, u32[]{:S(2)}) copy-start(bf16[2,128,2048]{2,1,0:T(8,128)(2,1)} %param.22) | copy-start | bytes 3145732
  222.8 103.2 %collective-permute-start = (bf16[16,64,896]{2,1,0:T(8,128)(2,1)}, bf16[16,64,896]{2,1,0:T(8,128)(2,1)S(1)}, u32[]{:S(2)}, u32[]{:S(2)}) collective-permute-start(bf16[16,64,896]{2,1,0:T(8,128)(2,1)} %get-tuple-element.59.source_a), channel_id=1, source_target_pairs={{0,16},{16,0},{1,17},{17,1},{2,18},{18,2},{3,19},{19,3},{4,20},{20... | collective-permute-start | bytes 5505032 | tf_op jit(solution)/shard_map/ppermute | solution.py:2225
  229.9 94.1 %copy-start.7 = (bf16[1,256,2048]{2,1,0:T(8,128)(2,1)S(1)}, bf16[1,256,2048]{2,1,0:T(8,128)(2,1)}, u32[]{:S(2)}) copy-start(bf16[1,256,2048]{2,1,0:T(8,128)(2,1)} %param.28) | copy-start | bytes 3145732
  326.0 1.2 copy-start.5
  676.9 94.8 %copy-start = (bf16[16,128,896]{2,1,0:T(8,128)(2,1)S(1)}, bf16[16,128,896]{2,1,0:T(8,128)(2,1)}, u32[]{:S(2)}) copy-start(bf16[16,128,896]{2,1,0:T(8,128)(2,1)} %get-tuple-element.77) | copy-start | bytes 11010052
  771.1 330.1 %collective-permute-start.3 = (bf16[640,2048]{1,0:T(8,128)(2,1)}, bf16[640,2048]{1,0:T(8,128)(2,1)}, u32[]{:S(2)}, u32[]{:S(2)}) collective-permute-start(bf16[640,2048]{1,0:T(8,128)(2,1)} %get-tuple-element.88), channel_id=1, source_target_pairs={{0,16},{16,0},{1,17},{17,1},{2,18},{18,2},{3,19},{19,3},{4,20},{20... | collective-permute-start | bytes 7864328 | tf_op jit(solution)/shard_map/ppermute | solution.py:2225
  773.1 98.9 %collective-permute-start.1 = (bf16[16,64,896]{2,1,0:T(8,128)(2,1)}, bf16[16,64,896]{2,1,0:T(8,128)(2,1)}, u32[]{:S(2)}, u32[]{:S(2)}) collective-permute-start(bf16[16,64,896]{2,1,0:T(8,128)(2,1)} %constant_dynamic-slice_fusion), channel_id=1, source_target_pairs={{0,16},{16,0},{1,17},{17,1},{2,18},{18,2},{3,19},{19,3},{4,20},{20... | collective-permute-start | bytes 5505032 | tf_op jit(solution)/shard_map/ppermute | solution.py:2225
  774.6 329.4 %collective-permute-start.4 = (bf16[640,2048]{1,0:T(8,128)(2,1)}, bf16[640,2048]{1,0:T(8,128)(2,1)}, u32[]{:S(2)}, u32[]{:S(2)}) collective-permute-start(bf16[640,2048]{1,0:T(8,128)(2,1)} %get-tuple-element.89), channel_id=1, source_target_pairs={{0,16},{16,0},{1,17},{17,1},{2,18},{18,2},{3,19},{19,3},{4,20},{20... | collective-permute-start | bytes 7864328 | tf_op jit(solution)/shard_map/ppermute | solution.py:2225
  775.1 96.9 %copy-start.1 = (bf16[16,128,896]{2,1,0:T(8,128)(2,1)S(1)}, bf16[16,128,896]{2,1,0:T(8,128)(2,1)}, u32[]{:S(2)}) copy-start(bf16[16,128,896]{2,1,0:T(8,128)(2,1)} %get-tuple-element.77) | copy-start | bytes 11010052
  956.7 138.5 %copy-start.11 = (f32[16,128]{1,0:T(8,128)S(1)}, f32[16,128]{1,0:T(8,128)}, u32[]{:S(2)}) copy-start(f32[16,128]{1,0:T(8,128)} %get-tuple-element.85) | copy-start | bytes 24580
  956.7 139.8 %copy-start.8 = (bf16[64,8192]{1,0:T(8,128)(2,1)S(1)}, bf16[64,8192]{1,0:T(8,128)(2,1)}, u32[]{:S(2)}) copy-start(bf16[64,8192]{1,0:T(8,128)(2,1)} %get-tuple-element.91) | copy-start | bytes 3145732
  956.7 144.5 %copy-start.2 = (bf16[640,2048]{1,0:T(8,128)(2,1)S(1)}, bf16[640,2048]{1,0:T(8,128)(2,1)}, u32[]{:S(2)}) copy-start(bf16[640,2048]{1,0:T(8,128)(2,1)} %get-tuple-element.88) | copy-start | bytes 7864324
  1096.5 45.1 %collective-permute-start.5 = (bf16[64,8192]{1,0:T(8,128)(2,1)S(1)}, bf16[64,8192]{1,0:T(8,128)(2,1)S(1)}, u32[]{:S(2)}, u32[]{:S(2)}) collective-permute-start(bf16[64,8192]{1,0:T(8,128)(2,1)S(1)} %copy-done.8), channel_id=1, source_target_pairs={{0,16},{16,0},{1,17},{17,1},{2,18},{18,2},{3,19},{19,3},{4,20},{20... | collective-permute-start | bytes 3145736 | tf_op jit(solution)/shard_map/ppermute | solution.py:2225
  1098.3 37.7 %collective-permute-start.2 = (bf16[64,6144]{1,0:T(8,128)(2,1)}, bf16[64,6144]{1,0:T(8,128)(2,1)S(1)}, u32[]{:S(2)}, u32[]{:S(2)}) collective-permute-start(bf16[64,6144]{1,0:T(8,128)(2,1)} %get-tuple-element.87), channel_id=1, source_target_pairs={{0,16},{16,0},{1,17},{17,1},{2,18},{18,2},{3,19},{19,3},{4,20},{20... | collective-permute-start | bytes 2359304 | tf_op jit(solution)/shard_map/ppermute | solution.py:2225
  1101.2 46.1 %copy-start.12 = (f32[2,1,128]{2,1,0:T(1,128)}, f32[2,1,128]{2,1,0:T(1,128)S(1)}, u32[]{:S(2)}) copy-start(f32[2,1,128]{2,1,0:T(1,128)S(1)} %get-tuple-element.108) | copy-start | bytes 3076
  1107.6 28.5 %copy-start.10 = (bf16[64,6144]{1,0:T(8,128)(2,1)S(1)}, bf16[64,6144]{1,0:T(8,128)(2,1)}, u32[]{:S(2)}) copy-start(bf16[64,6144]{1,0:T(8,128)(2,1)} %get-tuple-element.87) | copy-start | bytes 2359300
  1136.3 2.2 copy-start.6
  1141.7 1.6 copy-start.4
  1143.3 4.5 copy-start.3

commit v3 on v2

--- a/solution.py
+++ b/solution.py
@@ -478,6 +478,14 @@
     return lax.rem(lax.shift_right_logical(word, 2 * lax.rem(index, 8)), 4)
 
 
+def nibble(entries, index):
+    word = jnp.int32(0)
+    for start in range(0, len(entries), 7):
+        packed = sum(entry << (4 * place) for place, entry in enumerate(entries[start : start + 7]))
+        word = jnp.where(index >= start, jnp.int32(packed), word)
+    return lax.rem(lax.shift_right_logical(word, 4 * lax.rem(index, 7)), 16)
+
+
 def digit_of_row(table, row, index):
     value = digit(table[0], index)
     for number in range(1, len(table)):
@@ -569,6 +577,18 @@
     (1, 0, 1, 2, 3, 1, 2, 0, 0, 3, 3, 2, 2, 3, 0, 3, 1, 0, 1, 3, 2, 3, 3, 3, 0, 3, 1, 2, 0, 3, 1, 3, 2, 3, 1, 0, 2, 3, 3, 3),
     (1, 0, 2, 0, 2, 0, 2, 3, 1, 1, 0, 3, 2, 3, 3, 1, 3, 3, 0, 0, 2, 3, 1, 3, 1, 1, 2, 2, 3, 0, 3, 2, 3, 3, 0, 3, 1, 3, 3, 3),
 )
+FIRST_KIND = (
+    (0, 0, 0, 0, 0, 0, 0, 1, 0, 0, 0, 1, 0, 1, 0, 0, 0, 1, 0, 1, 1, 2, 0, 1, 0, 0, 0, 0, 1, 3, 0, 2, 3, 0, 2, 0, 2, 0, 3, 1, 0, 0, 3, 1, 1, 2, 2, 0, 1, 1, 0, 1, 1, 0, 1, 0, 1, 3, 3, 2, 1, 1, 1, 2, 3, 3),
+    (0, 0, 0, 0, 0, 1, 0, 0, 0, 0, 1, 0, 0, 0, 0, 2, 1, 0, 1, 0, 1, 0, 0, 0, 0, 0, 0, 2, 1, 0, 0, 1, 0, 2, 1, 0, 3, 1, 3, 0, 1, 2, 0, 0, 0, 1, 1, 1, 2, 3, 1, 1, 1, 1, 3, 3, 1, 3, 1, 0, 2, 2, 3, 1, 2, 3),
+)
+FIRST_STEP = (
+    (0, 0, 0, 1, 2, 0, 3, 0, 0, 0, 1, 0, 1, 0, 1, 2, 1, 1, 0, 1, 1, 0, 1, 1, 2, 3, 2, 2, 0, 1, 2, 1, 0, 0, 0, 1, 2, 0, 1, 2, 3, 2, 0, 0, 1, 1, 2, 3, 2, 2, 3, 2, 2, 3, 3, 3, 3, 2, 2, 3, 3, 3, 3, 3, 3, 3),
+    (0, 1, 2, 0, 0, 0, 0, 0, 0, 2, 0, 3, 0, 2, 1, 0, 0, 1, 0, 1, 1, 1, 2, 1, 2, 2, 3, 1, 1, 0, 3, 1, 3, 0, 1, 1, 1, 2, 1, 3, 2, 1, 3, 3, 0, 2, 2, 3, 3, 0, 2, 3, 3, 3, 0, 2, 3, 3, 0, 2, 2, 3, 3, 1, 2, 2),
+)
+FIRST_WHAT = (
+    (4, 5, 2, 4, 4, 0, 4, 0, 1, 6, 1, 1, 6, 2, 0, 6, 2, 2, 3, 0, 1, 3, 3, 3, 2, 6, 0, 1, 3, 3, 3, 3, 3, 7, 8, 8, 3, 8, 8, 0, 0, 8, 8, 8, 8, 8, 8, 1, 2, 1, 2, 3, 8, 3, 2, 8, 0, 3, 8, 3, 1, 3, 8, 8, 3, 8),
+    (4, 4, 4, 5, 0, 0, 1, 2, 3, 1, 1, 4, 6, 2, 0, 3, 2, 2, 3, 6, 0, 1, 0, 3, 3, 6, 6, 3, 1, 7, 0, 2, 2, 8, 3, 8, 3, 0, 8, 1, 2, 8, 3, 8, 8, 1, 3, 2, 3, 3, 8, 1, 0, 3, 8, 3, 8, 3, 8, 8, 3, 8, 8, 8, 8, 8),
+)
 OPS = len(GATHER_KIND[0])
 WORKS = tuple(
     tuple(
@@ -603,8 +623,12 @@
     return gather_slot(kind, step)[1]
 
 
-def gather_blocks(land, every, up, down, side, core, arrived, core_arrived, kept, work):
+def gather_blocks(
+    land, every, up, down, side, core, arrived, core_arrived, kept, work, tables=None, more=()
+):
     ctx, place, twin, across, _ = neighbours()
+    kinds, steps, parts = tables or (GATHER_KIND, GATHER_STEP, GATHER_PART)
+    at_end = (place == 0) | (place == SIDE - 1)
 
     def copies(kind, line, slot, part):
         start, size = PARTS[part]
@@ -629,9 +653,10 @@
             block, block, core.at[kind * SIDE + line], core_arrived.at[slot], "ctx", twin
         )
 
-    def step_op(number, worked):
-        kind, step = by_place(GATHER_KIND, number), by_place(GATHER_STEP, number)
-        part = by_place(GATHER_PART, number)
+    def step_op(number, counts):
+        worked, made = counts
+        kind, step = by_place(kinds, number), by_place(steps, number)
+        part = jnp.where(at_end, nibble(parts[0], number), nibble(parts[1], number))
         line, slot = gather_slot(kind, step)
         for which in range(len(PARTS)):
 
@@ -663,9 +688,15 @@
                 pltpu.make_async_copy(land.at[slot], every.at[slot], kept.at[slot]).start()
             work(worked, slot)
 
-        return worked + jnp.where(part == 3, 1, 0)
-
-    lax.fori_loop(0, OPS, step_op, jnp.int32(0))
+        for which, further in enumerate(more):
+
+            @pl.when(part == 4 + which)
+            def _(further=further):
+                further(step, slot, made)
+
+        return worked + jnp.where(part == 3, 1, 0), made + jnp.where(part == 8, 1, 0)
+
+    lax.fori_loop(0, len(kinds[0]), step_op, (jnp.int32(0), jnp.int32(0)))
 
     def finish(number, carry):
         kind, line = number // SIDE, lax.rem(number, SIDE)
@@ -749,34 +780,180 @@
         copy.wait()
 
 
-def forward_gather(hidden, gain, shift, bias, turns, sources, layer):
+def ring_scratch(rows):
+    return [
+        pltpu.VMEM((2, rows, HEAD_COLS), jnp.bfloat16),
+        pltpu.VMEM((2, rows, HEAD_COLS), jnp.bfloat16),
+        pltpu.VMEM((2, rows, HEAD_COLS), jnp.bfloat16),
+        pltpu.VMEM((2, rows, FEED_COLS), jnp.float32),
+        pltpu.VMEM((2, rows, FEED_COLS), jnp.bfloat16),
+        pltpu.SemaphoreType.DMA((2, 5)),
+    ]
+
+
+def ring_shapes(rows):
+    return [
+        jax.ShapeDtypeStruct((GROUP, rows, width), dtype)
+        for width, dtype in (
+            (HEAD_COLS, jnp.bfloat16),
+            (HEAD_COLS, jnp.bfloat16),
+            (HEAD_COLS, jnp.bfloat16),
+            (FEED_COLS, jnp.float32),
+            (FEED_COLS, jnp.bfloat16),
+        )
+    ]
+
+
+def ring_product(rings, sems, results, land, columns, bias, cosine, sine):
+    query, key, value, inner, active = rings
+
+    def leave(at, slot):
+        return [
+            pltpu.make_async_copy(ring.at[at], result.at[slot], sems.at[at, which])
+            for which, (ring, result) in enumerate(zip(rings, results))
+        ]
+
+    def product(number, slot):
+        whole = dot(land[slot], columns[...].reshape(D, COLS)) + bias[...]
+        one, two = HEAD_COLS, 2 * HEAD_COLS
+        at = lax.rem(number, 2)
+
+        @pl.when(number >= 2)
+        def _():
+            wait_all(leave(at, 0))
+
+        query[at] = spin(whole[:, :one], cosine[slot], sine[slot], 1.0).astype(jnp.bfloat16)
+        key[at] = spin(whole[:, one:two], cosine[slot], sine[slot], 1.0).astype(jnp.bfloat16)
+        value[at] = whole[:, two:JOINT_COLS].astype(jnp.bfloat16)
+        units = whole[:, JOINT_COLS:]
+        inner[at] = units
+        active[at] = jax.nn.gelu(units, approximate=True).astype(jnp.bfloat16)
+        for copy in leave(at, slot):
+            copy.start()
+
+    def finish():
+        for at in range(2):
+            wait_all(leave(at, 0))
+
+    return product, finish
+
+
+def norm_block(hidden, gain, shift, land, me):
+    def strip(part, carry):
+        values = hidden[part].astype(jnp.float32)
+        centred = values - jnp.mean(values, axis=1, keepdims=True)
+        spread = jnp.mean(centred * centred, axis=1, keepdims=True)
+        normed = centred * lax.rsqrt(spread + EPS) * gain[...] + shift[...]
+        land[me, part] = normed.astype(jnp.bfloat16)
+        return carry
+
+    each_strip(hidden.shape[0], strip, 0)
+
+
+def forward_gather(hidden, gain, shift, bias, tables, halves, layer):
     rows = hidden.shape[0]
     half = SHARE // 2
-    first = layer == 0
-
-    def kernel(hidden, gain, shift, bias, turn_a, turn_b, source_a, source_b, *refs):
+
+    def kernel(hidden, gain, shift, bias, turn_a, turn_b, own_half, other_half, *refs):
         every, columns_out, results, refs = refs[0], refs[1], refs[2:7], refs[7:]
-        rings, ring_sem, refs = refs[-6:-1], refs[-1], refs[:-6]
-        cosine, sine, refs = refs[0], refs[1], refs[2:]
+        cosine, sine, columns, load_sem, saved = refs[:5]
+        rings, ring_sem, refs = refs[5:10], refs[10], refs[11:]
+        land, sems = refs[0], refs[1:]
+        ctx, place, seq = lax.axis_index("ctx"), lax.axis_index("fsdp"), lax.axis_index("seq")
+        part_rows = pl.ds(pl.multiple_of(seq * half, half), half)
+        other_rows = pl.ds(pl.multiple_of((1 - seq) * half, half), half)
+        loads = load_all(
+            (
+                (own_half, columns.at[:, part_rows]),
+                (other_half, columns.at[:, other_rows]),
+                (turn_a, cosine),
+                (turn_b, sine),
+            ),
+            load_sem,
+        )
+        greet_neighbours()
+        norm_block(hidden, gain, shift, land, ctx * SIDE + place)
+        save = pltpu.make_async_copy(columns, columns_out, saved)
+        product, finish = ring_product(rings, ring_sem, results, land, columns, bias, cosine, sine)
+
+        def work(number, slot):
+            @pl.when(number == 0)
+            def _():
+                wait_all(loads)
+                save.start()
+
+            product(number, slot)
+
+        gather_blocks(land, every, *sems, work)
+        save.wait()
+        finish()
+
+    return pl.pallas_call(
+        kernel,
+        out_shape=[
+            jax.ShapeDtypeStruct((GROUP, rows, D), jnp.bfloat16),
+            jax.ShapeDtypeStruct((GROUP, SHARE, COLS), jnp.bfloat16),
+        ]
+        + ring_shapes(rows),
+        in_specs=[VMEM] * 4 + [HBM] * 4,
+        out_specs=[HBM] * 7,
+        scratch_shapes=[pltpu.VMEM((GROUP, rows, HEAD_COLS), jnp.float32)] * 2
+        + [
+            pltpu.VMEM((GROUP, SHARE, COLS), jnp.bfloat16),
+            pltpu.SemaphoreType.DMA((4,)),
+            pltpu.SemaphoreType.DMA,
+        ]
+        + ring_scratch(rows)
+        + gather_scratch(rows),
+        compiler_params=pltpu.CompilerParams(
+            collective_id=30 + layer, has_side_effects=True, vmem_limit_bytes=ROOM
+        ),
+    )(hidden, gain, shift, bias, *tables, *halves)
+
+
+GAIN_ROW, SHIFT_ROW, JOINT_BIAS_ROW, OUT_BIAS_ROW, DOWN_BIAS_ROW, LAYER_ROWS = 0, 1, 2, 5, 6, 7
+BEGIN_ROW = LAYERS * LAYER_ROWS
+
+
+def first_gather(hidden, packed, up_bias, frequency, qkv_weight, up_weight):
+    rows = hidden.shape[0]
+    half = SHARE // 2
+
+    def kernel(hidden, packed, up_bias, frequency, qkv_weight, up_weight, *refs):
+        every, columns_out, results, small, cosine, sine = refs[0], refs[1], refs[2:7], *refs[7:10]
+        refs = refs[10:]
         columns, plane_send, plane_recv, cross_send, cross_recv, own_sem, saved = refs[:7]
-        land = refs[7]
-        query, key, value, inner, active = rings
+        small_send, small_recv, gain, shift, bias = refs[7:12]
+        rings, ring_sem, refs = refs[12:17], refs[17], refs[18:]
+        land, sems = refs[0], refs[1:]
         ctx, place, seq = lax.axis_index("ctx"), lax.axis_index("fsdp"), lax.axis_index("seq")
         me = ctx * SIDE + place
         part_rows = pl.ds(pl.multiple_of(seq * half, half), half)
-        other_rows = pl.ds(pl.multiple_of((1 - seq) * half, half), half)
-        if first:
-            greet_plane(GROUP)
-        else:
-            greet_neighbours()
-        sources = (source_a, source_b)
+        sources = (qkv_weight, up_weight)
+        greet_plane(GROUP)
+
+        def small_copy(step):
+            return to_peer(
+                packed,
+                small.at[me],
+                small_send.at[step],
+                small_recv.at[me],
+                lax.rem(me + step, GROUP),
+            )
+
+        def small_begin(step, carry):
+            small_copy(step).start()
+            return carry
+
+        lax.fori_loop(1, GROUP, small_begin, 0)
+        small[me] = packed[...]
 
         def piece(step, number):
             peer = lax.rem(me + step, GROUP)
             which, start, at, width = column_places(peer)[number]
             return (
                 peer,
-                sources[which].at[layer, part_rows, pl.ds(start, width)],
+                sources[which].at[0, part_rows, pl.ds(start, width)],
                 columns.at[me, part_rows, pl.ds(at, width)],
             )
 
@@ -796,163 +973,138 @@
                 block, block, cross_send.at[source], cross_recv.at[source], "seq", 1 - seq
             )
 
-        if first:
-            for number in range(PLACES):
-                own_piece(number).start()
-        else:
-            halves = load_all(
-                (
-                    (source_a, columns.at[:, part_rows]),
-                    (source_b, columns.at[:, other_rows]),
-                    (turn_a, cosine),
-                    (turn_b, sine),
-                ),
-                own_sem,
+        for number in range(PLACES):
+            own_piece(number).start()
+
+        def send_columns(group, slot, made):
+            def send(more, carry):
+                step = SIDE * group + more
+
+                @pl.when(step > 0)
+                def _():
+                    for number in range(PLACES):
+                        send_piece(step, number).start()
+
+                return carry
+
+            lax.fori_loop(0, SIDE, send, 0)
+
+        def norm_own(group, slot, made):
+            def arrive(step, carry):
+                source = lax.rem(me + GROUP - step, GROUP)
+                to_peer(
+                    packed, small.at[source], small_send.at[step], small_recv.at[source], source
+                ).wait_recv()
+                return carry
+
+            lax.fori_loop(1, GROUP, arrive, 0)
+
+            def whole_row(row):
+                return jnp.concatenate(
+                    [small[block, row : row + 1] for block in range(GROUP)], axis=1
+                )
+
+            gain[...] = whole_row(GAIN_ROW)
+            shift[...] = whole_row(SHIFT_ROW)
+            for part in range(3):
+                at = part * GROUP + me
+                bias[:, part * HEAD_COLS : (part + 1) * HEAD_COLS] = small[
+                    at // 3, pl.ds(JOINT_BIAS_ROW + lax.rem(at, 3), 1)
+                ]
+            bias[:, JOINT_COLS:] = up_bias[...]
+            norm_block(hidden, gain, shift, land, me)
+
+        def pass_columns(group, slot, made):
+            def pass_on(more, carry):
+                step = SIDE * group + more
+                source = lax.rem(me + GROUP - step, GROUP)
+
+                @pl.when(step == 0)
+                def _():
+                    for number in range(PLACES):
+                        own_piece(number).wait()
+
+                @pl.when(step > 0)
+                def _():
+                    for number in range(PLACES):
+                        _, _, at, width = column_places(0)[number]
+                        target = columns.at[source, part_rows, pl.ds(at, width)]
+                        to_peer(
+                            target,
+                            target,
+                            plane_send.at[0, number],
+                            plane_recv.at[source, number],
+                            source,
+                        ).wait_recv()
+
+                cross(source).start()
+                return carry
+
+            lax.fori_loop(0, SIDE, pass_on, 0)
+
+        save = pltpu.make_async_copy(columns, columns_out, saved)
+
+        def wait_columns(group, slot, made):
+            def arrive(source, carry):
+                cross(source).wait_recv()
+                return carry
+
+            lax.fori_loop(0, GROUP, arrive, 0)
+            save.start()
+
+        product, finish = ring_product(rings, ring_sem, results, land, columns, bias, cosine, sine)
+
+        def next_product(group, slot, made):
+            product(made, slot)
+
+        def work(number, slot):
+            begin = jnp.concatenate(
+                [small[slot, BEGIN_ROW + part : BEGIN_ROW + part + 1] for part in range(rows // SHARE)],
+                axis=1,
             )
-
-        def send_columns(step, carry):
-            for number in range(PLACES):
-                send_piece(step, number).start()
-            return carry
-
-        def strip(part, carry):
-            values = hidden[part].astype(jnp.float32)
-            centred = values - jnp.mean(values, axis=1, keepdims=True)
-            spread = jnp.mean(centred * centred, axis=1, keepdims=True)
-            normed = centred * lax.rsqrt(spread + EPS) * gain[...] + shift[...]
-            land[me, part] = normed.astype(jnp.bfloat16)
-            return carry
-
-        each_strip(rows, strip, 0)
-
-        def pass_on(step):
-            source = lax.rem(me + GROUP - step, GROUP)
-
-            @pl.when(step == 0)
-            def _():
-                for number in range(PLACES):
-                    own_piece(number).wait()
+            begin = jnp.broadcast_to(begin, (8, rows)).T[:, :1]
+            first = (slot // SIDE) * rows
+            token = lax.broadcasted_iota(jnp.int32, (rows, 1), 0) + first
+            angle = (token.astype(jnp.float32) - begin) * frequency[...]
+            cosine[slot] = jnp.cos(angle)
+            sine[slot] = jnp.sin(angle)
+
+        gather_blocks(
+            land,
+            every,
+            *sems,
+            work,
+            (FIRST_KIND, FIRST_STEP, FIRST_WHAT),
+            (send_columns, norm_own, pass_columns, wait_columns, next_product),
+        )
+        save.wait()
+        finish()
+
+        def end(step, carry):
+            cross(step).wait_send()
 
             @pl.when(step > 0)
             def _():
-                for number in range(PLACES):
-                    _, _, at, width = column_places(0)[number]
-                    target = columns.at[source, part_rows, pl.ds(at, width)]
-                    to_peer(
-                        target, target, plane_send.at[0, number], plane_recv.at[source, number], source
-                    ).wait_recv()
-
-            cross(source).start()
-
-        def leave(number):
-            at = lax.rem(number, 2)
-            return [
-                pltpu.make_async_copy(
-                    ring.at[at], result.at[work_slot(number)], ring_sem.at[at, which]
-                )
-                for which, (ring, result) in enumerate(zip(rings, results))
-            ]
-
-        def product(number, slot):
-            whole = dot(land[slot], columns[...].reshape(D, COLS)) + bias[...]
-            one, two = HEAD_COLS, 2 * HEAD_COLS
-            at = lax.rem(number, 2)
-
-            @pl.when(number >= 2)
-            def _():
-                wait_all(leave(number - 2))
-
-            query[at] = spin(whole[:, :one], cosine[slot], sine[slot], 1.0).astype(jnp.bfloat16)
-            key[at] = spin(whole[:, one:two], cosine[slot], sine[slot], 1.0).astype(jnp.bfloat16)
-            value[at] = whole[:, two:JOINT_COLS].astype(jnp.bfloat16)
-            units = whole[:, JOINT_COLS:]
-            inner[at] = units
-            active[at] = jax.nn.gelu(units, approximate=True).astype(jnp.bfloat16)
-            for copy in leave(number):
-                copy.start()
-
-        save = pltpu.make_async_copy(columns, columns_out, saved)
-
-        def work_as_columns_come(number, slot):
-            @pl.when(number == 0)
-            def _():
-                lax.fori_loop(1, GROUP, send_columns, 0)
-
-            angle = turn_a[slot] * turn_b[...]
-            cosine[slot] = jnp.cos(angle)
-            sine[slot] = jnp.sin(angle)
-
-            @pl.when(number < GROUP // 2)
-            def _():
-                pass_on(2 * number)
-                pass_on(2 * number + 1)
-
-            @pl.when(number == GROUP // 2)
-            def _():
-                def arrive(source, carry):
-                    block = columns.at[source, part_rows]
-                    to_axis(
-                        block, block, cross_send.at[source], cross_recv.at[source], "seq", 1 - seq
-                    ).wait_recv()
-                    return carry
-
-                lax.fori_loop(0, GROUP, arrive, 0)
-                save.start()
-
-            @pl.when(number >= GROUP // 2)
-            def _():
-                def two_products(more, carry):
-                    which = 2 * number - GROUP + more
-                    product(which, work_slot(which))
-                    return carry
-
-                lax.fori_loop(0, 2, two_products, 0)
-
-        def work(number, slot):
-            @pl.when(number == 0)
-            def _():
-                wait_all(halves)
-                save.start()
-
-            product(number, slot)
-
-        gather_blocks(land, every, *refs[8:], work_as_columns_come if first else work)
-        save.wait()
-        for number in (GROUP - 2, GROUP - 1):
-            wait_all(leave(jnp.int32(number)))
-
-        def end(step, carry):
-            cross(step).wait_send()
-
-            @pl.when(step > 0)
-            def _():
+                small_copy(step).wait_send()
                 for number in range(PLACES):
                     send_piece(step, number).wait_send()
 
             return carry
 
-        if first:
-            lax.fori_loop(0, GROUP, end, 0)
-
-    def out(width, dtype):
-        return jax.ShapeDtypeStruct((GROUP, rows, width), dtype)
-
-    out_shape = [
-        out(D, jnp.bfloat16),
-        jax.ShapeDtypeStruct((GROUP, SHARE, COLS), jnp.bfloat16),
-        out(HEAD_COLS, jnp.bfloat16),
-        out(HEAD_COLS, jnp.bfloat16),
-        out(HEAD_COLS, jnp.bfloat16),
-        out(FEED_COLS, jnp.float32),
-        out(FEED_COLS, jnp.bfloat16),
-    ] + [out(HEAD_COLS, jnp.float32)] * (2 if first else 0)
+        lax.fori_loop(0, GROUP, end, 0)
+
     return pl.pallas_call(
         kernel,
-        out_shape=out_shape,
-        in_specs=[VMEM] * 4 + [VMEM if first else HBM] * 2 + [HBM] * 2,
-        out_specs=[HBM] * 7 + [VMEM] * (len(out_shape) - 7),
-        scratch_shapes=([] if first else [pltpu.VMEM((GROUP, rows, HEAD_COLS), jnp.float32)] * 2)
-        + [
+        out_shape=[
+            jax.ShapeDtypeStruct((GROUP, rows, D), jnp.bfloat16),
+            jax.ShapeDtypeStruct((GROUP, SHARE, COLS), jnp.bfloat16),
+        ]
+        + ring_shapes(rows)
+        + [jax.ShapeDtypeStruct((GROUP,) + packed.shape, packed.dtype)]
+        + [jax.ShapeDtypeStruct((GROUP, rows, HEAD_COLS), jnp.float32)] * 2,
+        in_specs=[VMEM] * 4 + [HBM] * 2,
+        out_specs=[HBM] * 7 + [VMEM] * 3,
+        scratch_shapes=[
             pltpu.VMEM((GROUP, SHARE, COLS), jnp.bfloat16),
             pltpu.SemaphoreType.DMA((GROUP, PLACES)),
             pltpu.SemaphoreType.DMA((GROUP, PLACES)),
@@ -960,20 +1112,18 @@
             pltpu.SemaphoreType.DMA((GROUP,)),
             pltpu.SemaphoreType.DMA((PLACES,)),
             pltpu.SemaphoreType.DMA,
+            pltpu.SemaphoreType.DMA((GROUP,)),
+            pltpu.SemaphoreType.DMA((GROUP,)),
+            pltpu.VMEM((1, D), jnp.float32),
+            pltpu.VMEM((1, D), jnp.float32),
+            pltpu.VMEM((1, COLS), jnp.float32),
         ]
-        + gather_scratch(rows)
-        + [
-            pltpu.VMEM((2, rows, HEAD_COLS), jnp.bfloat16),
-            pltpu.VMEM((2, rows, HEAD_COLS), jnp.bfloat16),
-            pltpu.VMEM((2, rows, HEAD_COLS), jnp.bfloat16),
-            pltpu.VMEM((2, rows, FEED_COLS), jnp.float32),
-            pltpu.VMEM((2, rows, FEED_COLS), jnp.bfloat16),
-            pltpu.SemaphoreType.DMA((2, 5)),
-        ],
+        + ring_scratch(rows)
+        + gather_scratch(rows),
         compiler_params=pltpu.CompilerParams(
-            collective_id=30 + layer, has_side_effects=True, vmem_limit_bytes=ROOM
+            collective_id=30, has_side_effects=True, vmem_limit_bytes=ROOM
         ),
-    )(hidden, gain, shift, bias, *turns, *sources)
+    )(hidden, packed, up_bias, frequency, qkv_weight, up_weight)
 
 
 def backward_gather(grad, out_weight, down_weight, inner, mixed, active):
@@ -1088,14 +1238,6 @@
 SPLIT = ((0, 208), (208, 48))
 
 
-def nibble(entries, index):
-    word = jnp.int32(0)
-    for start in range(0, len(entries), 7):
-        packed = sum(entry << (4 * place) for place, entry in enumerate(entries[start : start + 7]))
-        word = jnp.where(index >= start, jnp.int32(packed), word)
-    return lax.rem(lax.shift_right_logical(word, 4 * lax.rem(index, 7)), 16)
-
-
 def scatter_events(partial, other_work, late_work, ops, scratch):
     total, give, take, side_take, line_take, other_take = scratch[:6]
     core_send, core_recv, side_send, side_recv, line_send, line_recv = scratch[6:12]
@@ -1350,9 +1492,12 @@
 
 
 SMALL_ROWS = 16
-
-
-def backward_scatter(hidden, grad, gain, grad_joint, grad_inner, columns, every, layer, up=None):
+PAIRS = GROUP // 2
+
+
+def backward_scatter(
+    hidden, grad, gain, grad_joint, grad_inner, columns, every, layer, up=None, halves=()
+):
     rows = hidden.shape[0]
     half = SHARE // 2
     collects = up is not None
@@ -1360,11 +1505,11 @@
     tokens = GROUP * rows
 
     def kernel(*refs):
-        inputs, refs = refs[: 8 if collects else 7], refs[8 if collects else 7 :]
+        inputs, refs = refs[: 10 if collects else 7], refs[10 if collects else 7 :]
         gain, every = inputs[2], inputs[6]
         out, small_out, refs = refs[0], refs[1], refs[2:]
         if collects:
-            outputs, refs = refs[:2], refs[2:]
+            outputs, others, refs = refs[:2], refs[2:4], refs[4:]
         else:
             mine, refs = refs[0], refs[1:]
         hidden, grad, grad_joint, grad_inner, columns, load_sem, strips, load = refs[:8]
@@ -1375,8 +1520,8 @@
             mine, other, summed, arrived, arrived_up = refs[:5]
             cross_send, cross_recv, plane_send, plane_recv = refs[5:9]
             back_send, back_recv, keep = refs[9:12]
-            up_send, up_recv, up_own = refs[12:15]
-            refs = refs[15:]
+            up_send, up_recv, up_own, half_send, half_recv = refs[12:17]
+            refs = refs[17:]
         scratch = refs
         total = scratch[0]
         ctx, place, seq = lax.axis_index("ctx"), lax.axis_index("fsdp"), lax.axis_index("seq")
@@ -1384,14 +1529,14 @@
         part_rows = pl.ds(pl.multiple_of(seq * half, half), half)
         other_rows = pl.ds(pl.multiple_of((1 - seq) * half, half), half)
 
-        def block_of(turn):
-            return lax.rem(me + 1 + turn, GROUP)
+        def pair_of(turn):
+            return lax.rem(me // 2 + 1 + turn, PAIRS)
 
         def load_strip(turn):
-            start = pl.multiple_of(block_of(turn) * SHARE, SHARE)
+            start = pl.multiple_of(pair_of(turn) * 2 * SHARE, 2 * SHARE)
             buffer = lax.rem(turn, 2)
             return pltpu.make_async_copy(
-                every.at[:, :, pl.ds(start, SHARE)], strips.at[buffer], load.at[buffer]
+                every.at[:, :, pl.ds(start, 2 * SHARE)], strips.at[buffer], load.at[buffer]
             )
 
         loads = load_all(
@@ -1413,21 +1558,23 @@
             )
 
         def product(turn):
-            block = block_of(turn)
+            pair = pair_of(turn)
             load_strip(turn).wait()
 
-            @pl.when(turn + 1 < GROUP)
+            @pl.when(turn + 1 < PAIRS)
             def _():
                 load_strip(turn + 1).start()
 
-            strip = strips[lax.rem(turn, 2)].reshape(tokens, SHARE)
-            mine[block, :, :JOINT_COLS] = dot(
-                strip, grad_joint[...].reshape(tokens, JOINT_COLS), 0, 0
-            ).astype(jnp.bfloat16)
+            strip = strips[lax.rem(turn, 2)].reshape(tokens, 2 * SHARE)
+            made = dot(strip, grad_joint[...].reshape(tokens, JOINT_COLS), 0, 0).astype(jnp.bfloat16)
+            for which in range(2):
+                mine[2 * pair + which, :, :JOINT_COLS] = made[which * SHARE : (which + 1) * SHARE]
             if not collects:
-                mine[block, :, JOINT_COLS:] = dot(
-                    strip, grad_inner[...].reshape(tokens, FEED_COLS), 0, 0
-                ).astype(jnp.bfloat16)
+                made = dot(strip, grad_inner[...].reshape(tokens, FEED_COLS), 0, 0).astype(
+                    jnp.bfloat16
+                )
+                for which in range(2):
+                    mine[2 * pair + which, :, JOINT_COLS:] = made[which * SHARE : (which + 1) * SHARE]
 
         def cross_copy(block):
             return to_axis(
@@ -1448,6 +1595,20 @@
             peer = lax.rem(me + step, GROUP)
             return to_peer(inputs[7].at[peer], arrived_up.at[me], up_send.at[step], up_recv.at[me], peer)
 
+        def half_copies(pieces):
+            return [
+                to_axis(
+                    own.at[pl.ds(piece * (half // 4), half // 4)],
+                    there.at[pl.ds(piece * (half // 4), half // 4)],
+                    half_send.at[at, piece],
+                    half_recv.at[at, piece],
+                    "seq",
+                    1 - seq,
+                )
+                for at, (own, there) in enumerate(zip(inputs[8:10], others))
+                for piece in pieces
+            ]
+
         def final_pieces(source):
             pieces = []
             for number, (which, start, at, width) in enumerate(column_places(source)):
@@ -1475,24 +1636,35 @@
                     keep_copy(number, piece, target, source).start()
 
         def add(turn):
-            block = block_of(turn)
-            cross_copy(block).wait_recv()
-            summed[block] = (
-                mine[block, part_rows].astype(jnp.float32) + other[block].astype(jnp.float32)
-            ).astype(jnp.bfloat16)
-
-            @pl.when(turn < GROUP - 1)
+            for which in range(2):
+                block = 2 * pair_of(turn) + which
+                cross_copy(block).wait_recv()
+                summed[block] = (
+                    mine[block, part_rows].astype(jnp.float32) + other[block].astype(jnp.float32)
+                ).astype(jnp.bfloat16)
+
+                @pl.when(block != me)
+                def _(block=block):
+                    plane_copy(block).start()
+
+        def other_work(turn):
+            @pl.when(lax.rem(turn, 2) == 0)
             def _():
-                plane_copy(block).start()
-
-        def other_work(turn):
-            product(turn)
+                product(turn // 2)
+                if collects:
+                    for which in range(2):
+                        cross_copy(2 * pair_of(turn // 2) + which).start()
+
             if collects:
-                cross_copy(block_of(turn)).start()
-
-                @pl.when(turn >= SIDE)
+
+                @pl.when((lax.rem(turn, 2) == 1) & (turn > 4))
                 def _():
-                    add(turn - SIDE)
+                    add((turn - 5) // 2)
+
+                @pl.when(turn == GROUP - 1)
+                def _():
+                    for copy in half_copies((2, 3)):
+                        copy.start()
 
         def late_work(step):
             def pass_up(more, carry):
@@ -1526,6 +1698,8 @@
             own_up = pltpu.make_async_copy(inputs[7].at[me], arrived_up.at[me], up_own)
             own_up.start()
             lax.fori_loop(1, GROUP, send_up, 0)
+            for copy in half_copies((0, 1)):
+                copy.start()
         scatter_events(
             partial,
             other_work,
@@ -1534,7 +1708,7 @@
             scratch,
         )
         if collects:
-            lax.fori_loop(GROUP - SIDE, GROUP, last_adds, 0)
+            lax.fori_loop(PAIRS - 2, PAIRS, last_adds, 0)
             arrived[me] = summed[me]
         wait_all(loads[3:])
 
@@ -1644,6 +1818,7 @@
 
         if collects:
             lax.fori_loop(0, GROUP, end, 0)
+            wait_all(half_copies((0, 1, 2, 3)))
 
     def part(width, height=half):
         return pltpu.VMEM((GROUP, height, width), jnp.bfloat16)
@@ -1660,19 +1835,21 @@
             (
                 jax.ShapeDtypeStruct((SHARE, 3 * D), jnp.bfloat16),
                 jax.ShapeDtypeStruct((SHARE, FF), jnp.bfloat16),
+                jax.ShapeDtypeStruct((half, 3 * D), jnp.bfloat16),
+                jax.ShapeDtypeStruct((half, FF), jnp.bfloat16),
             )
             if collects
             else (jax.ShapeDtypeStruct((GROUP, SHARE, COLS), jnp.bfloat16),)
         ),
-        in_specs=[HBM, HBM, VMEM] + [HBM] * (5 if collects else 4),
-        out_specs=(VMEM, VMEM) + ((HBM, HBM) if collects else (VMEM,)),
+        in_specs=[HBM, HBM, VMEM] + [HBM] * (7 if collects else 4),
+        out_specs=(VMEM, VMEM) + ((HBM,) * 4 if collects else (VMEM,)),
         scratch_shapes=[
             pltpu.VMEM(array.shape, array.dtype)
             for array in (hidden, grad, grad_joint, grad_inner, columns)
         ]
         + [
             pltpu.SemaphoreType.DMA((5,)),
-            pltpu.VMEM((2, GROUP, rows, SHARE), jnp.bfloat16),
+            pltpu.VMEM((2, GROUP, rows, 2 * SHARE), jnp.bfloat16),
             pltpu.SemaphoreType.DMA((2,)),
             pltpu.VMEM((GROUP,) + small, jnp.float32),
             pltpu.VMEM((GROUP,) + small, jnp.float32),
@@ -1691,6 +1868,7 @@
             + [places] * 3
             + [sixteen] * 2
             + [pltpu.SemaphoreType.DMA]
+            + [pltpu.SemaphoreType.DMA((2, 4))] * 2
             if collects
             else []
         )
@@ -1698,45 +1876,7 @@
         compiler_params=pltpu.CompilerParams(
             collective_id=20 + layer, has_side_effects=True, vmem_limit_bytes=ROOM
         ),
-    )(hidden, grad, gain, grad_joint, grad_inner, columns, every, *((up,) if collects else ()))
-
-
-def gather_small(packed):
-    def kernel(packed, out, send, recv):
-        ctx, place = lax.axis_index("ctx"), lax.axis_index("fsdp")
-        me = ctx * SIDE + place
-        greet_plane(GROUP, False)
-        out[me] = packed[...]
-
-        def copy(step):
-            return to_peer(
-                packed, out.at[me], send.at[step], recv.at[me], lax.rem(me + step, GROUP)
-            )
-
-        def begin(step, carry):
-            copy(step).start()
-            return carry
-
-        lax.fori_loop(1, GROUP, begin, 0)
-
-        def end(step, carry):
-            source = lax.rem(me + GROUP - step, GROUP)
-            to_peer(packed, out.at[source], send.at[step], recv.at[source], source).wait_recv()
-            copy(step).wait_send()
-            return carry
-
-        lax.fori_loop(1, GROUP, end, 0)
-
-    return pl.pallas_call(
-        kernel,
-        out_shape=jax.ShapeDtypeStruct((GROUP,) + packed.shape, packed.dtype),
-        in_specs=[VMEM],
-        out_specs=VMEM,
-        scratch_shapes=[pltpu.SemaphoreType.DMA((GROUP,))] * 2,
-        compiler_params=pltpu.CompilerParams(
-            collective_id=6, has_side_effects=True, vmem_limit_bytes=ROOM
-        ),
-    )(packed)
+    )(hidden, grad, gain, grad_joint, grad_inner, columns, every, *((up, *halves) if collects else ()))
 
 
 def mask_rest(rows, begin, spot, first, lead):
@@ -1818,11 +1958,14 @@
     part_rows = pl.ds(pl.multiple_of(seq * half, half), half)
     other_rows = pl.ds(pl.multiple_of((1 - seq) * half, half), half)
 
+    def pair_of(turn):
+        return lax.rem(me // 2 + 1 + turn, PAIRS)
+
     def load_strip(turn):
-        start = pl.multiple_of(lax.rem(me + 1 + turn, GROUP) * SHARE, SHARE)
+        start = pl.multiple_of(pair_of(turn) * 2 * SHARE, 2 * SHARE)
         buffer = lax.rem(turn, 2)
         return pltpu.make_async_copy(
-            every.at[:, :, pl.ds(start, SHARE)], strips.at[buffer], load.at[buffer]
+            every.at[:, :, pl.ds(start, 2 * SHARE)], strips.at[buffer], load.at[buffer]
         )
 
     def cross_copy(block):
@@ -1843,38 +1986,41 @@
         load_strip(jnp.int32(0)).start()
 
     def product(turn, carry):
-        block = lax.rem(me + 1 + turn, GROUP)
+        pair = pair_of(turn)
         load_strip(turn).wait()
 
         @pl.when(turn == 0)
         def _():
             feed_copy().wait()
 
-        @pl.when(turn + 1 < GROUP)
+        @pl.when(turn + 1 < PAIRS)
         def _():
             load_strip(turn + 1).start()
 
-        strip = strips[lax.rem(turn, 2)].reshape(tokens, SHARE)
-        mine[block] = dot(strip, feed_part[...].reshape(tokens, FEED_COLS), 0, 0).astype(
-            jnp.bfloat16
-        )
-        cross_copy(block).start()
+        strip = strips[lax.rem(turn, 2)].reshape(tokens, 2 * SHARE)
+        made = dot(strip, feed_part[...].reshape(tokens, FEED_COLS), 0, 0).astype(jnp.bfloat16)
+        for which in range(2):
+            mine[2 * pair + which] = made[which * SHARE : (which + 1) * SHARE]
+            cross_copy(2 * pair + which).start()
         return carry
 
     def add(turn, carry):
-        block = lax.rem(me + 1 + turn, GROUP)
-        cross_copy(block).wait()
-        out[block] = (
-            mine[block, part_rows].astype(jnp.float32) + other[block].astype(jnp.float32)
-        ).astype(jnp.bfloat16)
+        for which in range(2):
+            block = 2 * pair_of(turn) + which
+            cross_copy(block).wait()
+            out[block] = (
+                mine[block, part_rows].astype(jnp.float32) + other[block].astype(jnp.float32)
+            ).astype(jnp.bfloat16)
         return carry
 
+    each = PAIRS // SIDE
+
     def make(step):
-        lax.fori_loop(SIDE * step, SIDE * step + SIDE, product, 0)
-        lax.fori_loop(SIDE * jnp.maximum(step - 1, 0), SIDE * step, add, 0)
+        lax.fori_loop(each * step, each * step + each, product, 0)
+        lax.fori_loop(each * jnp.maximum(step - 1, 0), each * step, add, 0)
 
     def end():
-        lax.fori_loop(GROUP - SIDE, GROUP, add, 0)
+        lax.fori_loop(PAIRS - each, PAIRS, add, 0)
 
     return begin, make, end
 
@@ -2124,7 +2270,7 @@
             EXCHANGE_SEMS
             + [
                 pltpu.VMEM((GROUP, rows, FEED_COLS), jnp.bfloat16),
-                pltpu.VMEM((2, GROUP, rows, SHARE), jnp.bfloat16),
+                pltpu.VMEM((2, GROUP, rows, 2 * SHARE), jnp.bfloat16),
                 pltpu.VMEM((GROUP, SHARE, FEED_COLS), jnp.bfloat16),
                 pltpu.VMEM((GROUP, half, FEED_COLS), jnp.bfloat16),
                 pltpu.SemaphoreType.DMA,
@@ -2172,50 +2318,21 @@
 ):
     rows = tokens.shape[1]
     length = SIDE * rows
-    docs = doc_lengths.shape[1]
     me = lax.axis_index("ctx") * SIDE + lax.axis_index("fsdp")
 
-    high = (doc_lengths[0] // 32).astype(jnp.bfloat16)
-    low = (doc_lengths[0] % 32).astype(jnp.bfloat16)
+    index = lax.axis_index("ctx") * rows + jnp.arange(rows, dtype=jnp.int32)
+    ends = jnp.cumsum(doc_lengths[0])
+    begin = jnp.max(jnp.where(index[:, None] >= ends[None, :], ends[None, :], 0), axis=1)
     fields = [ln_gain, ln_bias, qkv_bias, out_bias, down_bias]
     packed = jnp.concatenate(
-        [field.reshape(-1) for field in fields]
-        + [keep_mask[0].astype(jnp.bfloat16), high, low]
-    )
-    tile = 16 * 128
-    packed = jnp.pad(packed, (0, -packed.shape[0] % tile)).reshape(-1, 128)
-    everyone = gather_small(packed).reshape(GROUP, -1)
-    at = 0
-    whole = []
-    for field in fields:
-        width = field.shape[1]
-        part = everyone[:, at : at + LAYERS * width].reshape(GROUP, LAYERS, width)
-        whole.append(part.transpose(1, 0, 2).reshape(LAYERS, 1, GROUP * width).astype(jnp.float32))
-        at += LAYERS * width
-    gain, shift, joint_bias, output_bias, lower_bias = whole
-    keep = everyone[:, at : at + rows].reshape(SIDE, SIDE, rows)
-    keep = keep.transpose(1, 0, 2).reshape(SIDE, length)
-    at += rows
-    lengths = (
-        everyone[:SIDE, at : at + docs].astype(jnp.int32) * 32
-        + everyone[:SIDE, at + docs : at + 2 * docs].astype(jnp.int32)
-    )
-    own_bias = lax.dynamic_slice_in_dim(
-        joint_bias.reshape(LAYERS, 3, GROUP, HEAD_COLS), me, 1, axis=2
-    ).reshape(LAYERS, JOINT_COLS)
-    column_bias = jnp.concatenate([own_bias, up_bias.astype(jnp.float32)], axis=1)
-
-    index = jnp.arange(length, dtype=jnp.int32)
-    ends = jnp.cumsum(lengths, axis=1)
-    passed = jnp.where(index[None, None, :] >= ends[:, :, None], ends[:, :, None], 0)
-    begin = jnp.max(passed, axis=1)[:, None, :]
-    spot = jnp.where(keep > 0, index[None, :], -1)[:, :, None]
-    position = (index[None, None, :] - begin).astype(jnp.float32)
-    position = position.reshape(SIDE, SIDE, rows).transpose(1, 0, 2).reshape(GROUP, rows, 1)
+        [field[layer].astype(jnp.float32) for layer in range(LAYERS) for field in fields]
+        + [begin.astype(jnp.float32), keep_mask[0].astype(jnp.float32)]
+    )
+    packed = jnp.pad(packed, (0, -packed.shape[0] % (8 * SHARE))).reshape(-1, SHARE)
     lane = np.arange(HEAD_COLS) % HEAD_DIM
     inverse = 1.0 / 10000.0 ** (np.arange(0, ROT, 2, dtype=np.float32) / np.float32(ROT))
     inverse = np.where(lane < ROT, inverse[lane % (ROT // 2)], 0.0).astype(np.float32)
-    inverse = jnp.asarray(inverse)[None, :]
+    up_bias = up_bias.astype(jnp.float32)
 
     seq = lax.axis_index("seq")
     half = SHARE // 2
@@ -2225,25 +2342,48 @@
         return lax.ppermute(values, "seq", swap)
 
     hidden = tokens[0]
-    saved, tables = [], None
-    sources = (qkv_weight, up_weight)
+    saved, gains, joint_grads, upper_grads, branch_grads, small_grads = [], [], [], [], [], []
     for layer in range(LAYERS):
-        out = forward_gather(
-            hidden,
-            gain[layer],
-            shift[layer],
-            column_bias[layer][None, :],
-            tables or (position, inverse),
-            sources,
-            layer,
-        )
-        every, columns, query, key, value, inner, active = out[:7]
-        tables = tables or tuple(out[7:])
+        if layer == 0:
+            *out, small, cosine, sine = first_gather(
+                hidden, packed, up_bias[:1], jnp.asarray(inverse)[None, :], qkv_weight, up_weight
+            )
+            tables = (cosine, sine)
+            length_rows = rows // SHARE
+
+            def by_sequence(row):
+                values = small[:, row : row + length_rows].reshape(SIDE, SIDE, rows)
+                return values.transpose(1, 0, 2).reshape(SIDE, length).astype(jnp.int32)
+
+            begin = by_sequence(BEGIN_ROW)[:, None, :]
+            keep = by_sequence(BEGIN_ROW + length_rows)
+            spot = jnp.where(keep > 0, jnp.arange(length, dtype=jnp.int32)[None, :], -1)[:, :, None]
+        else:
+            out = forward_gather(
+                hidden,
+                gain_row,
+                row_of(layer, SHIFT_ROW),
+                jnp.concatenate([own_bias, up_bias[layer : layer + 1]], axis=1),
+                tables,
+                halves,
+                layer,
+            )
+
+        def row_of(layer, row):
+            return small[:, layer * LAYER_ROWS + row].reshape(1, D)
+
+        every, columns, query, key, value, inner, active = out
+        gains.append(row_of(layer, GAIN_ROW))
         if layer + 1 < LAYERS:
             mixed, turned, stats, arrived = attend_plane(
                 query, key, value, begin, spot, (qkv_weight, up_weight), layer + 1
             )
-            sources = (arrived, swapped(arrived))
+            halves = (arrived, swapped(arrived))
+            gain_row = row_of(layer + 1, GAIN_ROW)
+            at = (layer + 1) * LAYER_ROWS + JOINT_BIAS_ROW
+            own_bias = lax.dynamic_slice_in_dim(
+                small[:, at : at + 3].reshape(3, GROUP, HEAD_COLS), me, 1, axis=1
+            ).reshape(1, JOINT_COLS)
         else:
             mixed, turned, stats = attend_plane(query, key, value, begin, spot)
         saved.append(
@@ -2251,7 +2391,7 @@
         )
         hidden = forward_scatter(
             hidden,
-            output_bias[layer] + lower_bias[layer],
+            row_of(layer, OUT_BIAS_ROW) + row_of(layer, DOWN_BIAS_ROW),
             mixed,
             active,
             out_weight[layer],
@@ -2261,7 +2401,6 @@
     result = hidden.astype(jnp.bfloat16)[None]
 
     grad_hidden = cotangent[0].astype(jnp.float32) * keep_mask[0].astype(jnp.float32)[:, None]
-    joint_grads, upper_grads, branch_grads, small_grads = [], [], [], []
     summed = None
     for layer in reversed(range(LAYERS)):
         before, every, columns, query, key, value, inner, active, mixed, turned, stats = saved[layer]
@@ -2290,24 +2429,17 @@
             every,
             grad_inner,
         )
-        for grads, own in zip((joint_grads, upper_grads), rest[:2]):
-            other = swapped(own)
-            grads.insert(
-                0,
-                jnp.concatenate(
-                    [jnp.where(seq == 0, own, other), jnp.where(seq == 0, other, own)], axis=0
-                ),
-            )
         grad_hidden, small, *grads = backward_scatter(
             before,
             grad_hidden,
-            gain[layer],
+            gains[layer],
             grad_joint,
             grad_inner,
             columns.reshape(D, COLS),
             every,
             layer,
             rest[2] if rest else None,
+            rest[:2],
         )
         small_grads.insert(0, small)
         if layer > 0:
@@ -2315,8 +2447,11 @@
             other = swapped(lax.dynamic_slice_in_dim(grads[0], (1 - seq) * half, half, axis=1))
             summed = (own.astype(jnp.float32) + other.astype(jnp.float32)).astype(jnp.bfloat16)
         else:
-            joint_grads.insert(0, grads[0])
-            upper_grads.insert(0, grads[1])
+            for total, whole, own, other in zip(
+                (joint_grads, upper_grads), grads[:2], rest[:2], grads[2:]
+            ):
+                first, second = jnp.where(seq == 0, own, other), jnp.where(seq == 0, other, own)
+                total.extend([whole, jnp.concatenate([first, second], axis=0)])
     branch_grad = jnp.stack(branch_grads)
     small = jnp.stack(small_grads)
     return (

time: 1160 us -> 1100 us (0.948)
  Pallas kernels: 1060 us -> 1020 us
  waiting for transfers between devices: 24.5 us -> 0.01 us
    pallas_call x2, Pallas kernels: 103 us -> 71.6 us  [attend_plane_back(): pl.pallas_call(kernel, grid=(SIDE,), out_shape=(jax.ShapeDtypeStruct((SID...]
    ppermute x6 -> x4, waiting for transfers between devices: 24.5 us -> 0.01 us  [swapped(): return lax.ppermute(values, 'seq', swap)]
    pallas_call x3 -> x2, Pallas kernels: 258 us -> 257 us  [the longest x1 160 us: first_gather(): pl.pallas_call(kernel, out_shape=[jax.ShapeDtypeStruct((GROUP, rows, D),...]
  transfers between devices with their start and end apart: 6 -> 4, of which waited for: 1 -> 0; matrix products, arithmetic and copies ran while one was open for 3% -> 3% of each run, Pallas kernels for 35% -> 43%
where the time goes in v3:
time: 1100 us; the launch traced here: 1090 us
  Pallas kernels  1020 us (93%)
  other arithmetic  45.8 us (4%)
  local copies, waits for them, and re-layouts  19.1 us (2%)
    pallas_call x2, Pallas kernels, backward_scatter(): pl.pallas_call(kernel, out_shape=(jax.ShapeDtypeStruct((rows, D), jnp.flo...  246 us
    pallas_call x2, Pallas kernels, backward_gather(): pl.pallas_call(kernel, out_shape=(jax.ShapeDtypeStruct((GROUP, rows, HEAD...  191 us
    pallas_call x2, Pallas kernels, forward_scatter(): pl.pallas_call(kernel, out_shape=jax.ShapeDtypeStruct((rows, D), jnp.floa...  189 us
    pallas_call x1, Pallas kernels, first_gather(): pl.pallas_call(kernel, out_shape=[jax.ShapeDtypeStruct((GROUP, rows, D),...  160 us
    pallas_call x1, Pallas kernels, forward_gather(): pl.pallas_call(kernel, out_shape=[jax.ShapeDtypeStruct((GROUP, rows, D),...  97.6 us
    pallas_call x2, Pallas kernels, attend_plane_back(): pl.pallas_call(kernel, grid=(SIDE,), out_shape=(jax.ShapeDtypeStruct((SID...  71.6 us
    pallas_call x2, Pallas kernels, attend_plane(): pl.pallas_call(kernel, grid=(SIDE,), out_shape=(shape(rows, HEAD_COLS, jn...  64.8 us
  transfers between devices with their start and end apart: 4, of which 0 were waited for; matrix products, arithmetic and copies ran while one was open for 3% of the time, Pallas kernels for 43%

profile of v3, /device:TPU:0, one launch (start us, length us, event | category | flops | bytes accessed | tf_op | source)
XLA Modules:
  0.0 1090.9 jit_solution(8862113265950778901)
XLA Ops:
  10.3 159.5 %shard_map.238 = (bf16[16,256,2048]{2,1,0:T(8,128)(2,1)}, bf16[16,128,896]{2,1,0:T(8,128)(2,1)}, bf16[16,256,128]{2,1,0:T(8,128)(2,1)}, bf16[16,256,128]{2,1,0:T...) custom-call(bf16[256,2048]{1,0:T(8,128)(2,1)} %bitcast.110, ...), custom_call_target="tpu_custom_call" | custom-call | tf_op jit(solution)/shard_map/pallas_call | solution.py:1096
  174.7 45.5 %shard_map.239 = (bf16[4,4,256,128]{3,2,1,0:T(8,128)(2,1)}, f32[4,4,128,256]{3,2,1,0:T(8,128)}, f32[4,4,1024]{2,1,0:T(4,128)}, bf16[16,64,896]{2,1,0:T(8,128)(2,1)}) custom-call(bf16[4,4,256,128]{3,2,1,0:T(8,128)(2,1)} %bitcast.113, bf16[4,4,256,128]{3,2,1,0:T(8,128)(2,1)} %bitcast.115, bf16[4,4,256,128]{3,2,1,0:T(8,128)(2,1)} %bitcast.117, ...), custom_call_target="tpu_custom_call" | custom-call | tf_op jit(solution)/shard_map/pallas_call | solution.py:2128
  224.4 4.8 slice_bitcast_fusion
  229.2 94.4 %shard_map.240.hidden.refs_0_ = f32[256,2048]{1,0:T(8,128)} custom-call(bf16[256,2048]{1,0:T(8,128)(2,1)} %bitcast.111, f32[1,2048]{1,0:T(1,128)} %get-tuple-element.114.bias, bf16[16,256,128]{2,1,0:T(8,128)(2,1)} %bitcast.119, bf16[16,256,512]{2,1,0:T(8,128)(2,1)} %get-tuple-element.60.active, bf16[128,2048]{1,0:T(8,128)(2,1)} %get-tuple-element.109.out_weight, ...), custom_call_target="tpu_custom_call" | custom-call | tf_op jit(solution)/shard_map/pallas_call | solution.py:1477
  324.3 1.9 fusion.1
  327.4 97.6 %shard_map.241 = (bf16[16,256,2048]{2,1,0:T(8,128)(2,1)}, bf16[16,128,896]{2,1,0:T(8,128)(2,1)}, bf16[16,256,128]{2,1,0:T(8,128)(2,1)}, bf16[16,256,128]{2,1,0:T...) custom-call(f32[256,2048]{1,0:T(8,128)} %shard_map.240.hidden.refs_0_, ...), custom_call_target="tpu_custom_call" | custom-call | tf_op jit(solution)/shard_map/pallas_call | solution.py:891
  425.0 19.3 %shard_map.242 = (bf16[4,4,256,128]{3,2,1,0:T(8,128)(2,1)}, f32[4,4,128,256]{3,2,1,0:T(8,128)}, f32[4,4,1024]{2,1,0:T(4,128)}) custom-call(bf16[4,4,256,128]{3,2,1,0:T(8,128)(2,1)} %bitcast.123, bf16[4,4,256,128]{3,2,1,0:T(8,128)(2,1)} %bitcast.125, bf16[4,4,256,128]{3,2,1,0:T(8,128)(2,1)} %bitcast.127, s32[4,1,1024]{2,1,0:T(1,128)} %convert_element_type.180.begin, ...), custom_call_target="tpu_custom_call" | custom-call | tf_op jit(solution)/shard_map/pallas_call | solution.py:2128
  444.4 97.2 %shard_map.244 = (f32[16,256,128]{2,1,0:T(8,128)}, bf16[16,256,512]{2,1,0:T(8,128)(2,1)}, bf16[640,2048]{1,0:T(8,128)(2,1)}) custom-call(bf16[256,2048]{1,0:T(8,128)(2,1)} %get-tuple-element.106.own, bf16[128,2048]{1,0:T(8,128)(2,1)} %get-tuple-element.108.out_weight, bf16[512,2048]{1,0:T(8,128)(2,1)} %get-tuple-element.100.down_weight, ...), custom_call_target="tpu_custom_call" | custom-call | tf_op jit(solution)/shard_map/pallas_call | solution.py:1197
  541.5 21.6 %shard_map.245 = bf16[4,4,256,384]{3,2,1,0:T(8,128)(2,1)} custom-call(bf16[4,4,256,128]{3,2,1,0:T(8,128)(2,1)} %bitcast.124, bf16[4,4,256,128]{3,2,1,0:T(8,128)(2,1)} %bitcast.126, bf16[4,4,256,128]{3,2,1,0:T(8,128)(2,1)} %bitcast.128, f32[4,4,256,128]{3,2,1,0:T(8,128)} %bitcast.133, f32[4,4,256,128]{3,2,1,0:T(8,128)} %bitcast.105, ...), custom_call_target="tpu_custom_call" | custom-call | tf_op jit(solution)/shard_map/pallas_call | solution.py:2249
  563.1 107.6 %shard_map.246 = (f32[256,2048]{1,0:T(8,128)}, f32[16,128]{1,0:T(8,128)}, bf16[16,128,896]{2,1,0:T(8,128)(2,1)}) custom-call(f32[256,2048]{1,0:T(8,128)} %shard_map.240.hidden.refs_0_, f32[256,2048]{1,0:T(8,128)} %get-tuple-element.107.refs_1_, f32[1,2048]{1,0:T(1,128)} %get-tuple-element.112.gain.refs_2_, bf16[16,256,384]{2,1,0:T(8,128)(2,1)} %bitcast.109, ...), custom_call_target="tpu_custom_call" | custom-call | tf_op jit(solution)/shard_map/pallas_call | solution.py:1828
  670.8 3.0 constant_dynamic-slice_fusion
  673.8 2.3 collective-permute-start.1
  677.2 94.2 %shard_map.247 = (f32[16,256,128]{2,1,0:T(8,128)}, bf16[16,256,512]{2,1,0:T(8,128)(2,1)}, bf16[640,2048]{1,0:T(8,128)(2,1)}) custom-call(bf16[256,2048]{1,0:T(8,128)(2,1)} %convert_element_type.186.own, bf16[128,2048]{1,0:T(8,128)(2,1)} %get-tuple-element.109.out_weight, bf16[512,2048]{1,0:T(8,128)(2,1)} %get-tuple-element.101.down_weight, ...), custom_call_target="tpu_custom_call" | custom-call | tf_op jit(solution)/shard_map/pallas_call | solution.py:1197
  771.5 2.0 collective-permute-start.3
  773.5 94.1 %shard_map.243 = f32[256,2048]{1,0:T(8,128)} custom-call(f32[256,2048]{1,0:T(8,128)} %shard_map.240.hidden.refs_0_, f32[1,2048]{1,0:T(1,128)} %get-tuple-element.113.bias, bf16[16,256,128]{2,1,0:T(8,128)(2,1)} %bitcast.122, bf16[16,256,512]{2,1,0:T(8,128)(2,1)} %get-tuple-element.68.active, bf16[128,2048]{1,0:T(8,128)(2,1)} %get-tuple-element.108.out_weight, ...), custom_call_target="tpu_custom_call" | custom-call | tf_op jit(solution)/shard_map/pallas_call | solution.py:1477
  867.7 2.7 convert_bitcast_fusion
  870.4 3.3 add_convert_fusion.refs_0_
  873.7 50.0 %shard_map.248 = (bf16[4,4,256,384]{3,2,1,0:T(8,128)(2,1)}, bf16[64,6144]{1,0:T(8,128)(2,1)}, bf16[64,8192]{1,0:T(8,128)(2,1)}, bf16[16,64,512]{2,1,0:T(8,128)(2,1)}) custom-call(bf16[4,4,256,128]{3,2,1,0:T(8,128)(2,1)} %bitcast.114, bf16[4,4,256,128]{3,2,1,0:T(8,128)(2,1)} %bitcast.116, bf16[4,4,256,128]{3,2,1,0:T(8,128)(2,1)} %bitcast.118, ...), custom_call_target="tpu_custom_call" | custom-call | tf_op jit(solution)/shard_map/pallas_call | solution.py:2249
  923.7 138.7 %shard_map.249 = (f32[256,2048]{1,0:T(8,128)}, f32[16,128]{1,0:T(8,128)}, bf16[128,6144]{1,0:T(8,128)(2,1)}, bf16[128,8192]{1,0:T(8,128)(2,1)}, bf16[64,6144]{1,0:T(8,128)(2,1)}, /*index=5*/bf16[64,8192]{1,0:T(8,128)(2,1)}) custom-call(bf16[256,2048]{1,0:T(8,128)(2,1)} %bitcast.112, f32[256,2048]{1,0:T(8,128)} %get-tuple-element.76.refs_1_, ...), custom_call_target="tpu_custom_call" | custom-call | tf_op jit(solution)/shard_map/pallas_call | solution.py:1828
  1069.6 3.1 maximum_convert_fusion.1
  1072.7 3.9 maximum_convert_fusion
  1076.7 2.7 add_bitcast_fusion.1
  1079.4 3.6 add_bitcast_fusion
  1083.0 4.0 pad_maximum_fusion
  (81 shorter events, 32.5 us)
Async XLA Ops:
  174.7 46.9 %copy-start.10 = (bf16[2,128,2048]{2,1,0:T(8,128)(2,1)S(1)}, bf16[2,128,2048]{2,1,0:T(8,128)(2,1)}, u32[]{:S(2)}) copy-start(bf16[2,128,2048]{2,1,0:T(8,128)(2,1)} %param.22) | copy-start | bytes 3145732
  220.1 106.1 %collective-permute-start = (bf16[16,64,896]{2,1,0:T(8,128)(2,1)}, bf16[16,64,896]{2,1,0:T(8,128)(2,1)S(1)}, u32[]{:S(2)}, u32[]{:S(2)}) collective-permute-start(bf16[16,64,896]{2,1,0:T(8,128)(2,1)} %get-tuple-element.63.own_half), channel_id=1, source_target_pairs={{0,16},{16,0},{1,17},{17,1},{2,18},{18,2},{3,19},{19,3},{4,20},{20... | collective-permute-start | bytes 5505032 | tf_op jit(solution)/shard_map/ppermute | solution.py:2342
  229.2 95.0 %copy-start.9 = (bf16[1,256,2048]{2,1,0:T(8,128)(2,1)S(1)}, bf16[1,256,2048]{2,1,0:T(8,128)(2,1)}, u32[]{:S(2)}) copy-start(bf16[1,256,2048]{2,1,0:T(8,128)(2,1)} %param.28) | copy-start | bytes 3145732
  326.2 1.2 copy-start.7
  670.8 5.3 copy-start
  673.8 196.6 %collective-permute-start.1 = (bf16[16,64,896]{2,1,0:T(8,128)(2,1)}, bf16[16,64,896]{2,1,0:T(8,128)(2,1)}, u32[]{:S(2)}, u32[]{:S(2)}) collective-permute-start(bf16[16,64,896]{2,1,0:T(8,128)(2,1)} %constant_dynamic-slice_fusion), channel_id=1, source_target_pairs={{0,16},{16,0},{1,17},{17,1},{2,18},{18,2},{3,19},{19,3},{4,20},{20... | collective-permute-start | bytes 5505032 | tf_op jit(solution)/shard_map/ppermute | solution.py:2342
  771.4 305.2 %collective-permute-start.2 = (bf16[640,2048]{1,0:T(8,128)(2,1)}, bf16[640,2048]{1,0:T(8,128)(2,1)}, u32[]{:S(2)}, u32[]{:S(2)}) collective-permute-start(bf16[640,2048]{1,0:T(8,128)(2,1)} %get-tuple-element.94), channel_id=1, source_target_pairs={{0,16},{16,0},{1,17},{17,1},{2,18},{18,2},{3,19},{19,3},{4,20},{20... | collective-permute-start | bytes 7864328 | tf_op jit(solution)/shard_map/ppermute | solution.py:2342
  771.5 307.9 %collective-permute-start.3 = (bf16[640,2048]{1,0:T(8,128)(2,1)}, bf16[640,2048]{1,0:T(8,128)(2,1)}, u32[]{:S(2)}, u32[]{:S(2)}) collective-permute-start(bf16[640,2048]{1,0:T(8,128)(2,1)} %get-tuple-element.95), channel_id=1, source_target_pairs={{0,16},{16,0},{1,17},{17,1},{2,18},{18,2},{3,19},{19,3},{4,20},{20... | collective-permute-start | bytes 7864328 | tf_op jit(solution)/shard_map/ppermute | solution.py:2342
  773.5 96.9 %copy-start.2 = (bf16[16,128,896]{2,1,0:T(8,128)(2,1)S(1)}, bf16[16,128,896]{2,1,0:T(8,128)(2,1)}, u32[]{:S(2)}) copy-start(bf16[16,128,896]{2,1,0:T(8,128)(2,1)} %get-tuple-element.81) | copy-start | bytes 11010052
  923.7 138.8 %copy-start.12 = (f32[16,128]{1,0:T(8,128)S(1)}, f32[16,128]{1,0:T(8,128)}, u32[]{:S(2)}) copy-start(f32[16,128]{1,0:T(8,128)} %get-tuple-element.91) | copy-start | bytes 24580
  923.7 142.8 %copy-start.1 = (bf16[64,8192]{1,0:T(8,128)(2,1)S(1)}, bf16[64,8192]{1,0:T(8,128)(2,1)}, u32[]{:S(2)}) copy-start(bf16[64,8192]{1,0:T(8,128)(2,1)} %get-tuple-element.88.refs_9_) | copy-start | bytes 3145732
  1062.4 5.4 copy-start.3
  1062.5 5.4 copy-start.11
  1065.3 23.1 %copy-start.13 = (f32[2,1,128]{2,1,0:T(1,128)}, f32[2,1,128]{2,1,0:T(1,128)S(1)}, u32[]{:S(2)}) copy-start(f32[2,1,128]{2,1,0:T(1,128)S(1)} %get-tuple-element.115) | copy-start | bytes 3076
  1068.2 1.4 copy-start.8
  1069.6 3.1 copy-start.6
  1072.7 3.9 copy-start.4
  1087.0 2.3 copy-start.5

commit v4 on v3

--- a/solution.py
+++ b/solution.py
@@ -504,7 +504,7 @@
     return ctx, place, twin, across, lax.rem(twin + 2, 4)
 
 
-def greet_neighbours():
+def greet_neighbours(cross=False):
     ctx, place, twin, across, _ = neighbours()
     barrier = pltpu.get_barrier_semaphore()
     pl.semaphore_signal(barrier, inc=1, device_id={"ctx": twin}, device_id_type=MESH)
@@ -518,7 +518,11 @@
     def _():
         pl.semaphore_signal(barrier, inc=1, device_id={"fsdp": place + 1}, device_id_type=MESH)
 
-    inner = jnp.int32(2) + jnp.where(place > 0, 1, 0) + jnp.where(place < SIDE - 1, 1, 0)
+    if cross:
+        pl.semaphore_signal(
+            barrier, inc=1, device_id={"seq": 1 - lax.axis_index("seq")}, device_id_type=MESH
+        )
+    inner = jnp.int32(3 if cross else 2) + jnp.where(place > 0, 1, 0) + jnp.where(place < SIDE - 1, 1, 0)
     pl.semaphore_wait(barrier, inner)
 
 
@@ -578,16 +582,16 @@
     (1, 0, 2, 0, 2, 0, 2, 3, 1, 1, 0, 3, 2, 3, 3, 1, 3, 3, 0, 0, 2, 3, 1, 3, 1, 1, 2, 2, 3, 0, 3, 2, 3, 3, 0, 3, 1, 3, 3, 3),
 )
 FIRST_KIND = (
-    (0, 0, 0, 0, 0, 0, 0, 1, 0, 0, 0, 1, 0, 1, 0, 0, 0, 1, 0, 1, 1, 2, 0, 1, 0, 0, 0, 0, 1, 3, 0, 2, 3, 0, 2, 0, 2, 0, 3, 1, 0, 0, 3, 1, 1, 2, 2, 0, 1, 1, 0, 1, 1, 0, 1, 0, 1, 3, 3, 2, 1, 1, 1, 2, 3, 3),
-    (0, 0, 0, 0, 0, 1, 0, 0, 0, 0, 1, 0, 0, 0, 0, 2, 1, 0, 1, 0, 1, 0, 0, 0, 0, 0, 0, 2, 1, 0, 0, 1, 0, 2, 1, 0, 3, 1, 3, 0, 1, 2, 0, 0, 0, 1, 1, 1, 2, 3, 1, 1, 1, 1, 3, 3, 1, 3, 1, 0, 2, 2, 3, 1, 2, 3),
+    (0, 0, 0, 0, 0, 0, 0, 0, 0, 1, 3, 2, 3, 2, 0, 1, 3, 1, 0, 1, 0, 0, 0, 1, 1, 0, 0, 3, 0, 0, 2, 2, 0, 1, 0, 0, 1, 1, 1, 0, 0, 1, 1, 2, 2, 3, 3, 0, 1, 0, 0, 0, 0, 1, 1, 3, 2, 1, 0, 1, 1, 2, 0, 2, 2, 0, 1, 3, 0, 1, 0, 0, 3, 3, 2, 1, 1, 1, 2, 1, 3, 3),
+    (0, 0, 0, 0, 0, 2, 0, 0, 0, 1, 0, 0, 2, 1, 3, 1, 1, 0, 2, 0, 3, 3, 0, 0, 0, 0, 0, 0, 1, 1, 0, 1, 0, 0, 2, 3, 1, 2, 0, 1, 0, 0, 0, 1, 0, 1, 0, 2, 0, 1, 1, 1, 3, 2, 2, 3, 0, 3, 1, 0, 0, 0, 1, 2, 0, 0, 1, 1, 1, 1, 1, 3, 2, 3, 1, 2, 1, 1, 3, 3, 2, 3),
 )
 FIRST_STEP = (
-    (0, 0, 0, 1, 2, 0, 3, 0, 0, 0, 1, 0, 1, 0, 1, 2, 1, 1, 0, 1, 1, 0, 1, 1, 2, 3, 2, 2, 0, 1, 2, 1, 0, 0, 0, 1, 2, 0, 1, 2, 3, 2, 0, 0, 1, 1, 2, 3, 2, 2, 3, 2, 2, 3, 3, 3, 3, 2, 2, 3, 3, 3, 3, 3, 3, 3),
-    (0, 1, 2, 0, 0, 0, 0, 0, 0, 2, 0, 3, 0, 2, 1, 0, 0, 1, 0, 1, 1, 1, 2, 1, 2, 2, 3, 1, 1, 0, 3, 1, 3, 0, 1, 1, 1, 2, 1, 3, 2, 1, 3, 3, 0, 2, 2, 3, 3, 0, 2, 3, 3, 3, 0, 2, 3, 3, 0, 2, 2, 3, 3, 1, 2, 2),
+    (0, 0, 1, 2, 3, 3, 0, 0, 0, 3, 0, 0, 2, 1, 0, 0, 1, 1, 0, 0, 0, 1, 1, 0, 0, 2, 2, 3, 1, 1, 2, 3, 3, 2, 1, 2, 0, 1, 1, 2, 1, 1, 1, 0, 1, 0, 1, 0, 1, 2, 1, 0, 2, 2, 0, 0, 1, 2, 3, 2, 2, 2, 2, 2, 0, 3, 2, 1, 3, 3, 3, 3, 2, 2, 3, 3, 3, 3, 3, 3, 3, 3),
+    (0, 1, 2, 0, 0, 0, 2, 1, 3, 0, 0, 0, 3, 3, 1, 2, 0, 3, 1, 0, 2, 0, 0, 1, 2, 0, 2, 1, 1, 0, 1, 0, 3, 2, 0, 3, 1, 2, 1, 0, 2, 0, 1, 0, 3, 1, 2, 0, 0, 1, 1, 2, 0, 1, 1, 1, 3, 1, 2, 3, 2, 1, 2, 2, 3, 3, 2, 3, 1, 2, 3, 0, 2, 2, 3, 3, 3, 3, 3, 3, 3, 2),
 )
 FIRST_WHAT = (
-    (4, 5, 2, 4, 4, 0, 4, 0, 1, 6, 1, 1, 6, 2, 0, 6, 2, 2, 3, 0, 1, 3, 3, 3, 2, 6, 0, 1, 3, 3, 3, 3, 3, 7, 8, 8, 3, 8, 8, 0, 0, 8, 8, 8, 8, 8, 8, 1, 2, 1, 2, 3, 8, 3, 2, 8, 0, 3, 8, 3, 1, 3, 8, 8, 3, 8),
-    (4, 4, 4, 5, 0, 0, 1, 2, 3, 1, 1, 4, 6, 2, 0, 3, 2, 2, 3, 6, 0, 1, 0, 3, 3, 6, 6, 3, 1, 7, 0, 2, 2, 8, 3, 8, 3, 0, 8, 1, 2, 8, 3, 8, 8, 1, 3, 2, 3, 3, 8, 1, 0, 3, 8, 3, 8, 3, 8, 8, 3, 8, 8, 8, 8, 8),
+    (5, 4, 4, 4, 9, 4, 0, 9, 2, 9, 9, 9, 9, 9, 1, 2, 9, 9, 6, 0, 3, 1, 6, 1, 3, 9, 6, 9, 0, 9, 9, 9, 6, 9, 2, 1, 9, 1, 2, 2, 3, 0, 3, 3, 3, 3, 3, 7, 8, 0, 8, 8, 3, 1, 8, 8, 8, 0, 0, 2, 3, 3, 8, 8, 8, 1, 8, 8, 2, 0, 3, 8, 3, 8, 3, 2, 1, 3, 8, 8, 3, 8),
+    (4, 4, 4, 5, 0, 9, 9, 9, 9, 0, 9, 1, 9, 9, 9, 9, 9, 4, 9, 6, 9, 9, 2, 6, 1, 3, 6, 0, 9, 2, 1, 1, 6, 2, 3, 9, 0, 9, 2, 3, 0, 7, 3, 8, 0, 2, 3, 8, 8, 1, 3, 2, 3, 3, 8, 3, 1, 8, 0, 2, 8, 8, 1, 3, 3, 8, 3, 2, 8, 8, 1, 8, 8, 3, 0, 3, 3, 8, 3, 8, 8, 8),
 )
 OPS = len(GATHER_KIND[0])
 WORKS = tuple(
@@ -763,6 +767,11 @@
 
 
 PLACES = 4
+
+
+def plane_swap(swap, sems):
+    source, target = swap
+    return to_axis(source, target, sems.at[0], sems.at[1], "seq", 1 - lax.axis_index("seq"))
 
 
 def load_all(pairs, sems):
@@ -1057,7 +1066,7 @@
         def next_product(group, slot, made):
             product(made, slot)
 
-        def work(number, slot):
+        def turn_block(group, slot, made):
             begin = jnp.concatenate(
                 [small[slot, BEGIN_ROW + part : BEGIN_ROW + part + 1] for part in range(rows // SHARE)],
                 axis=1,
@@ -1073,9 +1082,9 @@
             land,
             every,
             *sems,
-            work,
+            lambda number, slot: None,
             (FIRST_KIND, FIRST_STEP, FIRST_WHAT),
-            (send_columns, norm_own, pass_columns, wait_columns, next_product),
+            (send_columns, norm_own, pass_columns, wait_columns, next_product, turn_block),
         )
         save.wait()
         finish()
@@ -1126,10 +1135,16 @@
     )(hidden, packed, up_bias, frequency, qkv_weight, up_weight)
 
 
-def backward_gather(grad, out_weight, down_weight, inner, mixed, active):
+def backward_gather(grad, out_weight, down_weight, inner, mixed, active, layer, swap=()):
     rows = grad.shape[0]
 
-    def kernel(own, out_weight, down_weight, inner, mixed, active, grad_mixed, grad_inner, branch, *refs):
+    def kernel(own, out_weight, down_weight, inner, mixed, active, *refs):
+        if swap:
+            source, grad_mixed, grad_inner, branch, target, swap_sem = refs[:6]
+            refs = refs[6:]
+        else:
+            grad_mixed, grad_inner, branch = refs[:3]
+            refs = refs[3:]
         out_part, down_part, weight_sem, total = refs[:4]
         fetched, fetch_sem, rings, ring_sem = refs[4:7], refs[7], refs[8:10], refs[10]
         land, sems = refs[11], refs[12:]
@@ -1150,10 +1165,14 @@
                 for which, (ring, result) in enumerate(zip(rings, (grad_mixed, grad_inner)))
             ]
 
-        weights = load_all(((out_weight, out_part), (down_weight, down_part)), weight_sem)
+        weights = load_all(
+            ((out_weight.at[layer], out_part), (down_weight.at[layer], down_part)), weight_sem
+        )
         for copy in fetch(jnp.int32(0)):
             copy.start()
-        greet_neighbours()
+        greet_neighbours(bool(swap))
+        if swap:
+            plane_swap((source, target), swap_sem).start()
         land[ctx * SIDE + place] = own[...]
         total[...] = jnp.zeros_like(total)
 
@@ -1191,6 +1210,8 @@
 
         gather_blocks(land, None, *sems, work)
         branch[...] = total[...].astype(jnp.bfloat16)
+        if swap:
+            plane_swap((source, target), swap_sem).wait()
         for number in (GROUP - 2, GROUP - 1):
             wait_all(leave(jnp.int32(number)))
 
@@ -1200,12 +1221,14 @@
             jax.ShapeDtypeStruct((GROUP, rows, HEAD_COLS), jnp.float32),
             jax.ShapeDtypeStruct((GROUP, rows, FEED_COLS), jnp.bfloat16),
             jax.ShapeDtypeStruct((BACK_COLS, D), jnp.bfloat16),
-        ),
-        in_specs=[VMEM] + [HBM] * 5,
-        out_specs=(HBM, HBM, VMEM),
-        scratch_shapes=[
-            pltpu.VMEM(out_weight.shape, jnp.bfloat16),
-            pltpu.VMEM(down_weight.shape, jnp.bfloat16),
+        )
+        + tuple(jax.ShapeDtypeStruct(array.shape, array.dtype) for array in swap),
+        in_specs=[VMEM] + [HBM] * (5 + len(swap)),
+        out_specs=(HBM, HBM, VMEM) + (HBM,) * len(swap),
+        scratch_shapes=[pltpu.SemaphoreType.DMA((2,))] * len(swap)
+        + [
+            pltpu.VMEM(out_weight.shape[1:], jnp.bfloat16),
+            pltpu.VMEM(down_weight.shape[1:], jnp.bfloat16),
             pltpu.SemaphoreType.DMA((2,)),
             pltpu.VMEM((BACK_COLS, D), jnp.float32),
             pltpu.VMEM((2, rows, FEED_COLS), jnp.float32),
@@ -1218,9 +1241,9 @@
         ]
         + gather_scratch(rows),
         compiler_params=pltpu.CompilerParams(
-            collective_id=4, has_side_effects=True, vmem_limit_bytes=ROOM
+            collective_id=50 + layer, has_side_effects=True, vmem_limit_bytes=ROOM
         ),
-    )(grad, out_weight, down_weight, inner, mixed, active)
+    )(grad, out_weight, down_weight, inner, mixed, active, *swap)
 
 
 SCATTER_OPS = (
@@ -1448,23 +1471,30 @@
     ]
 
 
-def forward_scatter(hidden, bias, mixed, active, out_weight, down_weight, layer):
+def forward_scatter(hidden, bias, mixed, active, out_weight, down_weight, layer, swap=()):
     rows = hidden.shape[0]
 
-    def kernel(hidden, bias, mixed, active, out_weight, down_weight, out, *refs):
+    def kernel(hidden, bias, mixed, active, out_weight, down_weight, *refs):
+        if swap:
+            source, out, target, swap_sem = refs[:4]
+            refs = refs[4:]
+        else:
+            out, refs = refs[0], refs[1:]
         hidden_part, mixed_part, active_part, out_part, down_part, load_sem = refs[:6]
         scratch = refs[6:]
         loads = load_all(
             (
                 (mixed, mixed_part),
                 (active, active_part),
-                (out_weight, out_part),
-                (down_weight, down_part),
+                (out_weight.at[layer], out_part),
+                (down_weight.at[layer], down_part),
                 (hidden, hidden_part),
             ),
             load_sem,
         )
-        greet_neighbours()
+        greet_neighbours(bool(swap))
+        if swap:
+            plane_swap((source, target), swap_sem).start()
         wait_all(loads[:4])
 
         def partial(slot):
@@ -1473,22 +1503,27 @@
         scatter_events(partial, None, None, SCATTER_OPS, scratch)
         loads[4].wait()
         out[...] = hidden_part[...].astype(jnp.float32) + (scratch[0][...] + bias[...])
+        if swap:
+            plane_swap((source, target), swap_sem).wait()
 
     return pl.pallas_call(
         kernel,
-        out_shape=jax.ShapeDtypeStruct((rows, D), jnp.float32),
-        in_specs=[HBM, VMEM] + [HBM] * 4,
-        out_specs=VMEM,
-        scratch_shapes=[
-            pltpu.VMEM(array.shape, array.dtype)
-            for array in (hidden, mixed, active, out_weight, down_weight)
+        out_shape=(jax.ShapeDtypeStruct((rows, D), jnp.float32),)
+        + tuple(jax.ShapeDtypeStruct(array.shape, array.dtype) for array in swap),
+        in_specs=[HBM, VMEM] + [HBM] * (4 + len(swap)),
+        out_specs=(VMEM,) + (HBM,) * len(swap),
+        scratch_shapes=[pltpu.SemaphoreType.DMA((2,))] * len(swap)
+        + [pltpu.VMEM(array.shape, array.dtype) for array in (hidden, mixed, active)]
+        + [
+            pltpu.VMEM(out_weight.shape[1:], jnp.bfloat16),
+            pltpu.VMEM(down_weight.shape[1:], jnp.bfloat16),
         ]
         + [pltpu.SemaphoreType.DMA((5,))]
         + scatter_scratch(rows),
         compiler_params=pltpu.CompilerParams(
             collective_id=10 + layer, has_side_effects=True, vmem_limit_bytes=ROOM
         ),
-    )(hidden, bias, mixed, active, out_weight, down_weight)
+    )(hidden, bias, mixed, active, out_weight, down_weight, *swap)
 
 
 SMALL_ROWS = 16
@@ -1511,17 +1546,17 @@
         if collects:
             outputs, others, refs = refs[:2], refs[2:4], refs[4:]
         else:
-            mine, refs = refs[0], refs[1:]
+            summed, refs = refs[0], refs[1:]
         hidden, grad, grad_joint, grad_inner, columns, load_sem, strips, load = refs[:8]
         shares, small_land, small_mine, small_other = refs[8:12]
         small_send, small_recv, swap_send, swap_recv = refs[12:16]
-        refs = refs[16:]
+        mine, other, cross_send, cross_recv = refs[16:20]
+        refs = refs[20:]
         if collects:
-            mine, other, summed, arrived, arrived_up = refs[:5]
-            cross_send, cross_recv, plane_send, plane_recv = refs[5:9]
-            back_send, back_recv, keep = refs[9:12]
-            up_send, up_recv, up_own, half_send, half_recv = refs[12:17]
-            refs = refs[17:]
+            summed, arrived, arrived_up, plane_send, plane_recv = refs[:5]
+            back_send, back_recv, keep = refs[5:8]
+            up_send, up_recv, up_own, half_send, half_recv, half_own = refs[8:14]
+            refs = refs[14:]
         scratch = refs
         total = scratch[0]
         ctx, place, seq = lax.axis_index("ctx"), lax.axis_index("fsdp"), lax.axis_index("seq")
@@ -1550,6 +1585,7 @@
             load_sem,
         )
         load_strip(jnp.int32(0)).start()
+        shares[...] = jnp.zeros_like(shares)
         greet_plane(GROUP)
 
         def partial(slot):
@@ -1566,15 +1602,15 @@
                 load_strip(turn + 1).start()
 
             strip = strips[lax.rem(turn, 2)].reshape(tokens, 2 * SHARE)
-            made = dot(strip, grad_joint[...].reshape(tokens, JOINT_COLS), 0, 0).astype(jnp.bfloat16)
+            result = dot(strip, grad_joint[...].reshape(tokens, JOINT_COLS), 0, 0).astype(jnp.bfloat16)
             for which in range(2):
-                mine[2 * pair + which, :, :JOINT_COLS] = made[which * SHARE : (which + 1) * SHARE]
+                mine[2 * pair + which, :, :JOINT_COLS] = result[which * SHARE : (which + 1) * SHARE]
             if not collects:
-                made = dot(strip, grad_inner[...].reshape(tokens, FEED_COLS), 0, 0).astype(
+                result = dot(strip, grad_inner[...].reshape(tokens, FEED_COLS), 0, 0).astype(
                     jnp.bfloat16
                 )
                 for which in range(2):
-                    mine[2 * pair + which, :, JOINT_COLS:] = made[which * SHARE : (which + 1) * SHARE]
+                    mine[2 * pair + which, :, JOINT_COLS:] = result[which * SHARE : (which + 1) * SHARE]
 
         def cross_copy(block):
             return to_axis(
@@ -1599,7 +1635,7 @@
             return [
                 to_axis(
                     own.at[pl.ds(piece * (half // 4), half // 4)],
-                    there.at[pl.ds(piece * (half // 4), half // 4)],
+                    there.at[pl.ds(pl.multiple_of(seq * half + piece * (half // 4), half // 4), half // 4)],
                     half_send.at[at, piece],
                     half_recv.at[at, piece],
                     "seq",
@@ -1607,6 +1643,12 @@
                 )
                 for at, (own, there) in enumerate(zip(inputs[8:10], others))
                 for piece in pieces
+            ]
+
+        def half_kept():
+            return [
+                pltpu.make_async_copy(own, there.at[part_rows], half_own.at[at])
+                for at, (own, there) in enumerate(zip(inputs[8:10], others))
             ]
 
         def final_pieces(source):
@@ -1643,23 +1685,38 @@
                     mine[block, part_rows].astype(jnp.float32) + other[block].astype(jnp.float32)
                 ).astype(jnp.bfloat16)
 
-                @pl.when(block != me)
-                def _(block=block):
-                    plane_copy(block).start()
+                if collects:
+
+                    @pl.when(block != me)
+                    def _(block=block):
+                        plane_copy(block).start()
+
+        def bias_sums():
+            ones = jnp.ones((16, tokens), jnp.bfloat16)
+            joint_bias = dot(ones, grad_joint[...].reshape(tokens, JOINT_COLS))[:1]
+            upper_bias = dot(ones, grad_inner[...].reshape(tokens, FEED_COLS))[:1]
+            for part in range(3):
+                at = part * GROUP + me
+                shares[at // 3, pl.ds(3 + lax.rem(at, 3), 1)] = joint_bias[
+                    :, part * HEAD_COLS : (part + 1) * HEAD_COLS
+                ]
+            for part in range(FEED_COLS // SHARE):
+                shares[me, 6 + part : 7 + part] = upper_bias[:, part * SHARE : (part + 1) * SHARE]
 
         def other_work(turn):
+            pl.when(turn == 1)(bias_sums)
+
             @pl.when(lax.rem(turn, 2) == 0)
             def _():
                 product(turn // 2)
-                if collects:
-                    for which in range(2):
-                        cross_copy(2 * pair_of(turn // 2) + which).start()
+                for which in range(2):
+                    cross_copy(2 * pair_of(turn // 2) + which).start()
+
+            @pl.when((lax.rem(turn, 2) == 1) & (turn > 4))
+            def _():
+                add((turn - 5) // 2)
 
             if collects:
-
-                @pl.when((lax.rem(turn, 2) == 1) & (turn > 4))
-                def _():
-                    add((turn - 5) // 2)
 
                 @pl.when(turn == GROUP - 1)
                 def _():
@@ -1667,6 +1724,11 @@
                         copy.start()
 
         def late_work(step):
+            @pl.when(step == 0)
+            def _():
+                lax.fori_loop(PAIRS - 2, PAIRS, last_adds, 0)
+                arrived[me] = summed[me]
+
             def pass_up(more, carry):
                 number = SIDE * step + more
                 source = lax.rem(me + GROUP - number, GROUP)
@@ -1684,6 +1746,22 @@
                 return carry
 
             lax.fori_loop(0, SIDE, pass_up, 0)
+
+        def pass_joint(step, carry):
+            source = lax.rem(me + GROUP - step, GROUP)
+
+            @pl.when(step > 0)
+            def _():
+                to_peer(
+                    summed.at[source],
+                    arrived.at[source],
+                    plane_send.at[source],
+                    plane_recv.at[source],
+                    source,
+                ).wait_recv()
+
+            pass_on(source, 0)
+            return carry
 
         def last_adds(turn, carry):
             add(turn)
@@ -1698,7 +1776,7 @@
             own_up = pltpu.make_async_copy(inputs[7].at[me], arrived_up.at[me], up_own)
             own_up.start()
             lax.fori_loop(1, GROUP, send_up, 0)
-            for copy in half_copies((0, 1)):
+            for copy in half_copies((0, 1)) + half_kept():
                 copy.start()
         scatter_events(
             partial,
@@ -1708,8 +1786,9 @@
             scratch,
         )
         if collects:
+            lax.fori_loop(0, GROUP, pass_joint, 0)
+        else:
             lax.fori_loop(PAIRS - 2, PAIRS, last_adds, 0)
-            arrived[me] = summed[me]
         wait_all(loads[3:])
 
         def norm_back(part, sums):
@@ -1733,22 +1812,10 @@
 
         zeros = jnp.zeros((8, D), jnp.float32)
         sums = each_strip(rows, norm_back, (zeros, zeros, zeros))
-        shares[...] = jnp.zeros_like(shares)
         for number, folded in enumerate(sums):
             row = jnp.sum(folded, axis=0, keepdims=True)
             for block in range(GROUP):
                 shares[block, number : number + 1] = row[:, block * SHARE : (block + 1) * SHARE]
-        ones = jnp.ones((16, tokens), jnp.bfloat16)
-        joint_bias = dot(ones, grad_joint[...].reshape(tokens, JOINT_COLS))[:1]
-        upper_bias = dot(ones, grad_inner[...].reshape(tokens, FEED_COLS))[:1]
-        for part in range(3):
-            at = part * GROUP + me
-            shares[at // 3, pl.ds(3 + lax.rem(at, 3), 1)] = joint_bias[
-                :, part * HEAD_COLS : (part + 1) * HEAD_COLS
-            ]
-        for part in range(FEED_COLS // SHARE):
-            shares[me, 6 + part : 7 + part] = upper_bias[:, part * SHARE : (part + 1) * SHARE]
-
         def small_copy(step):
             peer = lax.rem(me + step, GROUP)
             return to_peer(
@@ -1761,25 +1828,6 @@
 
         lax.fori_loop(1, GROUP, small_begin, 0)
         small_land[me] = shares[me]
-
-        def pass_joint(step, carry):
-            source = lax.rem(me + GROUP - step, GROUP)
-
-            @pl.when(step > 0)
-            def _():
-                to_peer(
-                    summed.at[source],
-                    arrived.at[source],
-                    plane_send.at[source],
-                    plane_recv.at[source],
-                    source,
-                ).wait_recv()
-
-            pass_on(source, 0)
-            return carry
-
-        if collects:
-            lax.fori_loop(0, GROUP, pass_joint, 0)
 
         def small_end(step, carry):
             source = lax.rem(me + GROUP - step, GROUP)
@@ -1800,9 +1848,13 @@
         swap.wait()
         small_out[...] = small_mine[...] + small_other[...]
 
+        def end_cross(block, carry):
+            cross_copy(block).wait_send()
+            return carry
+
+        lax.fori_loop(0, GROUP, end_cross, 0)
+
         def end(block, carry):
-            cross_copy(block).wait_send()
-
             @pl.when(block != me)
             def _():
                 plane_copy(block).wait_send()
@@ -1818,7 +1870,7 @@
 
         if collects:
             lax.fori_loop(0, GROUP, end, 0)
-            wait_all(half_copies((0, 1, 2, 3)))
+            wait_all(half_copies((0, 1, 2, 3)) + half_kept())
 
     def part(width, height=half):
         return pltpu.VMEM((GROUP, height, width), jnp.bfloat16)
@@ -1835,11 +1887,10 @@
             (
                 jax.ShapeDtypeStruct((SHARE, 3 * D), jnp.bfloat16),
                 jax.ShapeDtypeStruct((SHARE, FF), jnp.bfloat16),
-                jax.ShapeDtypeStruct((half, 3 * D), jnp.bfloat16),
-                jax.ShapeDtypeStruct((half, FF), jnp.bfloat16),
             )
+            * 2
             if collects
-            else (jax.ShapeDtypeStruct((GROUP, SHARE, COLS), jnp.bfloat16),)
+            else (jax.ShapeDtypeStruct((GROUP, half, COLS), jnp.bfloat16),)
         ),
         in_specs=[HBM, HBM, VMEM] + [HBM] * (7 if collects else 4),
         out_specs=(VMEM, VMEM) + ((HBM,) * 4 if collects else (VMEM,)),
@@ -1859,16 +1910,20 @@
             sixteen,
             pltpu.SemaphoreType.DMA,
             pltpu.SemaphoreType.DMA,
+            part(made, SHARE),
+            part(made),
+            sixteen,
+            sixteen,
         ]
         + (
-            [part(JOINT_COLS, SHARE)]
-            + [part(JOINT_COLS)] * 3
+            [part(JOINT_COLS)] * 2
             + [part(FEED_COLS)]
-            + [sixteen] * 4
+            + [sixteen] * 2
             + [places] * 3
             + [sixteen] * 2
             + [pltpu.SemaphoreType.DMA]
             + [pltpu.SemaphoreType.DMA((2, 4))] * 2
+            + [pltpu.SemaphoreType.DMA((2,))]
             if collects
             else []
         )
@@ -2342,7 +2397,7 @@
         return lax.ppermute(values, "seq", swap)
 
     hidden = tokens[0]
-    saved, gains, joint_grads, upper_grads, branch_grads, small_grads = [], [], [], [], [], []
+    saved, gains, joint_grads, upper_grads, small_grads = [], [], [], [], []
     for layer in range(LAYERS):
         if layer == 0:
             *out, small, cosine, sine = first_gather(
@@ -2389,32 +2444,38 @@
         saved.append(
             (hidden, every, columns, query, key, value, inner, active, mixed, turned, stats)
         )
-        hidden = forward_scatter(
+        branches = (
             hidden,
             row_of(layer, OUT_BIAS_ROW) + row_of(layer, DOWN_BIAS_ROW),
             mixed,
             active,
-            out_weight[layer],
-            down_weight[layer],
+            out_weight,
+            down_weight,
             layer,
         )
-    result = hidden.astype(jnp.bfloat16)[None]
+        if layer + 1 < LAYERS:
+            hidden = forward_scatter(*branches)[0]
 
     grad_hidden = cotangent[0].astype(jnp.float32) * keep_mask[0].astype(jnp.float32)[:, None]
-    summed = None
+    summed = branch = None
+    own_branches, other_branches = [], []
     for layer in reversed(range(LAYERS)):
         before, every, columns, query, key, value, inner, active, mixed, turned, stats = saved[layer]
-        grad_mixed, grad_inner, branch = backward_gather(
+        grad_mixed, grad_inner, branch, *other = backward_gather(
             grad_hidden.astype(jnp.bfloat16),
-            out_weight[layer],
-            down_weight[layer],
+            out_weight,
+            down_weight,
             inner,
             mixed,
             active,
-        )
-        branch_grads.insert(
-            0, branch.astype(jnp.float32) + swapped(branch).astype(jnp.float32)
-        )
+            layer,
+            () if layer + 1 == LAYERS else (branch,),
+        )
+        own_branches.insert(0, branch)
+        other_branches = list(other) + other_branches
+        if layer == 0:
+            hidden, other = forward_scatter(*branches, (branch,))
+            other_branches.insert(0, other)
         grad_joint, *rest = attend_plane_back(
             query,
             key,
@@ -2443,16 +2504,16 @@
         )
         small_grads.insert(0, small)
         if layer > 0:
-            own = lax.dynamic_slice_in_dim(grads[0], seq * half, half, axis=1)
-            other = swapped(lax.dynamic_slice_in_dim(grads[0], (1 - seq) * half, half, axis=1))
-            summed = (own.astype(jnp.float32) + other.astype(jnp.float32)).astype(jnp.bfloat16)
+            summed = grads[0]
         else:
-            for total, whole, own, other in zip(
-                (joint_grads, upper_grads), grads[:2], rest[:2], grads[2:]
-            ):
-                first, second = jnp.where(seq == 0, own, other), jnp.where(seq == 0, other, own)
-                total.extend([whole, jnp.concatenate([first, second], axis=0)])
-    branch_grad = jnp.stack(branch_grads)
+            joint_grads.extend(grads[0::2])
+            upper_grads.extend(grads[1::2])
+    here, there = jnp.stack(own_branches), jnp.stack(other_branches)
+    result = hidden.astype(jnp.bfloat16)[None]
+
+    def branch_grad(part):
+        return here[:, part].astype(jnp.float32) + there[:, part].astype(jnp.float32)
+
     small = jnp.stack(small_grads)
     return (
         result,
@@ -2461,11 +2522,11 @@
         small[:, 1],
         jnp.stack(joint_grads).astype(jnp.float32),
         small[:, 3:6].reshape(LAYERS, JOINT_COLS),
-        branch_grad[:, :HEAD_COLS],
+        branch_grad(slice(0, HEAD_COLS)),
         small[:, 2],
         jnp.stack(upper_grads).astype(jnp.float32),
         small[:, 6:10].reshape(LAYERS, FEED_COLS),
-        branch_grad[:, HEAD_COLS:],
+        branch_grad(slice(HEAD_COLS, None)),
         small[:, 2],
     )
 

time: 1100 us -> 1060 us (0.964)
  Pallas kernels: 1020 us -> 1000 us
    pallas_call x1, Pallas kernels: 160 us -> 144 us  [first_gather(): pl.pallas_call(kernel, out_shape=[jax.ShapeDtypeStruct((GROUP, rows, D),...]
  transfers between devices with their start and end apart: 4 -> 1, of which waited for: 0 -> 0; matrix products, arithmetic and copies ran while one was open for 3% -> 0% of each run, Pallas kernels for 43% -> 9%
where the time goes in v4:
time: 1060 us; the launch traced here: 1050 us
  Pallas kernels  1000 us (94%)
  other arithmetic  36.7 us (3%)
  local copies, waits for them, and re-layouts  10.8 us (1%)
    pallas_call x2, Pallas kernels, backward_scatter(): pl.pallas_call(kernel, out_shape=(jax.ShapeDtypeStruct((rows, D), jnp.flo...  245 us
    pallas_call x2, Pallas kernels, backward_gather(): pl.pallas_call(kernel, out_shape=(jax.ShapeDtypeStruct((GROUP, rows, HEAD...  191 us
    pallas_call x2, Pallas kernels, forward_scatter(): pl.pallas_call(kernel, out_shape=(jax.ShapeDtypeStruct((rows, D), jnp.flo...  190 us
    pallas_call x1, Pallas kernels, first_gather(): pl.pallas_call(kernel, out_shape=[jax.ShapeDtypeStruct((GROUP, rows, D),...  144 us
    pallas_call x1, Pallas kernels, forward_gather(): pl.pallas_call(kernel, out_shape=[jax.ShapeDtypeStruct((GROUP, rows, D),...  98.8 us
    pallas_call x2, Pallas kernels, attend_plane_back(): pl.pallas_call(kernel, grid=(SIDE,), out_shape=(jax.ShapeDtypeStruct((SID...  68.1 us
    pallas_call x2, Pallas kernels, attend_plane(): pl.pallas_call(kernel, grid=(SIDE,), out_shape=(shape(rows, HEAD_COLS, jn...  65.5 us
  transfers between devices with their start and end apart: 1, of which 0 were waited for; matrix products, arithmetic and copies ran while one was open for 0% of the time, Pallas kernels for 9%

profile of v4, /device:TPU:0, one launch (start us, length us, event | category | flops | bytes accessed | tf_op | source)
XLA Modules:
  0.0 1052.1 jit_solution(18359818497191945803)
XLA Ops:
  2.1 1.3 fusion.2
  10.3 143.9 %shard_map.238 = (bf16[16,256,2048]{2,1,0:T(8,128)(2,1)}, bf16[16,128,896]{2,1,0:T(8,128)(2,1)}, bf16[16,256,128]{2,1,0:T(8,128)(2,1)}, bf16[16,256,128]{2,1,0:T...) custom-call(bf16[256,2048]{1,0:T(8,128)(2,1)} %bitcast.108, ...), custom_call_target="tpu_custom_call" | custom-call | tf_op jit(solution)/shard_map/pallas_call | solution.py:1105
  157.5 1.5 iota_select_fusion.spot
  159.0 46.2 %shard_map.239 = (bf16[4,4,256,128]{3,2,1,0:T(8,128)(2,1)}, f32[4,4,128,256]{3,2,1,0:T(8,128)}, f32[4,4,1024]{2,1,0:T(4,128)}, bf16[16,64,896]{2,1,0:T(8,128)(2,1)}) custom-call(bf16[4,4,256,128]{3,2,1,0:T(8,128)(2,1)} %bitcast.111, bf16[4,4,256,128]{3,2,1,0:T(8,128)(2,1)} %bitcast.113, bf16[4,4,256,128]{3,2,1,0:T(8,128)(2,1)} %bitcast.115, ...), custom_call_target="tpu_custom_call" | custom-call | tf_op jit(solution)/shard_map/pallas_call | solution.py:2183
  205.2 1.6 collective-permute-start
  207.6 1.8 slice_bitcast_fusion
  209.5 94.0 %shard_map.240.hidden.refs_0_ = f32[256,2048]{1,0:T(8,128)} custom-call(bf16[256,2048]{1,0:T(8,128)(2,1)} %bitcast.109, f32[1,2048]{1,0:T(1,128)} %get-tuple-element.112.bias, bf16[16,256,128]{2,1,0:T(8,128)(2,1)} %bitcast.117, bf16[16,256,512]{2,1,0:T(8,128)(2,1)} %get-tuple-element.63.active, bf16[2,128,2048]{2,1,0:T(8,128)(2,1)} %out_weight.7, ...), custom_call_target="tpu_custom_call" | custom-call | tf_op jit(solution)/shard_map/pallas_call | solution.py:1509
  304.1 1.9 fusion.1
  307.2 98.8 %shard_map.241 = (bf16[16,256,2048]{2,1,0:T(8,128)(2,1)}, bf16[16,128,896]{2,1,0:T(8,128)(2,1)}, bf16[16,256,128]{2,1,0:T(8,128)(2,1)}, bf16[16,256,128]{2,1,0:T...) custom-call(f32[256,2048]{1,0:T(8,128)} %shard_map.240.hidden.refs_0_, ...), custom_call_target="tpu_custom_call" | custom-call | tf_op jit(solution)/shard_map/pallas_call | solution.py:900
  406.0 19.3 %shard_map.242 = (bf16[4,4,256,128]{3,2,1,0:T(8,128)(2,1)}, f32[4,4,128,256]{3,2,1,0:T(8,128)}, f32[4,4,1024]{2,1,0:T(4,128)}) custom-call(bf16[4,4,256,128]{3,2,1,0:T(8,128)(2,1)} %bitcast.121, bf16[4,4,256,128]{3,2,1,0:T(8,128)(2,1)} %bitcast.123, bf16[4,4,256,128]{3,2,1,0:T(8,128)(2,1)} %bitcast.125, s32[4,1,1024]{2,1,0:T(1,128)} %convert_element_type.171.begin, ...), custom_call_target="tpu_custom_call" | custom-call | tf_op jit(solution)/shard_map/pallas_call | solution.py:2183
  425.3 96.5 %shard_map.243 = (f32[16,256,128]{2,1,0:T(8,128)}, bf16[16,256,512]{2,1,0:T(8,128)(2,1)}, bf16[640,2048]{1,0:T(8,128)(2,1)}) custom-call(bf16[256,2048]{1,0:T(8,128)(2,1)} %get-tuple-element.106.own, bf16[2,128,2048]{2,1,0:T(8,128)(2,1)} %out_weight.7, bf16[2,512,2048]{2,1,0:T(8,128)(2,1)} %down_weight.7, f32[16,256,512]{2,1,0:T(8,128)} %get-tuple-element.72.inner, ...), custom_call_target="tpu_custom_call" | custom-call | tf_op jit(solution)/shard_map/pallas_call | solution.py:1218
  521.9 21.6 %shard_map.244 = bf16[4,4,256,384]{3,2,1,0:T(8,128)(2,1)} custom-call(bf16[4,4,256,128]{3,2,1,0:T(8,128)(2,1)} %bitcast.122, bf16[4,4,256,128]{3,2,1,0:T(8,128)(2,1)} %bitcast.124, bf16[4,4,256,128]{3,2,1,0:T(8,128)(2,1)} %bitcast.126, f32[4,4,256,128]{3,2,1,0:T(8,128)} %bitcast.131, f32[4,4,256,128]{3,2,1,0:T(8,128)} %bitcast.99, ...), custom_call_target="tpu_custom_call" | custom-call | tf_op jit(solution)/shard_map/pallas_call | solution.py:2304
  543.5 107.4 %shard_map.245 = (f32[256,2048]{1,0:T(8,128)}, f32[16,128]{1,0:T(8,128)}, bf16[16,64,896]{2,1,0:T(8,128)(2,1)}) custom-call(f32[256,2048]{1,0:T(8,128)} %shard_map.240.hidden.refs_0_, f32[256,2048]{1,0:T(8,128)} %get-tuple-element.107.refs_1_, f32[1,2048]{1,0:T(1,128)} %get-tuple-element.110.gain.refs_2_, bf16[16,256,384]{2,1,0:T(8,128)(2,1)} %bitcast.103, ...), custom_call_target="tpu_custom_call" | custom-call | tf_op jit(solution)/shard_map/pallas_call | solution.py:1880
  650.9 2.7 convert_element_type.176.own
  653.6 94.6 %shard_map.246 = (f32[16,256,128]{2,1,0:T(8,128)}, bf16[16,256,512]{2,1,0:T(8,128)(2,1)}, bf16[640,2048]{1,0:T(8,128)(2,1)}, bf16[640,2048]{1,0:T(8,128)(2,1)}) custom-call(bf16[256,2048]{1,0:T(8,128)(2,1)} %convert_element_type.176.own, bf16[2,128,2048]{2,1,0:T(8,128)(2,1)} %out_weight.7, bf16[2,512,2048]{2,1,0:T(8,128)(2,1)} %down_weight.7, ...), custom_call_target="tpu_custom_call" | custom-call | tf_op jit(solution)/shard_map/pallas_call | solution.py:1218
  748.2 46.5 %shard_map.248 = (bf16[4,4,256,384]{3,2,1,0:T(8,128)(2,1)}, bf16[64,6144]{1,0:T(8,128)(2,1)}, bf16[64,8192]{1,0:T(8,128)(2,1)}, bf16[16,64,512]{2,1,0:T(8,128)(2,1)}) custom-call(bf16[4,4,256,128]{3,2,1,0:T(8,128)(2,1)} %bitcast.112, bf16[4,4,256,128]{3,2,1,0:T(8,128)(2,1)} %bitcast.114, bf16[4,4,256,128]{3,2,1,0:T(8,128)(2,1)} %bitcast.116, ...), custom_call_target="tpu_custom_call" | custom-call | tf_op jit(solution)/shard_map/pallas_call | solution.py:2304
  794.7 137.3 %shard_map.249 = (f32[256,2048]{1,0:T(8,128)}, f32[16,128]{1,0:T(8,128)}, bf16[128,6144]{1,0:T(8,128)(2,1)}, bf16[128,8192]{1,0:T(8,128)(2,1)}, bf16[128,6144]{1,0:T(8,128)(2,1)}, /*index=5*/bf16[128,8192]{1,0:T(8,128)(2,1)}) custom-call(bf16[256,2048]{1,0:T(8,128)(2,1)} %bitcast.110, f32[256,2048]{1,0:T(8,128)} %get-tuple-element.79.refs_1_, ...), custom_call_target="tpu_custom_call" | custom-call | tf_op jit(solution)/shard_map/pallas_call | solution.py:1880
  932.0 1.4 pad_maximum_fusion.4
  934.8 95.7 %shard_map.247 = (f32[256,2048]{1,0:T(8,128)}, bf16[640,2048]{1,0:T(8,128)(2,1)}) custom-call(f32[256,2048]{1,0:T(8,128)} %shard_map.240.hidden.refs_0_, f32[1,2048]{1,0:T(1,128)} %get-tuple-element.111.bias, bf16[16,256,128]{2,1,0:T(8,128)(2,1)} %bitcast.120, bf16[16,256,512]{2,1,0:T(8,128)(2,1)} %get-tuple-element.71.active, ...), custom_call_target="tpu_custom_call" | custom-call | tf_op jit(solution)/shard_map/pallas_call | solution.py:1509
  1030.5 3.2 convert_add_fusion.1
  1035.0 4.2 convert_add_fusion
  1041.5 3.5 maximum_convert_fusion.1
  1045.8 3.9 maximum_convert_fusion
  1050.3 1.3 copy.57
  (65 shorter events, 20.6 us)
Async XLA Ops:
  205.2 100.8 %collective-permute-start = (bf16[16,64,896]{2,1,0:T(8,128)(2,1)}, bf16[16,64,896]{2,1,0:T(8,128)(2,1)S(1)}, u32[]{:S(2)}, u32[]{:S(2)}) collective-permute-start(bf16[16,64,896]{2,1,0:T(8,128)(2,1)} %get-tuple-element.66.own_half), channel_id=1, source_target_pairs={{0,16},{16,0},{1,17},{17,1},{2,18},{18,2},{3,19},{19,3},{4,20},{20... | collective-permute-start | bytes 5505032 | tf_op jit(solution)/shard_map/ppermute | solution.py:2397
  209.5 94.6 %copy-start.11 = (bf16[1,256,2048]{2,1,0:T(8,128)(2,1)S(1)}, bf16[1,256,2048]{2,1,0:T(8,128)(2,1)}, u32[]{:S(2)}) copy-start(bf16[1,256,2048]{2,1,0:T(8,128)(2,1)} %param.28) | copy-start | bytes 3145732
  306.0 1.2 copy-start.8
  794.7 137.3 %copy-start.12 = (f32[16,128]{1,0:T(8,128)S(1)}, f32[16,128]{1,0:T(8,128)}, u32[]{:S(2)}) copy-start(f32[16,128]{1,0:T(8,128)} %get-tuple-element.97) | copy-start | bytes 24580
  933.4 116.4 %copy-start.13 = (f32[2,1,128]{2,1,0:T(1,128)}, f32[2,1,128]{2,1,0:T(1,128)S(1)}, u32[]{:S(2)}) copy-start(f32[2,1,128]{2,1,0:T(1,128)S(1)} %get-tuple-element.113) | copy-start | bytes 3076
  934.8 95.7 %copy-start = (bf16[640,2048]{1,0:T(8,128)(2,1)S(1)}, bf16[640,2048]{1,0:T(8,128)(2,1)}, u32[]{:S(2)}) copy-start(bf16[640,2048]{1,0:T(8,128)(2,1)} %get-tuple-element.82.refs_0_) | copy-start | bytes 7864324
  1030.5 3.2 copy-start.1
  1030.5 3.3 copy-start.2
  1030.5 4.5 copy-start.3
  1035.0 4.2 copy-start.4
  1039.2 2.3 copy-start.9
  1039.2 2.3 copy-start.10
  1041.5 3.5 copy-start.6
  1041.5 4.3 copy-start.7
  1045.8 4.5 copy-start.5

commit v5 on v4

--- a/solution.py
+++ b/solution.py
@@ -1471,17 +1471,147 @@
     ]
 
 
-def forward_scatter(hidden, bias, mixed, active, out_weight, down_weight, layer, swap=()):
+SMALL_ROWS = 16
+PAIRS = GROUP // 2
+
+
+def norm_back_strip(hidden, grad, total, gain, out, part):
+    values = hidden[part].astype(jnp.float32)
+    centred = values - jnp.mean(values, axis=1, keepdims=True)
+    spread = jnp.mean(centred * centred, axis=1, keepdims=True)
+    root = lax.rsqrt(spread + EPS)
+    normed = centred * root
+    above = total[part]
+    scaled = above * gain[...]
+    down = jnp.mean(scaled, axis=1, keepdims=True)
+    along = jnp.mean(scaled * normed, axis=1, keepdims=True)
+    passing = grad[part]
+    out[part] = passing + root * (scaled - down - normed * along)
+    low = passing.astype(jnp.bfloat16).astype(jnp.float32)
+    return tuple(
+        jnp.sum(sums.reshape(STRIP // 8, 8, D), axis=0) for sums in (above * normed, above, low)
+    )
+
+
+def small_exchange(shares, land, mine, other, out, sems):
+    send, recv, swap_send, swap_recv = sems
+    me = lax.axis_index("ctx") * SIDE + lax.axis_index("fsdp")
+
+    def copy(step):
+        peer = lax.rem(me + step, GROUP)
+        return to_peer(shares.at[peer], land.at[me], send.at[step], recv.at[me], peer)
+
+    def swap():
+        return to_axis(mine, other, swap_send, swap_recv, "seq", 1 - lax.axis_index("seq"))
+
+    def begin(sums):
+        for number, folded in enumerate(sums):
+            row = jnp.sum(folded, axis=0, keepdims=True)
+            for block in range(GROUP):
+                shares[block, number : number + 1] = row[:, block * SHARE : (block + 1) * SHARE]
+
+        def start(step, carry):
+            copy(step).start()
+            return carry
+
+        lax.fori_loop(1, GROUP, start, 0)
+        land[me] = shares[me]
+
+    def middle():
+        def arrive(step, carry):
+            source = lax.rem(me + GROUP - step, GROUP)
+            to_peer(shares.at[source], land.at[source], send.at[step], recv.at[source], source).wait_recv()
+            copy(step).wait_send()
+            return carry
+
+        lax.fori_loop(1, GROUP, arrive, 0)
+        mine[...] = jnp.sum(land[...], axis=0)
+        swap().start()
+
+    def end():
+        swap().wait()
+        out[...] = mine[...] + other[...]
+
+    return begin, middle, end
+
+
+def small_scratch():
+    small = (SMALL_ROWS, SHARE)
+    return [
+        pltpu.VMEM((GROUP,) + small, jnp.float32),
+        pltpu.VMEM(small, jnp.float32),
+        pltpu.VMEM(small, jnp.float32),
+        pltpu.SemaphoreType.DMA((GROUP,)),
+        pltpu.SemaphoreType.DMA((GROUP,)),
+        pltpu.SemaphoreType.DMA,
+        pltpu.SemaphoreType.DMA,
+    ]
+
+
+def half_swaps(halves, wholes, sems, pieces=4):
+    send, recv, own = sems
+    seq = lax.axis_index("seq")
+    half = SHARE // 2
+    size = half // pieces
+
+    def copies(which):
+        return [
+            to_axis(
+                source.at[pl.ds(piece * size, size)],
+                target.at[pl.ds(pl.multiple_of(seq * half + piece * size, size), size)],
+                send.at[at, piece],
+                recv.at[at, piece],
+                "seq",
+                1 - seq,
+            )
+            for at, (source, target) in enumerate(zip(halves, wholes))
+            for piece in which
+        ]
+
+    def kept():
+        rows = pl.ds(pl.multiple_of(seq * half, half), half)
+        return [
+            pltpu.make_async_copy(source, target.at[rows], own.at[at])
+            for at, (source, target) in enumerate(zip(halves, wholes))
+        ]
+
+    return copies, kept
+
+
+def half_sems(pieces=4):
+    return [
+        pltpu.SemaphoreType.DMA((2, pieces)),
+        pltpu.SemaphoreType.DMA((2, pieces)),
+        pltpu.SemaphoreType.DMA((2,)),
+    ]
+
+
+WHOLES = (
+    jax.ShapeDtypeStruct((SHARE, 3 * D), jnp.bfloat16),
+    jax.ShapeDtypeStruct((SHARE, FF), jnp.bfloat16),
+)
+HALVES = (
+    jax.ShapeDtypeStruct((SHARE // 2, 3 * D), jnp.bfloat16),
+    jax.ShapeDtypeStruct((SHARE // 2, FF), jnp.bfloat16),
+)
+
+
+def forward_scatter(hidden, bias, mixed, active, out_weight, down_weight, layer, rest=None):
     rows = hidden.shape[0]
+    last = rest is not None
 
     def kernel(hidden, bias, mixed, active, out_weight, down_weight, *refs):
-        if swap:
-            source, out, target, swap_sem = refs[:4]
-            refs = refs[4:]
+        if last:
+            (below_total, below_hidden, below_grad, gain, below_shares, joint, upper, branch), refs = (
+                refs[:8],
+                refs[8:],
+            )
+            out, grad_out, small_out, joint_out, upper_out, branch_out = refs[:6]
+            refs = refs[6:]
         else:
             out, refs = refs[0], refs[1:]
         hidden_part, mixed_part, active_part, out_part, down_part, load_sem = refs[:6]
-        scratch = refs[6:]
+        refs = refs[6:]
         loads = load_all(
             (
                 (mixed, mixed_part),
@@ -1492,71 +1622,134 @@
             ),
             load_sem,
         )
-        greet_neighbours(bool(swap))
-        if swap:
-            plane_swap((source, target), swap_sem).start()
+        other_work = None
+        if last:
+            parts, part_sem, sums, swap_sem = refs[:4], refs[4], refs[5], refs[6]
+            shares, small, swap_sems, refs = parts[3], refs[7:14], refs[14:17], refs[17:]
+            below = load_all(
+                tuple(zip((below_total, below_hidden, below_grad, below_shares), parts)), part_sem
+            )
+            small_begin, small_middle, small_end = small_exchange(
+                shares, small[0], small[1], small[2], small_out, small[3:]
+            )
+            copies, kept = half_swaps((joint, upper), (joint_out, upper_out), swap_sems)
+            greet_plane(GROUP)
+            for copy in copies((0, 1, 2, 3)) + kept():
+                copy.start()
+            sums[...] = jnp.zeros_like(sums)
+            strips = rows // STRIP
+
+            def other_work(turn):
+                @pl.when(turn == 0)
+                def _():
+                    wait_all(below)
+
+                @pl.when(turn < strips)
+                def _():
+                    part = pl.ds(pl.multiple_of(turn * STRIP, STRIP), STRIP)
+                    found = norm_back_strip(parts[1], parts[2], parts[0], gain, grad_out, part)
+                    for number, folded in enumerate(found):
+                        sums[number] += folded
+
+                @pl.when(turn == strips)
+                def _():
+                    small_begin([sums[number] for number in range(3)])
+
+                @pl.when(turn == GROUP - 4)
+                def _():
+                    small_middle()
+                    plane_swap((branch, branch_out), swap_sem).start()
+
+        else:
+            greet_neighbours()
+        scratch = refs
         wait_all(loads[:4])
 
         def partial(slot):
             return dot(mixed_part[slot], out_part[...]) + dot(active_part[slot], down_part[...])
 
-        scatter_events(partial, None, None, SCATTER_OPS, scratch)
+        scatter_events(
+            partial, other_work, None, SCATTER_OPS_WORK if last else SCATTER_OPS, scratch
+        )
         loads[4].wait()
         out[...] = hidden_part[...].astype(jnp.float32) + (scratch[0][...] + bias[...])
-        if swap:
-            plane_swap((source, target), swap_sem).wait()
-
+        if last:
+            small_end()
+            wait_all(copies((0, 1, 2, 3)) + kept())
+            plane_swap((branch, branch_out), swap_sem).wait()
+
+    out_shape = (jax.ShapeDtypeStruct((rows, D), jnp.float32),)
+    out_specs = (VMEM,)
+    extra_scratch = []
+    if last:
+        total, before, grad, _, shares, _, _, branch = rest
+        out_shape += (
+            (
+                jax.ShapeDtypeStruct((rows, D), jnp.float32),
+                jax.ShapeDtypeStruct((SMALL_ROWS, SHARE), jnp.float32),
+            )
+            + WHOLES
+            + (jax.ShapeDtypeStruct(branch.shape, branch.dtype),)
+        )
+        out_specs += (VMEM, VMEM, HBM, HBM, HBM)
+        extra_scratch = (
+            [pltpu.VMEM(array.shape, array.dtype) for array in (total, before, grad, shares)]
+            + [
+                pltpu.SemaphoreType.DMA((4,)),
+                pltpu.VMEM((3, 8, D), jnp.float32),
+                pltpu.SemaphoreType.DMA((2,)),
+            ]
+            + small_scratch()
+            + half_sems()
+        )
     return pl.pallas_call(
         kernel,
-        out_shape=(jax.ShapeDtypeStruct((rows, D), jnp.float32),)
-        + tuple(jax.ShapeDtypeStruct(array.shape, array.dtype) for array in swap),
-        in_specs=[HBM, VMEM] + [HBM] * (4 + len(swap)),
-        out_specs=(VMEM,) + (HBM,) * len(swap),
-        scratch_shapes=[pltpu.SemaphoreType.DMA((2,))] * len(swap)
-        + [pltpu.VMEM(array.shape, array.dtype) for array in (hidden, mixed, active)]
+        out_shape=out_shape,
+        in_specs=[HBM, VMEM] + [HBM] * 4 + ([HBM] * 3 + [VMEM] + [HBM] * 4 if last else []),
+        out_specs=out_specs,
+        scratch_shapes=[pltpu.VMEM(array.shape, array.dtype) for array in (hidden, mixed, active)]
         + [
             pltpu.VMEM(out_weight.shape[1:], jnp.bfloat16),
             pltpu.VMEM(down_weight.shape[1:], jnp.bfloat16),
         ]
         + [pltpu.SemaphoreType.DMA((5,))]
+        + extra_scratch
         + scatter_scratch(rows),
         compiler_params=pltpu.CompilerParams(
             collective_id=10 + layer, has_side_effects=True, vmem_limit_bytes=ROOM
         ),
-    )(hidden, bias, mixed, active, out_weight, down_weight, *swap)
-
-
-SMALL_ROWS = 16
-PAIRS = GROUP // 2
+    )(hidden, bias, mixed, active, out_weight, down_weight, *(rest or ()))
 
 
 def backward_scatter(
     hidden, grad, gain, grad_joint, grad_inner, columns, every, layer, up=None, halves=()
 ):
-    rows = hidden.shape[0]
+    rows = grad.shape[0]
     half = SHARE // 2
     collects = up is not None
     made = JOINT_COLS if collects else COLS
     tokens = GROUP * rows
 
     def kernel(*refs):
-        inputs, refs = refs[: 10 if collects else 7], refs[10 if collects else 7 :]
-        gain, every = inputs[2], inputs[6]
-        out, small_out, refs = refs[0], refs[1], refs[2:]
         if collects:
-            outputs, others, refs = refs[:2], refs[2:4], refs[4:]
+            (joint_in, inner_in, columns_in, every, up, *halves), refs = refs[:7], refs[7:]
+            out, shares, joint_half, up_half, *wholes = refs[:6]
+            refs = refs[6:]
         else:
-            summed, refs = refs[0], refs[1:]
-        hidden, grad, grad_joint, grad_inner, columns, load_sem, strips, load = refs[:8]
-        shares, small_land, small_mine, small_other = refs[8:12]
-        small_send, small_recv, swap_send, swap_recv = refs[12:16]
-        mine, other, cross_send, cross_recv = refs[16:20]
-        refs = refs[20:]
+            (joint_in, inner_in, columns_in, every, hidden_in, grad_in, gain), refs = refs[:7], refs[7:]
+            out, small_out, summed, refs = refs[0], refs[1], refs[2], refs[3:]
+        grad_joint, grad_inner, columns, load_sem, strips, load = refs[:6]
+        mine, other, cross_send, cross_recv = refs[6:10]
+        refs = refs[10:]
         if collects:
-            summed, arrived, arrived_up, plane_send, plane_recv = refs[:5]
-            back_send, back_recv, keep = refs[5:8]
-            up_send, up_recv, up_own, half_send, half_recv, half_own = refs[8:14]
-            refs = refs[14:]
+            summed, plane_send, plane_recv, plane_own, up_send, up_recv, up_own = refs[:7]
+            swap_sems, refs = refs[7:10], refs[10:]
+            copies, kept = half_swaps(halves, wholes, swap_sems)
+        else:
+            hidden, grad, shares, small, refs = refs[0], refs[1], refs[2], refs[3:10], refs[10:]
+            small_begin, small_middle, small_end = small_exchange(
+                shares, small[0], small[1], small[2], small_out, small[3:]
+            )
         scratch = refs
         total = scratch[0]
         ctx, place, seq = lax.axis_index("ctx"), lax.axis_index("fsdp"), lax.axis_index("seq")
@@ -1574,16 +1767,10 @@
                 every.at[:, :, pl.ds(start, 2 * SHARE)], strips.at[buffer], load.at[buffer]
             )
 
-        loads = load_all(
-            (
-                (inputs[3], grad_joint),
-                (inputs[4], grad_inner),
-                (inputs[5], columns),
-                (inputs[0], hidden),
-                (inputs[1], grad),
-            ),
-            load_sem,
-        )
+        pairs = [(joint_in, grad_joint), (inner_in, grad_inner), (columns_in, columns)]
+        if not collects:
+            pairs += [(hidden_in, hidden), (grad_in, grad)]
+        loads = load_all(pairs, load_sem)
         load_strip(jnp.int32(0)).start()
         shares[...] = jnp.zeros_like(shares)
         greet_plane(GROUP)
@@ -1602,7 +1789,9 @@
                 load_strip(turn + 1).start()
 
             strip = strips[lax.rem(turn, 2)].reshape(tokens, 2 * SHARE)
-            result = dot(strip, grad_joint[...].reshape(tokens, JOINT_COLS), 0, 0).astype(jnp.bfloat16)
+            result = dot(strip, grad_joint[...].reshape(tokens, JOINT_COLS), 0, 0).astype(
+                jnp.bfloat16
+            )
             for which in range(2):
                 mine[2 * pair + which, :, :JOINT_COLS] = result[which * SHARE : (which + 1) * SHARE]
             if not collects:
@@ -1610,7 +1799,9 @@
                     jnp.bfloat16
                 )
                 for which in range(2):
-                    mine[2 * pair + which, :, JOINT_COLS:] = result[which * SHARE : (which + 1) * SHARE]
+                    mine[2 * pair + which, :, JOINT_COLS:] = result[
+                        which * SHARE : (which + 1) * SHARE
+                    ]
 
         def cross_copy(block):
             return to_axis(
@@ -1622,60 +1813,39 @@
                 1 - seq,
             )
 
-        def plane_copy(block):
-            return to_peer(
-                summed.at[block], arrived.at[me], plane_send.at[block], plane_recv.at[me], block
-            )
+        def joint_places():
+            return [
+                (at, joint_half.at[:, pl.ds(start, width)], pl.ds(at * HEAD_COLS, HEAD_COLS))
+                for at, (_, start, _, width) in enumerate(column_places(me)[:3])
+            ]
+
+        def plane_copies(block):
+            return [
+                to_peer(
+                    summed.at[block, :, piece],
+                    target,
+                    plane_send.at[block, at],
+                    plane_recv.at[me, at],
+                    block,
+                )
+                for at, target, piece in joint_places()
+            ]
+
+        def own_copies():
+            return [
+                pltpu.make_async_copy(summed.at[me, :, piece], target, plane_own.at[at])
+                for at, target, piece in joint_places()
+            ]
+
+        def up_place(block):
+            return up_half.at[:, pl.ds(pl.multiple_of(block * FEED_COLS, FEED_COLS), FEED_COLS)]
 
         def up_copy(step):
             peer = lax.rem(me + step, GROUP)
-            return to_peer(inputs[7].at[peer], arrived_up.at[me], up_send.at[step], up_recv.at[me], peer)
-
-        def half_copies(pieces):
-            return [
-                to_axis(
-                    own.at[pl.ds(piece * (half // 4), half // 4)],
-                    there.at[pl.ds(pl.multiple_of(seq * half + piece * (half // 4), half // 4), half // 4)],
-                    half_send.at[at, piece],
-                    half_recv.at[at, piece],
-                    "seq",
-                    1 - seq,
-                )
-                for at, (own, there) in enumerate(zip(inputs[8:10], others))
-                for piece in pieces
-            ]
-
-        def half_kept():
-            return [
-                pltpu.make_async_copy(own, there.at[part_rows], half_own.at[at])
-                for at, (own, there) in enumerate(zip(inputs[8:10], others))
-            ]
-
-        def final_pieces(source):
-            pieces = []
-            for number, (which, start, at, width) in enumerate(column_places(source)):
-                piece = arrived_up.at[source] if which else arrived.at[source, :, pl.ds(at, width)]
-                pieces.append((number, piece, outputs[which].at[part_rows, pl.ds(start, width)]))
-            return pieces
-
-        def back_copy(number, piece, target, source):
-            return to_axis(
-                piece,
-                target,
-                back_send.at[source, number],
-                back_recv.at[source, number],
-                "seq",
-                1 - seq,
-            )
-
-        def keep_copy(number, piece, target, source):
-            return pltpu.make_async_copy(piece, target, keep.at[source, number])
-
-        def pass_on(source, which):
-            for number, piece, target in final_pieces(source):
-                if (number == PLACES - 1) == (which == 1):
-                    back_copy(number, piece, target, source).start()
-                    keep_copy(number, piece, target, source).start()
+            return to_peer(up.at[peer], up_place(me), up_send.at[step], up_recv.at[me], peer)
+
+        def own_up():
+            return pltpu.make_async_copy(up.at[me], up_place(me), up_own)
 
         def add(turn):
             for which in range(2):
@@ -1684,12 +1854,17 @@
                 summed[block] = (
                     mine[block, part_rows].astype(jnp.float32) + other[block].astype(jnp.float32)
                 ).astype(jnp.bfloat16)
-
                 if collects:
 
                     @pl.when(block != me)
                     def _(block=block):
-                        plane_copy(block).start()
+                        for copy in plane_copies(block):
+                            copy.start()
+
+                    @pl.when(block == me)
+                    def _(block=block):
+                        for copy in own_copies():
+                            copy.start()
 
         def bias_sums():
             ones = jnp.ones((16, tokens), jnp.bfloat16)
@@ -1720,52 +1895,17 @@
 
                 @pl.when(turn == GROUP - 1)
                 def _():
-                    for copy in half_copies((2, 3)):
+                    for copy in copies((2, 3)):
                         copy.start()
+
+        def last_adds(turn, carry):
+            add(turn)
+            return carry
 
         def late_work(step):
             @pl.when(step == 0)
             def _():
                 lax.fori_loop(PAIRS - 2, PAIRS, last_adds, 0)
-                arrived[me] = summed[me]
-
-            def pass_up(more, carry):
-                number = SIDE * step + more
-                source = lax.rem(me + GROUP - number, GROUP)
-
-                @pl.when(number == 0)
-                def _():
-                    own_up.wait()
-
-                @pl.when(number > 0)
-                def _():
-                    block = arrived_up.at[source]
-                    to_peer(block, block, up_send.at[number], up_recv.at[source], source).wait_recv()
-
-                pass_on(source, 1)
-                return carry
-
-            lax.fori_loop(0, SIDE, pass_up, 0)
-
-        def pass_joint(step, carry):
-            source = lax.rem(me + GROUP - step, GROUP)
-
-            @pl.when(step > 0)
-            def _():
-                to_peer(
-                    summed.at[source],
-                    arrived.at[source],
-                    plane_send.at[source],
-                    plane_recv.at[source],
-                    source,
-                ).wait_recv()
-
-            pass_on(source, 0)
-            return carry
-
-        def last_adds(turn, carry):
-            add(turn)
-            return carry
 
         def send_up(step, carry):
             up_copy(step).start()
@@ -1773,10 +1913,9 @@
 
         wait_all(loads[:3])
         if collects:
-            own_up = pltpu.make_async_copy(inputs[7].at[me], arrived_up.at[me], up_own)
-            own_up.start()
+            own_up().start()
             lax.fori_loop(1, GROUP, send_up, 0)
-            for copy in half_copies((0, 1)) + half_kept():
+            for copy in copies((0, 1)) + kept():
                 copy.start()
         scatter_events(
             partial,
@@ -1785,153 +1924,99 @@
             SCATTER_OPS_EARLY if collects else SCATTER_OPS_WORK,
             scratch,
         )
-        if collects:
-            lax.fori_loop(0, GROUP, pass_joint, 0)
-        else:
-            lax.fori_loop(PAIRS - 2, PAIRS, last_adds, 0)
-        wait_all(loads[3:])
-
-        def norm_back(part, sums):
-            values = hidden[part].astype(jnp.float32)
-            centred = values - jnp.mean(values, axis=1, keepdims=True)
-            spread = jnp.mean(centred * centred, axis=1, keepdims=True)
-            root = lax.rsqrt(spread + EPS)
-            normed = centred * root
-            above = total[part]
-            scaled = above * gain[...]
-            down = jnp.mean(scaled, axis=1, keepdims=True)
-            along = jnp.mean(scaled * normed, axis=1, keepdims=True)
-            passing = grad[part]
-            out[part] = passing + root * (scaled - down - normed * along)
-            low = passing.astype(jnp.bfloat16).astype(jnp.float32)
-
-            def fold(values):
-                return jnp.sum(values.reshape(STRIP // 8, 8, D), axis=0)
-
-            return (sums[0] + fold(above * normed), sums[1] + fold(above), sums[2] + fold(low))
-
-        zeros = jnp.zeros((8, D), jnp.float32)
-        sums = each_strip(rows, norm_back, (zeros, zeros, zeros))
-        for number, folded in enumerate(sums):
-            row = jnp.sum(folded, axis=0, keepdims=True)
-            for block in range(GROUP):
-                shares[block, number : number + 1] = row[:, block * SHARE : (block + 1) * SHARE]
-        def small_copy(step):
-            peer = lax.rem(me + step, GROUP)
-            return to_peer(
-                shares.at[peer], small_land.at[me], small_send.at[step], small_recv.at[me], peer
-            )
-
-        def small_begin(step, carry):
-            small_copy(step).start()
-            return carry
-
-        lax.fori_loop(1, GROUP, small_begin, 0)
-        small_land[me] = shares[me]
-
-        def small_end(step, carry):
-            source = lax.rem(me + GROUP - step, GROUP)
-            to_peer(
-                shares.at[source],
-                small_land.at[source],
-                small_send.at[step],
-                small_recv.at[source],
-                source,
-            ).wait_recv()
-            small_copy(step).wait_send()
-            return carry
-
-        lax.fori_loop(1, GROUP, small_end, 0)
-        small_mine[...] = jnp.sum(small_land[...], axis=0)
-        swap = to_axis(small_mine, small_other, swap_send, swap_recv, "seq", 1 - seq)
-        swap.start()
-        swap.wait()
-        small_out[...] = small_mine[...] + small_other[...]
 
         def end_cross(block, carry):
             cross_copy(block).wait_send()
             return carry
 
+        def end(step, carry):
+            source = lax.rem(me + GROUP - step, GROUP)
+            target = up_place(source)
+            to_peer(target, target, up_send.at[step], up_recv.at[source], source).wait_recv()
+            up_copy(step).wait_send()
+            for at, (_, start, _, width) in enumerate(column_places(source)[:3]):
+                target = joint_half.at[:, pl.ds(start, width)]
+                to_peer(
+                    target, target, plane_send.at[source, at], plane_recv.at[source, at], source
+                ).wait_recv()
+            for copy in plane_copies(lax.rem(me + step, GROUP)):
+                copy.wait_send()
+            return carry
+
+        if collects:
+            out[...] = total[...]
+            lax.fori_loop(1, GROUP, end, 0)
+            wait_all(own_copies() + [own_up()] + copies((0, 1, 2, 3)) + kept())
+        else:
+            lax.fori_loop(PAIRS - 2, PAIRS, last_adds, 0)
+            wait_all(loads[3:])
+
+            def norm_back(part, sums):
+                found = norm_back_strip(hidden, grad, total, gain, out, part)
+                return tuple(before + more for before, more in zip(sums, found))
+
+            zeros = jnp.zeros((8, D), jnp.float32)
+            small_begin(each_strip(rows, norm_back, (zeros, zeros, zeros)))
+            small_middle()
+            small_end()
         lax.fori_loop(0, GROUP, end_cross, 0)
-
-        def end(block, carry):
-            @pl.when(block != me)
-            def _():
-                plane_copy(block).wait_send()
-
-            @pl.when(block > 0)
-            def _():
-                up_copy(block).wait_send()
-
-            for number, piece, target in final_pieces(block):
-                back_copy(number, piece, target, block).wait()
-                keep_copy(number, piece, target, block).wait()
-            return carry
-
-        if collects:
-            lax.fori_loop(0, GROUP, end, 0)
-            wait_all(half_copies((0, 1, 2, 3)) + half_kept())
 
     def part(width, height=half):
         return pltpu.VMEM((GROUP, height, width), jnp.bfloat16)
 
+    def same(*arrays):
+        return [pltpu.VMEM(array.shape, array.dtype) for array in arrays]
+
     small = (SMALL_ROWS, SHARE)
-    sixteen, places = pltpu.SemaphoreType.DMA((GROUP,)), pltpu.SemaphoreType.DMA((GROUP, PLACES))
-    return pl.pallas_call(
-        kernel,
-        out_shape=(
-            jax.ShapeDtypeStruct((rows, D), jnp.float32),
-            jax.ShapeDtypeStruct(small, jnp.float32),
-        )
-        + (
-            (
-                jax.ShapeDtypeStruct((SHARE, 3 * D), jnp.bfloat16),
-                jax.ShapeDtypeStruct((SHARE, FF), jnp.bfloat16),
-            )
-            * 2
-            if collects
-            else (jax.ShapeDtypeStruct((GROUP, half, COLS), jnp.bfloat16),)
-        ),
-        in_specs=[HBM, HBM, VMEM] + [HBM] * (7 if collects else 4),
-        out_specs=(VMEM, VMEM) + ((HBM,) * 4 if collects else (VMEM,)),
-        scratch_shapes=[
-            pltpu.VMEM(array.shape, array.dtype)
-            for array in (hidden, grad, grad_joint, grad_inner, columns)
-        ]
+    shares = (GROUP,) + small
+    sixteen = pltpu.SemaphoreType.DMA((GROUP,))
+    row_shape = jax.ShapeDtypeStruct((rows, D), jnp.float32)
+    common = (
+        same(grad_joint, grad_inner, columns)
         + [
             pltpu.SemaphoreType.DMA((5,)),
             pltpu.VMEM((2, GROUP, rows, 2 * SHARE), jnp.bfloat16),
             pltpu.SemaphoreType.DMA((2,)),
-            pltpu.VMEM((GROUP,) + small, jnp.float32),
-            pltpu.VMEM((GROUP,) + small, jnp.float32),
-            pltpu.VMEM(small, jnp.float32),
-            pltpu.VMEM(small, jnp.float32),
-            sixteen,
-            sixteen,
-            pltpu.SemaphoreType.DMA,
-            pltpu.SemaphoreType.DMA,
             part(made, SHARE),
             part(made),
             sixteen,
             sixteen,
         ]
-        + (
-            [part(JOINT_COLS)] * 2
-            + [part(FEED_COLS)]
-            + [sixteen] * 2
-            + [places] * 3
-            + [sixteen] * 2
-            + [pltpu.SemaphoreType.DMA]
-            + [pltpu.SemaphoreType.DMA((2, 4))] * 2
-            + [pltpu.SemaphoreType.DMA((2,))]
-            if collects
-            else []
-        )
-        + scatter_scratch(rows),
+    )
+    if collects:
+        out_shape = (row_shape, jax.ShapeDtypeStruct(shares, jnp.float32)) + HALVES + WHOLES
+        out_specs = (VMEM, VMEM) + (HBM,) * 4
+        operands = (grad_joint, grad_inner, columns, every, up, *halves)
+        in_specs = [HBM] * 7
+        special = [
+            part(JOINT_COLS),
+            pltpu.SemaphoreType.DMA((GROUP, 3)),
+            pltpu.SemaphoreType.DMA((GROUP, 3)),
+            pltpu.SemaphoreType.DMA((3,)),
+            sixteen,
+            sixteen,
+            pltpu.SemaphoreType.DMA,
+        ] + half_sems()
+    else:
+        out_shape = (
+            row_shape,
+            jax.ShapeDtypeStruct(small, jnp.float32),
+            jax.ShapeDtypeStruct((GROUP, half, COLS), jnp.bfloat16),
+        )
+        out_specs = (VMEM,) * 3
+        operands = (grad_joint, grad_inner, columns, every, hidden, grad, gain)
+        in_specs = [HBM] * 6 + [VMEM]
+        special = same(hidden, grad) + [pltpu.VMEM(shares, jnp.float32)] + small_scratch()
+    return pl.pallas_call(
+        kernel,
+        out_shape=out_shape,
+        in_specs=in_specs,
+        out_specs=out_specs,
+        scratch_shapes=common + special + scatter_scratch(rows),
         compiler_params=pltpu.CompilerParams(
             collective_id=20 + layer, has_side_effects=True, vmem_limit_bytes=ROOM
         ),
-    )(hidden, grad, gain, grad_joint, grad_inner, columns, every, *((up, *halves) if collects else ()))
+    )(*operands)
 
 
 def mask_rest(rows, begin, spot, first, lead):
@@ -2473,9 +2558,6 @@
         )
         own_branches.insert(0, branch)
         other_branches = list(other) + other_branches
-        if layer == 0:
-            hidden, other = forward_scatter(*branches, (branch,))
-            other_branches.insert(0, other)
         grad_joint, *rest = attend_plane_back(
             query,
             key,
@@ -2490,7 +2572,8 @@
             every,
             grad_inner,
         )
-        grad_hidden, small, *grads = backward_scatter(
+        grad_above = grad_hidden
+        out = backward_scatter(
             before,
             grad_hidden,
             gains[layer],
@@ -2499,15 +2582,22 @@
             columns.reshape(D, COLS),
             every,
             layer,
-            rest[2] if rest else None,
-            rest[:2],
+            *((rest[2], rest[:2]) if rest else ()),
+        )
+        if layer > 0:
+            grad_hidden, small, summed = out
+            small_grads.insert(0, small)
+            continue
+        total, shares, joint, upper, *wholes = out
+        joint_grads.append(wholes[0])
+        upper_grads.append(wholes[1])
+        hidden, grad_hidden, small, joint, upper, other = forward_scatter(
+            *branches, (total, before, grad_above, gains[layer], shares, joint, upper, branch)
         )
         small_grads.insert(0, small)
-        if layer > 0:
-            summed = grads[0]
-        else:
-            joint_grads.extend(grads[0::2])
-            upper_grads.extend(grads[1::2])
+        joint_grads.insert(0, joint)
+        upper_grads.insert(0, upper)
+        other_branches.insert(0, other)
     here, there = jnp.stack(own_branches), jnp.stack(other_branches)
     result = hidden.astype(jnp.bfloat16)[None]
 

time: 1060 us -> 1100 us (1.038)
  Pallas kernels: 1000 us -> 1050 us
    pallas_call x4, Pallas kernels: 434 us -> 479 us  [the longest x2 250 us: forward_scatter(): pl.pallas_call(kernel, out_shape=out_shape, in_specs=[HBM, VMEM] + [HBM]...]
where the time goes in v5:
time: 1100 us
  Pallas kernels  1050 us (95%)
  other arithmetic  36.7 us (3%)
    pallas_call x2, Pallas kernels, forward_scatter(): pl.pallas_call(kernel, out_shape=out_shape, in_specs=[HBM, VMEM] + [HBM]...  250 us
    pallas_call x2, Pallas kernels, backward_scatter(): pl.pallas_call(kernel, out_shape=out_shape, in_specs=in_specs, out_specs=...  229 us
    pallas_call x2, Pallas kernels, backward_gather(): pl.pallas_call(kernel, out_shape=(jax.ShapeDtypeStruct((GROUP, rows, HEAD...  191 us
    pallas_call x1, Pallas kernels, first_gather(): pl.pallas_call(kernel, out_shape=[jax.ShapeDtypeStruct((GROUP, rows, D),...  144 us
    pallas_call x1, Pallas kernels, forward_gather(): pl.pallas_call(kernel, out_shape=[jax.ShapeDtypeStruct((GROUP, rows, D),...  98.8 us
    pallas_call x2, Pallas kernels, attend_plane_back(): pl.pallas_call(kernel, grid=(SIDE,), out_shape=(jax.ShapeDtypeStruct((SID...  68.1 us
    pallas_call x2, Pallas kernels, attend_plane(): pl.pallas_call(kernel, grid=(SIDE,), out_shape=(shape(rows, HEAD_COLS, jn...  65.4 us
  transfers between devices with their start and end apart: 1, of which 0 were waited for; matrix products, arithmetic and copies ran while one was open for 0% of the time, Pallas kernels for 9%

profile of v5, /device:TPU:0, one launch (start us, length us, event | category | flops | bytes accessed | tf_op | source)
XLA Modules:
  0.0 1096.9 jit_solution(6181473590001004636)
XLA Ops:
  2.1 1.3 fusion.2
  10.3 144.0 %shard_map.238 = (bf16[16,256,2048]{2,1,0:T(8,128)(2,1)}, bf16[16,128,896]{2,1,0:T(8,128)(2,1)}, bf16[16,256,128]{2,1,0:T(8,128)(2,1)}, bf16[16,256,128]{2,1,0:T...) custom-call(bf16[256,2048]{1,0:T(8,128)(2,1)} %bitcast.108, ...), custom_call_target="tpu_custom_call" | custom-call | tf_op jit(solution)/shard_map/pallas_call | solution.py:1105
  157.6 1.5 iota_select_fusion.spot
  159.1 46.1 %shard_map.239 = (bf16[4,4,256,128]{3,2,1,0:T(8,128)(2,1)}, f32[4,4,128,256]{3,2,1,0:T(8,128)}, f32[4,4,1024]{2,1,0:T(4,128)}, bf16[16,64,896]{2,1,0:T(8,128)(2,1)}) custom-call(bf16[4,4,256,128]{3,2,1,0:T(8,128)(2,1)} %bitcast.111, bf16[4,4,256,128]{3,2,1,0:T(8,128)(2,1)} %bitcast.113, bf16[4,4,256,128]{3,2,1,0:T(8,128)(2,1)} %bitcast.115, ...), custom_call_target="tpu_custom_call" | custom-call | tf_op jit(solution)/shard_map/pallas_call | solution.py:2268
  205.2 1.6 collective-permute-start
  207.7 1.8 slice_bitcast_fusion
  209.5 93.9 %shard_map.240.hidden.refs_4_ = f32[256,2048]{1,0:T(8,128)} custom-call(bf16[256,2048]{1,0:T(8,128)(2,1)} %bitcast.109, f32[1,2048]{1,0:T(1,128)} %get-tuple-element.120.bias, bf16[16,256,128]{2,1,0:T(8,128)(2,1)} %bitcast.117, bf16[16,256,512]{2,1,0:T(8,128)(2,1)} %get-tuple-element.67.active, bf16[2,128,2048]{2,1,0:T(8,128)(2,1)} %out_weight.7, ...), custom_call_target="tpu_custom_call" | custom-call | tf_op jit(solution)/shard_map/pallas_call | solution.py:1705
  304.0 1.9 convert_multiply_fusion
  307.2 98.8 %shard_map.241 = (bf16[16,256,2048]{2,1,0:T(8,128)(2,1)}, bf16[16,128,896]{2,1,0:T(8,128)(2,1)}, bf16[16,256,128]{2,1,0:T(8,128)(2,1)}, bf16[16,256,128]{2,1,0:T...) custom-call(f32[256,2048]{1,0:T(8,128)} %shard_map.240.hidden.refs_4_, ...), custom_call_target="tpu_custom_call" | custom-call | tf_op jit(solution)/shard_map/pallas_call | solution.py:900
  405.9 19.3 %shard_map.242 = (bf16[4,4,256,128]{3,2,1,0:T(8,128)(2,1)}, f32[4,4,128,256]{3,2,1,0:T(8,128)}, f32[4,4,1024]{2,1,0:T(4,128)}) custom-call(bf16[4,4,256,128]{3,2,1,0:T(8,128)(2,1)} %bitcast.121, bf16[4,4,256,128]{3,2,1,0:T(8,128)(2,1)} %bitcast.123, bf16[4,4,256,128]{3,2,1,0:T(8,128)(2,1)} %bitcast.125, s32[4,1,1024]{2,1,0:T(1,128)} %convert_element_type.171.begin, ...), custom_call_target="tpu_custom_call" | custom-call | tf_op jit(solution)/shard_map/pallas_call | solution.py:2268
  425.3 96.8 %shard_map.243 = (f32[16,256,128]{2,1,0:T(8,128)}, bf16[16,256,512]{2,1,0:T(8,128)(2,1)}, bf16[640,2048]{1,0:T(8,128)(2,1)}) custom-call(bf16[256,2048]{1,0:T(8,128)(2,1)} %get-tuple-element.115.own, bf16[2,128,2048]{2,1,0:T(8,128)(2,1)} %out_weight.7, bf16[2,512,2048]{2,1,0:T(8,128)(2,1)} %down_weight.7, f32[16,256,512]{2,1,0:T(8,128)} %get-tuple-element.76.inner, ...), custom_call_target="tpu_custom_call" | custom-call | tf_op jit(solution)/shard_map/pallas_call | solution.py:1218
  522.1 21.6 %shard_map.244 = bf16[4,4,256,384]{3,2,1,0:T(8,128)(2,1)} custom-call(bf16[4,4,256,128]{3,2,1,0:T(8,128)(2,1)} %bitcast.122, bf16[4,4,256,128]{3,2,1,0:T(8,128)(2,1)} %bitcast.124, bf16[4,4,256,128]{3,2,1,0:T(8,128)(2,1)} %bitcast.126, f32[4,4,256,128]{3,2,1,0:T(8,128)} %bitcast.131, f32[4,4,256,128]{3,2,1,0:T(8,128)} %bitcast.99, ...), custom_call_target="tpu_custom_call" | custom-call | tf_op jit(solution)/shard_map/pallas_call | solution.py:2389
  543.7 107.5 %shard_map.245 = (f32[256,2048]{1,0:T(8,128)}, f32[16,128]{1,0:T(8,128)}, bf16[16,64,896]{2,1,0:T(8,128)(2,1)}) custom-call(bf16[16,256,384]{2,1,0:T(8,128)(2,1)} %bitcast.103, bf16[16,256,512]{2,1,0:T(8,128)(2,1)} %get-tuple-element.80.refs_1_, bf16[2048,896]{1,0:T(8,128)(2,1)} %bitcast.127, bf16[16,256,2048]{2,1,0:T(8,128)(2,1)} %get-tuple-element.82.refs_3_, ...), custom_call_target="tpu_custom_call" | custom-call | tf_op jit(solution)/shard_map/pallas_call | solution.py:2010
  651.2 2.7 convert_element_type.176.own
  653.9 94.6 %shard_map.246 = (f32[16,256,128]{2,1,0:T(8,128)}, bf16[16,256,512]{2,1,0:T(8,128)(2,1)}, bf16[640,2048]{1,0:T(8,128)(2,1)}, bf16[640,2048]{1,0:T(8,128)(2,1)}) custom-call(bf16[256,2048]{1,0:T(8,128)(2,1)} %convert_element_type.176.own, bf16[2,128,2048]{2,1,0:T(8,128)(2,1)} %out_weight.7, bf16[2,512,2048]{2,1,0:T(8,128)(2,1)} %down_weight.7, ...), custom_call_target="tpu_custom_call" | custom-call | tf_op jit(solution)/shard_map/pallas_call | solution.py:1218
  748.5 46.5 %shard_map.247 = (bf16[4,4,256,384]{3,2,1,0:T(8,128)(2,1)}, bf16[64,6144]{1,0:T(8,128)(2,1)}, bf16[64,8192]{1,0:T(8,128)(2,1)}, bf16[16,64,512]{2,1,0:T(8,128)(2,1)}) custom-call(bf16[4,4,256,128]{3,2,1,0:T(8,128)(2,1)} %bitcast.112, bf16[4,4,256,128]{3,2,1,0:T(8,128)(2,1)} %bitcast.114, bf16[4,4,256,128]{3,2,1,0:T(8,128)(2,1)} %bitcast.116, ...), custom_call_target="tpu_custom_call" | custom-call | tf_op jit(solution)/shard_map/pallas_call | solution.py:2389
  795.1 121.2 %shard_map.248 = (f32[256,2048]{1,0:T(8,128)}, f32[16,16,128]{2,1,0:T(8,128)}, bf16[64,6144]{1,0:T(8,128)(2,1)}, bf16[64,8192]{1,0:T(8,128)(2,1)}, bf16[128,6144]{1,0:T(8,128)(2,1)}, /*index=5*/bf16[128,8192]{1,0:T(8,128)(2,1)}) custom-call(bf16[16,256,384]{2,1,0:T(8,128)(2,1)} %bitcast.129, bf16[16,256,512]{2,1,0:T(8,128)(2,1)} %get-tuple-element.91.refs_2_.refs_1_, ...), custom_call_target="tpu_custom_call" | custom-call | tf_op jit(solution)/shard_map/pallas_call | solution.py:2010
  916.2 156.3 %shard_map.249 = (f32[256,2048]{1,0:T(8,128)}, f32[256,2048]{1,0:T(8,128)}, f32[16,128]{1,0:T(8,128)}, bf16[128,6144]{1,0:T(8,128)(2,1)}, bf16[128,8192]{1,0:T(8,128)(2,1)}, /*index=5*/bf16[640,2048]{1,0:T(8,128)(2,1)}) custom-call(f32[256,2048]{1,0:T(8,128)} %shard_map.240.hidden.refs_4_, f32[1,2048]{1,0:T(1,128)} %get-tuple-element.119.bias, ...), custom_call_target="tpu_custom_call" | custom-call | tf_op jit(solution)/shard_map/pallas_call | solution.py:1705
  1072.5 1.4 pad_maximum_fusion.4
  1075.3 3.2 convert_add_fusion.1
  1079.8 4.2 convert_add_fusion
  1086.3 3.5 maximum_convert_fusion.1
  1090.6 3.9 maximum_convert_fusion
  1095.1 1.3 copy.57
  (65 shorter events, 20.6 us)
Async XLA Ops:
  205.2 100.7 %collective-permute-start = (bf16[16,64,896]{2,1,0:T(8,128)(2,1)}, bf16[16,64,896]{2,1,0:T(8,128)(2,1)S(1)}, u32[]{:S(2)}, u32[]{:S(2)}) collective-permute-start(bf16[16,64,896]{2,1,0:T(8,128)(2,1)} %get-tuple-element.70.own_half), channel_id=1, source_target_pairs={{0,16},{16,0},{1,17},{17,1},{2,18},{18,2},{3,19},{19,3},{4,20},{20... | collective-permute-start | bytes 5505032 | tf_op jit(solution)/shard_map/ppermute | solution.py:2482
  209.5 94.5 %copy-start.11 = (bf16[1,256,2048]{2,1,0:T(8,128)(2,1)S(1)}, bf16[1,256,2048]{2,1,0:T(8,128)(2,1)}, u32[]{:S(2)}) copy-start(bf16[1,256,2048]{2,1,0:T(8,128)(2,1)} %param.28) | copy-start | bytes 3145732
  306.0 1.2 copy-start.8
  916.2 156.3 %copy-start.12 = (f32[16,128]{1,0:T(8,128)S(1)}, f32[16,128]{1,0:T(8,128)}, u32[]{:S(2)}) copy-start(f32[16,128]{1,0:T(8,128)} %get-tuple-element.105) | copy-start | bytes 24580
  916.2 159.0 %copy-start = (bf16[640,2048]{1,0:T(8,128)(2,1)S(1)}, bf16[640,2048]{1,0:T(8,128)(2,1)}, u32[]{:S(2)}) copy-start(bf16[640,2048]{1,0:T(8,128)(2,1)} %get-tuple-element.101.refs_7_) | copy-start | bytes 7864324
  1073.9 20.6 %copy-start.13 = (f32[2,1,128]{2,1,0:T(1,128)}, f32[2,1,128]{2,1,0:T(1,128)S(1)}, u32[]{:S(2)}) copy-start(f32[2,1,128]{2,1,0:T(1,128)S(1)} %get-tuple-element.121) | copy-start | bytes 3076
  1075.3 3.2 copy-start.1
  1075.3 3.3 copy-start.2
  1075.3 4.5 copy-start.3
  1079.8 4.2 copy-start.4
  1084.0 2.3 copy-start.9
  1084.0 2.3 copy-start.10
  1086.3 3.5 copy-start.6
  1086.3 4.3 copy-start.7
  1090.6 4.5 copy-start.5

commit v6 on v5

--- a/solution.py
+++ b/solution.py
@@ -774,6 +774,25 @@
     return to_axis(source, target, sems.at[0], sems.at[1], "seq", 1 - lax.axis_index("seq"))
 
 
+def row_swap(source, target, sems, first, blocks):
+    size = source.shape[0] // SWAP_BLOCKS
+    return [
+        to_axis(
+            source.at[pl.ds(block * size, size)],
+            target.at[pl.ds((block - first) * size, size)],
+            sems.at[0, block],
+            sems.at[1, block],
+            "seq",
+            1 - lax.axis_index("seq"),
+        )
+        for block in blocks
+    ]
+
+
+SWAP_BLOCKS = 4
+SWAP_FIRST = SWAP_BLOCKS // 2
+
+
 def load_all(pairs, sems):
     copies = [
         pltpu.make_async_copy(source, target, sems.at[number])
@@ -1634,7 +1653,12 @@
             )
             copies, kept = half_swaps((joint, upper), (joint_out, upper_out), swap_sems)
             greet_plane(GROUP)
-            for copy in copies((0, 1, 2, 3)) + kept():
+            blocks = tuple(range(SWAP_FIRST, SWAP_BLOCKS))
+            early, late = (
+                row_swap(branch, branch_out, swap_sem, SWAP_FIRST, which)
+                for which in (blocks[:-1], blocks[-1:])
+            )
+            for copy in copies((0, 1, 2, 3)) + kept() + early:
                 copy.start()
             sums[...] = jnp.zeros_like(sums)
             strips = rows // STRIP
@@ -1658,7 +1682,8 @@
                 @pl.when(turn == GROUP - 4)
                 def _():
                     small_middle()
-                    plane_swap((branch, branch_out), swap_sem).start()
+                    for copy in late:
+                        copy.start()
 
         else:
             greet_neighbours()
@@ -1675,8 +1700,7 @@
         out[...] = hidden_part[...].astype(jnp.float32) + (scratch[0][...] + bias[...])
         if last:
             small_end()
-            wait_all(copies((0, 1, 2, 3)) + kept())
-            plane_swap((branch, branch_out), swap_sem).wait()
+            wait_all(copies((0, 1, 2, 3)) + kept() + early + late)
 
     out_shape = (jax.ShapeDtypeStruct((rows, D), jnp.float32),)
     out_specs = (VMEM,)
@@ -1689,7 +1713,7 @@
                 jax.ShapeDtypeStruct((SMALL_ROWS, SHARE), jnp.float32),
             )
             + WHOLES
-            + (jax.ShapeDtypeStruct(branch.shape, branch.dtype),)
+            + (jax.ShapeDtypeStruct((BACK_COLS // 2, D), branch.dtype),)
         )
         out_specs += (VMEM, VMEM, HBM, HBM, HBM)
         extra_scratch = (
@@ -1697,7 +1721,7 @@
             + [
                 pltpu.SemaphoreType.DMA((4,)),
                 pltpu.VMEM((3, 8, D), jnp.float32),
-                pltpu.SemaphoreType.DMA((2,)),
+                pltpu.SemaphoreType.DMA((2, SWAP_BLOCKS)),
             ]
             + small_scratch()
             + half_sems()
@@ -1722,7 +1746,7 @@
 
 
 def backward_scatter(
-    hidden, grad, gain, grad_joint, grad_inner, columns, every, layer, up=None, halves=()
+    hidden, grad, gain, grad_joint, grad_inner, columns, every, layer, up=None, halves=(), branch=None
 ):
     rows = grad.shape[0]
     half = SHARE // 2
@@ -1733,8 +1757,8 @@
     def kernel(*refs):
         if collects:
             (joint_in, inner_in, columns_in, every, up, *halves), refs = refs[:7], refs[7:]
-            out, shares, joint_half, up_half, *wholes = refs[:6]
-            refs = refs[6:]
+            branch, out, shares, joint_half, up_half, *wholes = refs[:7]
+            branch_out, refs = refs[7], refs[8:]
         else:
             (joint_in, inner_in, columns_in, every, hidden_in, grad_in, gain), refs = refs[:7], refs[7:]
             out, small_out, summed, refs = refs[0], refs[1], refs[2], refs[3:]
@@ -1743,8 +1767,9 @@
         refs = refs[10:]
         if collects:
             summed, plane_send, plane_recv, plane_own, up_send, up_recv, up_own = refs[:7]
-            swap_sems, refs = refs[7:10], refs[10:]
+            swap_sems, branch_sem, refs = refs[7:10], refs[10], refs[11:]
             copies, kept = half_swaps(halves, wholes, swap_sems)
+            swaps = row_swap(branch, branch_out, branch_sem, 0, range(SWAP_FIRST))
         else:
             hidden, grad, shares, small, refs = refs[0], refs[1], refs[2], refs[3:10], refs[10:]
             small_begin, small_middle, small_end = small_exchange(
@@ -1895,7 +1920,7 @@
 
                 @pl.when(turn == GROUP - 1)
                 def _():
-                    for copy in copies((2, 3)):
+                    for copy in copies((2, 3)) + swaps:
                         copy.start()
 
         def last_adds(turn, carry):
@@ -1946,7 +1971,7 @@
         if collects:
             out[...] = total[...]
             lax.fori_loop(1, GROUP, end, 0)
-            wait_all(own_copies() + [own_up()] + copies((0, 1, 2, 3)) + kept())
+            wait_all(own_copies() + [own_up()] + copies((0, 1, 2, 3)) + kept() + swaps)
         else:
             lax.fori_loop(PAIRS - 2, PAIRS, last_adds, 0)
             wait_all(loads[3:])
@@ -1985,9 +2010,10 @@
     )
     if collects:
         out_shape = (row_shape, jax.ShapeDtypeStruct(shares, jnp.float32)) + HALVES + WHOLES
-        out_specs = (VMEM, VMEM) + (HBM,) * 4
-        operands = (grad_joint, grad_inner, columns, every, up, *halves)
-        in_specs = [HBM] * 7
+        out_shape += (jax.ShapeDtypeStruct((BACK_COLS // 2, D), branch.dtype),)
+        out_specs = (VMEM, VMEM) + (HBM,) * 5
+        operands = (grad_joint, grad_inner, columns, every, up, *halves, branch)
+        in_specs = [HBM] * 8
         special = [
             part(JOINT_COLS),
             pltpu.SemaphoreType.DMA((GROUP, 3)),
@@ -1996,7 +2022,7 @@
             sixteen,
             sixteen,
             pltpu.SemaphoreType.DMA,
-        ] + half_sems()
+        ] + half_sems() + [pltpu.SemaphoreType.DMA((2, SWAP_BLOCKS))]
     else:
         out_shape = (
             row_shape,
@@ -2582,13 +2608,13 @@
             columns.reshape(D, COLS),
             every,
             layer,
-            *((rest[2], rest[:2]) if rest else ()),
+            *((rest[2], rest[:2], branch) if rest else ()),
         )
         if layer > 0:
             grad_hidden, small, summed = out
             small_grads.insert(0, small)
             continue
-        total, shares, joint, upper, *wholes = out
+        total, shares, joint, upper, *wholes, first = out
         joint_grads.append(wholes[0])
         upper_grads.append(wholes[1])
         hidden, grad_hidden, small, joint, upper, other = forward_scatter(
@@ -2597,7 +2623,7 @@
         small_grads.insert(0, small)
         joint_grads.insert(0, joint)
         upper_grads.insert(0, upper)
-        other_branches.insert(0, other)
+        other_branches.insert(0, jnp.concatenate([first, other], axis=0))
     here, there = jnp.stack(own_branches), jnp.stack(other_branches)
     result = hidden.astype(jnp.bfloat16)[None]
 

time: 1100 us -> 1060 us (0.964)
  Pallas kernels: 1050 us -> 1000 us
    pallas_call x2, Pallas kernels: 250 us -> 208 us  [forward_scatter(): pl.pallas_call(kernel, out_shape=out_shape, in_specs=[HBM, VMEM] + [HBM]...]
where the time goes in v6:
time: 1060 us; the launch traced here: 1050 us
  Pallas kernels  1000 us (94%)
  other arithmetic  36.9 us (3%)
  local copies, waits for them, and re-layouts  10.6 us (1%)
    pallas_call x2, Pallas kernels, backward_scatter(): pl.pallas_call(kernel, out_shape=out_shape, in_specs=in_specs, out_specs=...  229 us
    pallas_call x2, Pallas kernels, forward_scatter(): pl.pallas_call(kernel, out_shape=out_shape, in_specs=[HBM, VMEM] + [HBM]...  208 us
    pallas_call x2, Pallas kernels, backward_gather(): pl.pallas_call(kernel, out_shape=(jax.ShapeDtypeStruct((GROUP, rows, HEAD...  190 us
    pallas_call x1, Pallas kernels, first_gather(): pl.pallas_call(kernel, out_shape=[jax.ShapeDtypeStruct((GROUP, rows, D),...  144 us
    pallas_call x1, Pallas kernels, forward_gather(): pl.pallas_call(kernel, out_shape=[jax.ShapeDtypeStruct((GROUP, rows, D),...  98.8 us
    pallas_call x2, Pallas kernels, attend_plane_back(): pl.pallas_call(kernel, grid=(SIDE,), out_shape=(jax.ShapeDtypeStruct((SID...  68.2 us
    pallas_call x2, Pallas kernels, attend_plane(): pl.pallas_call(kernel, grid=(SIDE,), out_shape=(shape(rows, HEAD_COLS, jn...  65.5 us
  transfers between devices with their start and end apart: 1, of which 0 were waited for; matrix products, arithmetic and copies ran while one was open for 0% of the time, Pallas kernels for 9%

profile of v6, /device:TPU:0, one launch (start us, length us, event | category | flops | bytes accessed | tf_op | source)
XLA Modules:
  0.0 1054.5 jit_solution(4879725112663410364)
XLA Ops:
  2.1 1.3 fusion.2
  10.3 144.0 %shard_map.238 = (bf16[16,256,2048]{2,1,0:T(8,128)(2,1)}, bf16[16,128,896]{2,1,0:T(8,128)(2,1)}, bf16[16,256,128]{2,1,0:T(8,128)(2,1)}, bf16[16,256,128]{2,1,0:T...) custom-call(bf16[256,2048]{1,0:T(8,128)(2,1)} %bitcast.107, ...), custom_call_target="tpu_custom_call" | custom-call | tf_op jit(solution)/shard_map/pallas_call | solution.py:1124
  157.6 1.5 iota_select_fusion.spot
  159.1 46.2 %shard_map.239 = (bf16[4,4,256,128]{3,2,1,0:T(8,128)(2,1)}, f32[4,4,128,256]{3,2,1,0:T(8,128)}, f32[4,4,1024]{2,1,0:T(4,128)}, bf16[16,64,896]{2,1,0:T(8,128)(2,1)}) custom-call(bf16[4,4,256,128]{3,2,1,0:T(8,128)(2,1)} %bitcast.110, bf16[4,4,256,128]{3,2,1,0:T(8,128)(2,1)} %bitcast.112, bf16[4,4,256,128]{3,2,1,0:T(8,128)(2,1)} %bitcast.114, ...), custom_call_target="tpu_custom_call" | custom-call | tf_op jit(solution)/shard_map/pallas_call | solution.py:2294
  205.3 1.5 collective-permute-start
  207.7 1.7 slice_bitcast_fusion
  209.4 94.0 %shard_map.240.hidden.refs_4_ = f32[256,2048]{1,0:T(8,128)} custom-call(bf16[256,2048]{1,0:T(8,128)(2,1)} %bitcast.108, f32[1,2048]{1,0:T(1,128)} %get-tuple-element.122.bias, bf16[16,256,128]{2,1,0:T(8,128)(2,1)} %bitcast.116, bf16[16,256,512]{2,1,0:T(8,128)(2,1)} %get-tuple-element.68.active, bf16[2,128,2048]{2,1,0:T(8,128)(2,1)} %out_weight.7, ...), custom_call_target="tpu_custom_call" | custom-call | tf_op jit(solution)/shard_map/pallas_call | solution.py:1729
  304.0 1.9 convert_multiply_fusion
  307.2 98.8 %shard_map.241 = (bf16[16,256,2048]{2,1,0:T(8,128)(2,1)}, bf16[16,128,896]{2,1,0:T(8,128)(2,1)}, bf16[16,256,128]{2,1,0:T(8,128)(2,1)}, bf16[16,256,128]{2,1,0:T...) custom-call(f32[256,2048]{1,0:T(8,128)} %shard_map.240.hidden.refs_4_, ...), custom_call_target="tpu_custom_call" | custom-call | tf_op jit(solution)/shard_map/pallas_call | solution.py:919
  406.0 19.3 %shard_map.242 = (bf16[4,4,256,128]{3,2,1,0:T(8,128)(2,1)}, f32[4,4,128,256]{3,2,1,0:T(8,128)}, f32[4,4,1024]{2,1,0:T(4,128)}) custom-call(bf16[4,4,256,128]{3,2,1,0:T(8,128)(2,1)} %bitcast.120, bf16[4,4,256,128]{3,2,1,0:T(8,128)(2,1)} %bitcast.122, bf16[4,4,256,128]{3,2,1,0:T(8,128)(2,1)} %bitcast.124, s32[4,1,1024]{2,1,0:T(1,128)} %convert_element_type.171.begin, ...), custom_call_target="tpu_custom_call" | custom-call | tf_op jit(solution)/shard_map/pallas_call | solution.py:2294
  425.3 95.9 %shard_map.243 = (f32[16,256,128]{2,1,0:T(8,128)}, bf16[16,256,512]{2,1,0:T(8,128)(2,1)}, bf16[640,2048]{1,0:T(8,128)(2,1)}) custom-call(bf16[256,2048]{1,0:T(8,128)(2,1)} %get-tuple-element.117.own, bf16[2,128,2048]{2,1,0:T(8,128)(2,1)} %out_weight.7, bf16[2,512,2048]{2,1,0:T(8,128)(2,1)} %down_weight.7, f32[16,256,512]{2,1,0:T(8,128)} %get-tuple-element.77.inner, ...), custom_call_target="tpu_custom_call" | custom-call | tf_op jit(solution)/shard_map/pallas_call | solution.py:1237
  521.3 21.6 %shard_map.244 = bf16[4,4,256,384]{3,2,1,0:T(8,128)(2,1)} custom-call(bf16[4,4,256,128]{3,2,1,0:T(8,128)(2,1)} %bitcast.121, bf16[4,4,256,128]{3,2,1,0:T(8,128)(2,1)} %bitcast.123, bf16[4,4,256,128]{3,2,1,0:T(8,128)(2,1)} %bitcast.125, f32[4,4,256,128]{3,2,1,0:T(8,128)} %bitcast.130, f32[4,4,256,128]{3,2,1,0:T(8,128)} %bitcast.100, ...), custom_call_target="tpu_custom_call" | custom-call | tf_op jit(solution)/shard_map/pallas_call | solution.py:2415
  542.9 107.5 %shard_map.245 = (f32[256,2048]{1,0:T(8,128)}, f32[16,128]{1,0:T(8,128)}, bf16[16,64,896]{2,1,0:T(8,128)(2,1)}) custom-call(bf16[16,256,384]{2,1,0:T(8,128)(2,1)} %bitcast.104, bf16[16,256,512]{2,1,0:T(8,128)(2,1)} %get-tuple-element.81.refs_1_, bf16[2048,896]{1,0:T(8,128)(2,1)} %bitcast.126, bf16[16,256,2048]{2,1,0:T(8,128)(2,1)} %get-tuple-element.83.refs_3_, ...), custom_call_target="tpu_custom_call" | custom-call | tf_op jit(solution)/shard_map/pallas_call | solution.py:2036
  650.4 2.7 convert_element_type.176.own
  653.1 94.6 %shard_map.246 = (f32[16,256,128]{2,1,0:T(8,128)}, bf16[16,256,512]{2,1,0:T(8,128)(2,1)}, bf16[640,2048]{1,0:T(8,128)(2,1)}, bf16[640,2048]{1,0:T(8,128)(2,1)}) custom-call(bf16[256,2048]{1,0:T(8,128)(2,1)} %convert_element_type.176.own, bf16[2,128,2048]{2,1,0:T(8,128)(2,1)} %out_weight.7, bf16[2,512,2048]{2,1,0:T(8,128)(2,1)} %down_weight.7, ...), custom_call_target="tpu_custom_call" | custom-call | tf_op jit(solution)/shard_map/pallas_call | solution.py:1237
  747.7 46.6 %shard_map.247 = (bf16[4,4,256,384]{3,2,1,0:T(8,128)(2,1)}, bf16[64,6144]{1,0:T(8,128)(2,1)}, bf16[64,8192]{1,0:T(8,128)(2,1)}, bf16[16,64,512]{2,1,0:T(8,128)(2,1)}) custom-call(bf16[4,4,256,128]{3,2,1,0:T(8,128)(2,1)} %bitcast.111, bf16[4,4,256,128]{3,2,1,0:T(8,128)(2,1)} %bitcast.113, bf16[4,4,256,128]{3,2,1,0:T(8,128)(2,1)} %bitcast.115, ...), custom_call_target="tpu_custom_call" | custom-call | tf_op jit(solution)/shard_map/pallas_call | solution.py:2415
  794.3 121.3 %shard_map.248 = (f32[256,2048]{1,0:T(8,128)}, f32[16,16,128]{2,1,0:T(8,128)}, bf16[64,6144]{1,0:T(8,128)(2,1)}, bf16[64,8192]{1,0:T(8,128)(2,1)}, bf16[128,6144...) custom-call(bf16[16,256,384]{2,1,0:T(8,128)(2,1)} %bitcast.128, ...), custom_call_target="tpu_custom_call" | custom-call | tf_op jit(solution)/shard_map/pallas_call | solution.py:2036
  915.7 114.3 %shard_map.249 = (f32[256,2048]{1,0:T(8,128)}, f32[256,2048]{1,0:T(8,128)}, f32[16,128]{1,0:T(8,128)}, bf16[128,6144]{1,0:T(8,128)(2,1)}, bf16[128,8192]{1,0:T(8,128)(2,1)}, /*index=5*/bf16[320,2048]{1,0:T(8,128)(2,1)}) custom-call(f32[256,2048]{1,0:T(8,128)} %shard_map.240.hidden.refs_4_, f32[1,2048]{1,0:T(1,128)} %get-tuple-element.121.bias, ...), custom_call_target="tpu_custom_call" | custom-call | tf_op jit(solution)/shard_map/pallas_call | solution.py:1729
  1030.0 1.3 pad_maximum_fusion.4
  1032.7 1.8 maximum_bitcast_fusion
  1035.7 1.7 convert_add_fusion.1
  1037.4 4.2 convert_add_fusion
  1043.9 3.5 maximum_convert_fusion.1
  1048.2 3.9 maximum_convert_fusion
  (66 shorter events, 21.7 us)
Async XLA Ops:
  205.3 100.6 %collective-permute-start = (bf16[16,64,896]{2,1,0:T(8,128)(2,1)}, bf16[16,64,896]{2,1,0:T(8,128)(2,1)S(1)}, u32[]{:S(2)}, u32[]{:S(2)}) collective-permute-start(bf16[16,64,896]{2,1,0:T(8,128)(2,1)} %get-tuple-element.71.own_half), channel_id=1, source_target_pairs={{0,16},{16,0},{1,17},{17,1},{2,18},{18,2},{3,19},{19,3},{4,20},{20... | collective-permute-start | bytes 5505032 | tf_op jit(solution)/shard_map/ppermute | solution.py:2508
  209.4 94.6 %copy-start.11 = (bf16[1,256,2048]{2,1,0:T(8,128)(2,1)S(1)}, bf16[1,256,2048]{2,1,0:T(8,128)(2,1)}, u32[]{:S(2)}) copy-start(bf16[1,256,2048]{2,1,0:T(8,128)(2,1)} %param.28) | copy-start | bytes 3145732
  306.0 1.2 copy-start.7
  915.7 114.3 %copy-start.12 = (f32[16,128]{1,0:T(8,128)S(1)}, f32[16,128]{1,0:T(8,128)}, u32[]{:S(2)}) copy-start(f32[16,128]{1,0:T(8,128)} %get-tuple-element.106) | copy-start | bytes 24580
  915.7 117.0 %copy-start.10 = (bf16[320,2048]{1,0:T(8,128)(2,1)S(1)}, bf16[320,2048]{1,0:T(8,128)(2,1)}, u32[]{:S(2)}) copy-start(bf16[320,2048]{1,0:T(8,128)(2,1)} %get-tuple-element.109) | copy-start | bytes 3932164
  915.7 118.8 %copy-start.2 = (bf16[640,2048]{1,0:T(8,128)(2,1)S(1)}, bf16[640,2048]{1,0:T(8,128)(2,1)}, u32[]{:S(2)}) copy-start(bf16[640,2048]{1,0:T(8,128)(2,1)} %get-tuple-element.111) | copy-start | bytes 7864324
  1031.4 20.8 %copy-start.13 = (f32[2,1,128]{2,1,0:T(1,128)}, f32[2,1,128]{2,1,0:T(1,128)S(1)}, u32[]{:S(2)}) copy-start(f32[2,1,128]{2,1,0:T(1,128)S(1)} %get-tuple-element.123) | copy-start | bytes 3076
  1032.7 2.1 copy-start
  1032.7 2.9 copy-start.1
  1037.4 4.2 copy-start.3
  1041.6 2.3 copy-start.8
  1041.6 2.3 copy-start.9
  1043.9 3.5 copy-start.5
  1043.9 4.3 copy-start.6
  1048.2 4.5 copy-start.4

commit v7 on v6

--- a/solution.py
+++ b/solution.py
@@ -1641,7 +1641,7 @@
             ),
             load_sem,
         )
-        other_work = None
+        other_work = late_work = None
         if last:
             parts, part_sem, sums, swap_sem = refs[:4], refs[4], refs[5], refs[6]
             shares, small, swap_sems, refs = parts[3], refs[7:14], refs[14:17], refs[17:]
@@ -1653,12 +1653,10 @@
             )
             copies, kept = half_swaps((joint, upper), (joint_out, upper_out), swap_sems)
             greet_plane(GROUP)
-            blocks = tuple(range(SWAP_FIRST, SWAP_BLOCKS))
-            early, late = (
-                row_swap(branch, branch_out, swap_sem, SWAP_FIRST, which)
-                for which in (blocks[:-1], blocks[-1:])
+            swaps = copies((0, 1, 2, 3)) + row_swap(
+                branch, branch_out, swap_sem, SWAP_FIRST, range(SWAP_FIRST, SWAP_BLOCKS)
             )
-            for copy in copies((0, 1, 2, 3)) + kept() + early:
+            for copy in swaps + kept():
                 copy.start()
             sums[...] = jnp.zeros_like(sums)
             strips = rows // STRIP
@@ -1679,11 +1677,8 @@
                 def _():
                     small_begin([sums[number] for number in range(3)])
 
-                @pl.when(turn == GROUP - 4)
-                def _():
-                    small_middle()
-                    for copy in late:
-                        copy.start()
+            def late_work(step):
+                pl.when(step == SIDE - 1)(small_middle)
 
         else:
             greet_neighbours()
@@ -1694,13 +1689,13 @@
             return dot(mixed_part[slot], out_part[...]) + dot(active_part[slot], down_part[...])
 
         scatter_events(
-            partial, other_work, None, SCATTER_OPS_WORK if last else SCATTER_OPS, scratch
+            partial, other_work, late_work, SCATTER_OPS_EARLY if last else SCATTER_OPS, scratch
         )
         loads[4].wait()
         out[...] = hidden_part[...].astype(jnp.float32) + (scratch[0][...] + bias[...])
         if last:
             small_end()
-            wait_all(copies((0, 1, 2, 3)) + kept() + early + late)
+            wait_all(swaps + kept())
 
     out_shape = (jax.ShapeDtypeStruct((rows, D), jnp.float32),)
     out_specs = (VMEM,)

time: 1060 us -> 1050 us (level)
  Pallas kernels: 1000 us -> 989 us
    pallas_call x2, Pallas kernels: 208 us -> 193 us  [forward_scatter(): pl.pallas_call(kernel, out_shape=out_shape, in_specs=[HBM, VMEM] + [HBM]...]
where the time goes in v7:
time: 1050 us; the launch traced here: 1040 us
  Pallas kernels  989 us (94%)
  other arithmetic  36.9 us (4%)
  local copies, waits for them, and re-layouts  10.6 us (1%)
    pallas_call x2, Pallas kernels, backward_scatter(): pl.pallas_call(kernel, out_shape=out_shape, in_specs=in_specs, out_specs=...  229 us
    pallas_call x2, Pallas kernels, forward_scatter(): pl.pallas_call(kernel, out_shape=out_shape, in_specs=[HBM, VMEM] + [HBM]...  193 us
    pallas_call x2, Pallas kernels, backward_gather(): pl.pallas_call(kernel, out_shape=(jax.ShapeDtypeStruct((GROUP, rows, HEAD...  190 us
    pallas_call x1, Pallas kernels, first_gather(): pl.pallas_call(kernel, out_shape=[jax.ShapeDtypeStruct((GROUP, rows, D),...  144 us
    pallas_call x1, Pallas kernels, forward_gather(): pl.pallas_call(kernel, out_shape=[jax.ShapeDtypeStruct((GROUP, rows, D),...  98.8 us
    pallas_call x2, Pallas kernels, attend_plane_back(): pl.pallas_call(kernel, grid=(SIDE,), out_shape=(jax.ShapeDtypeStruct((SID...  68.2 us
    pallas_call x2, Pallas kernels, attend_plane(): pl.pallas_call(kernel, grid=(SIDE,), out_shape=(shape(rows, HEAD_COLS, jn...  65.5 us
  transfers between devices with their start and end apart: 1, of which 0 were waited for; matrix products, arithmetic and copies ran while one was open for 0% of the time, Pallas kernels for 9%

profile of v7, /device:TPU:0, one launch (start us, length us, event | category | flops | bytes accessed | tf_op | source)
XLA Modules:
  0.0 1039.5 jit_solution(7474104779520972170)
XLA Ops:
  2.1 1.3 fusion.2
  10.3 144.0 %shard_map.238 = (bf16[16,256,2048]{2,1,0:T(8,128)(2,1)}, bf16[16,128,896]{2,1,0:T(8,128)(2,1)}, bf16[16,256,128]{2,1,0:T(8,128)(2,1)}, bf16[16,256,128]{2,1,0:T...) custom-call(bf16[256,2048]{1,0:T(8,128)(2,1)} %bitcast.107, ...), custom_call_target="tpu_custom_call" | custom-call | tf_op jit(solution)/shard_map/pallas_call | solution.py:1124
  157.6 1.5 iota_select_fusion.spot
  159.1 46.2 %shard_map.239 = (bf16[4,4,256,128]{3,2,1,0:T(8,128)(2,1)}, f32[4,4,128,256]{3,2,1,0:T(8,128)}, f32[4,4,1024]{2,1,0:T(4,128)}, bf16[16,64,896]{2,1,0:T(8,128)(2,1)}) custom-call(bf16[4,4,256,128]{3,2,1,0:T(8,128)(2,1)} %bitcast.110, bf16[4,4,256,128]{3,2,1,0:T(8,128)(2,1)} %bitcast.112, bf16[4,4,256,128]{3,2,1,0:T(8,128)(2,1)} %bitcast.114, ...), custom_call_target="tpu_custom_call" | custom-call | tf_op jit(solution)/shard_map/pallas_call | solution.py:2289
  205.3 1.5 collective-permute-start
  207.7 1.7 slice_bitcast_fusion
  209.4 94.0 %shard_map.240.hidden.refs_4_ = f32[256,2048]{1,0:T(8,128)} custom-call(bf16[256,2048]{1,0:T(8,128)(2,1)} %bitcast.108, f32[1,2048]{1,0:T(1,128)} %get-tuple-element.122.bias, bf16[16,256,128]{2,1,0:T(8,128)(2,1)} %bitcast.116, bf16[16,256,512]{2,1,0:T(8,128)(2,1)} %get-tuple-element.68.active, bf16[2,128,2048]{2,1,0:T(8,128)(2,1)} %out_weight.7, ...), custom_call_target="tpu_custom_call" | custom-call | tf_op jit(solution)/shard_map/pallas_call | solution.py:1724
  304.0 1.9 convert_multiply_fusion
  307.2 98.8 %shard_map.241 = (bf16[16,256,2048]{2,1,0:T(8,128)(2,1)}, bf16[16,128,896]{2,1,0:T(8,128)(2,1)}, bf16[16,256,128]{2,1,0:T(8,128)(2,1)}, bf16[16,256,128]{2,1,0:T...) custom-call(f32[256,2048]{1,0:T(8,128)} %shard_map.240.hidden.refs_4_, ...), custom_call_target="tpu_custom_call" | custom-call | tf_op jit(solution)/shard_map/pallas_call | solution.py:919
  406.0 19.3 %shard_map.242 = (bf16[4,4,256,128]{3,2,1,0:T(8,128)(2,1)}, f32[4,4,128,256]{3,2,1,0:T(8,128)}, f32[4,4,1024]{2,1,0:T(4,128)}) custom-call(bf16[4,4,256,128]{3,2,1,0:T(8,128)(2,1)} %bitcast.120, bf16[4,4,256,128]{3,2,1,0:T(8,128)(2,1)} %bitcast.122, bf16[4,4,256,128]{3,2,1,0:T(8,128)(2,1)} %bitcast.124, s32[4,1,1024]{2,1,0:T(1,128)} %convert_element_type.171.begin, ...), custom_call_target="tpu_custom_call" | custom-call | tf_op jit(solution)/shard_map/pallas_call | solution.py:2289
  425.3 95.9 %shard_map.243 = (f32[16,256,128]{2,1,0:T(8,128)}, bf16[16,256,512]{2,1,0:T(8,128)(2,1)}, bf16[640,2048]{1,0:T(8,128)(2,1)}) custom-call(bf16[256,2048]{1,0:T(8,128)(2,1)} %get-tuple-element.117.own, bf16[2,128,2048]{2,1,0:T(8,128)(2,1)} %out_weight.7, bf16[2,512,2048]{2,1,0:T(8,128)(2,1)} %down_weight.7, f32[16,256,512]{2,1,0:T(8,128)} %get-tuple-element.77.inner, ...), custom_call_target="tpu_custom_call" | custom-call | tf_op jit(solution)/shard_map/pallas_call | solution.py:1237
  521.3 21.6 %shard_map.244 = bf16[4,4,256,384]{3,2,1,0:T(8,128)(2,1)} custom-call(bf16[4,4,256,128]{3,2,1,0:T(8,128)(2,1)} %bitcast.121, bf16[4,4,256,128]{3,2,1,0:T(8,128)(2,1)} %bitcast.123, bf16[4,4,256,128]{3,2,1,0:T(8,128)(2,1)} %bitcast.125, f32[4,4,256,128]{3,2,1,0:T(8,128)} %bitcast.130, f32[4,4,256,128]{3,2,1,0:T(8,128)} %bitcast.100, ...), custom_call_target="tpu_custom_call" | custom-call | tf_op jit(solution)/shard_map/pallas_call | solution.py:2410
  542.9 107.5 %shard_map.245 = (f32[256,2048]{1,0:T(8,128)}, f32[16,128]{1,0:T(8,128)}, bf16[16,64,896]{2,1,0:T(8,128)(2,1)}) custom-call(bf16[16,256,384]{2,1,0:T(8,128)(2,1)} %bitcast.104, bf16[16,256,512]{2,1,0:T(8,128)(2,1)} %get-tuple-element.81.refs_1_, bf16[2048,896]{1,0:T(8,128)(2,1)} %bitcast.126, bf16[16,256,2048]{2,1,0:T(8,128)(2,1)} %get-tuple-element.83.refs_3_, ...), custom_call_target="tpu_custom_call" | custom-call | tf_op jit(solution)/shard_map/pallas_call | solution.py:2031
  650.4 2.7 convert_element_type.176.own
  653.1 94.6 %shard_map.246 = (f32[16,256,128]{2,1,0:T(8,128)}, bf16[16,256,512]{2,1,0:T(8,128)(2,1)}, bf16[640,2048]{1,0:T(8,128)(2,1)}, bf16[640,2048]{1,0:T(8,128)(2,1)}) custom-call(bf16[256,2048]{1,0:T(8,128)(2,1)} %convert_element_type.176.own, bf16[2,128,2048]{2,1,0:T(8,128)(2,1)} %out_weight.7, bf16[2,512,2048]{2,1,0:T(8,128)(2,1)} %down_weight.7, ...), custom_call_target="tpu_custom_call" | custom-call | tf_op jit(solution)/shard_map/pallas_call | solution.py:1237
  747.7 46.6 %shard_map.247 = (bf16[4,4,256,384]{3,2,1,0:T(8,128)(2,1)}, bf16[64,6144]{1,0:T(8,128)(2,1)}, bf16[64,8192]{1,0:T(8,128)(2,1)}, bf16[16,64,512]{2,1,0:T(8,128)(2,1)}) custom-call(bf16[4,4,256,128]{3,2,1,0:T(8,128)(2,1)} %bitcast.111, bf16[4,4,256,128]{3,2,1,0:T(8,128)(2,1)} %bitcast.113, bf16[4,4,256,128]{3,2,1,0:T(8,128)(2,1)} %bitcast.115, ...), custom_call_target="tpu_custom_call" | custom-call | tf_op jit(solution)/shard_map/pallas_call | solution.py:2410
  794.3 121.3 %shard_map.248 = (f32[256,2048]{1,0:T(8,128)}, f32[16,16,128]{2,1,0:T(8,128)}, bf16[64,6144]{1,0:T(8,128)(2,1)}, bf16[64,8192]{1,0:T(8,128)(2,1)}, bf16[128,6144...) custom-call(bf16[16,256,384]{2,1,0:T(8,128)(2,1)} %bitcast.128, ...), custom_call_target="tpu_custom_call" | custom-call | tf_op jit(solution)/shard_map/pallas_call | solution.py:2031
  915.7 99.3 %shard_map.249 = (f32[256,2048]{1,0:T(8,128)}, f32[256,2048]{1,0:T(8,128)}, f32[16,128]{1,0:T(8,128)}, bf16[128,6144]{1,0:T(8,128)(2,1)}, bf16[128,8192]{1,0:T(8,128)(2,1)}, /*index=5*/bf16[320,2048]{1,0:T(8,128)(2,1)}) custom-call(f32[256,2048]{1,0:T(8,128)} %shard_map.240.hidden.refs_4_, f32[1,2048]{1,0:T(1,128)} %get-tuple-element.121.bias, ...), custom_call_target="tpu_custom_call" | custom-call | tf_op jit(solution)/shard_map/pallas_call | solution.py:1724
  1015.0 1.3 pad_maximum_fusion.4
  1017.7 1.8 maximum_bitcast_fusion
  1020.7 1.7 convert_add_fusion.1
  1022.4 4.2 convert_add_fusion
  1028.9 3.5 maximum_convert_fusion.1
  1033.2 3.9 maximum_convert_fusion
  (66 shorter events, 21.7 us)
Async XLA Ops:
  205.3 100.6 %collective-permute-start = (bf16[16,64,896]{2,1,0:T(8,128)(2,1)}, bf16[16,64,896]{2,1,0:T(8,128)(2,1)S(1)}, u32[]{:S(2)}, u32[]{:S(2)}) collective-permute-start(bf16[16,64,896]{2,1,0:T(8,128)(2,1)} %get-tuple-element.71.own_half), channel_id=1, source_target_pairs={{0,16},{16,0},{1,17},{17,1},{2,18},{18,2},{3,19},{19,3},{4,20},{20... | collective-permute-start | bytes 5505032 | tf_op jit(solution)/shard_map/ppermute | solution.py:2503
  209.4 94.6 %copy-start.11 = (bf16[1,256,2048]{2,1,0:T(8,128)(2,1)S(1)}, bf16[1,256,2048]{2,1,0:T(8,128)(2,1)}, u32[]{:S(2)}) copy-start(bf16[1,256,2048]{2,1,0:T(8,128)(2,1)} %param.28) | copy-start | bytes 3145732
  306.0 1.2 copy-start.7
  915.7 99.3 %copy-start.12 = (f32[16,128]{1,0:T(8,128)S(1)}, f32[16,128]{1,0:T(8,128)}, u32[]{:S(2)}) copy-start(f32[16,128]{1,0:T(8,128)} %get-tuple-element.106) | copy-start | bytes 24580
  915.7 102.0 %copy-start.10 = (bf16[320,2048]{1,0:T(8,128)(2,1)S(1)}, bf16[320,2048]{1,0:T(8,128)(2,1)}, u32[]{:S(2)}) copy-start(bf16[320,2048]{1,0:T(8,128)(2,1)} %get-tuple-element.109) | copy-start | bytes 3932164
  915.7 103.8 %copy-start.2 = (bf16[640,2048]{1,0:T(8,128)(2,1)S(1)}, bf16[640,2048]{1,0:T(8,128)(2,1)}, u32[]{:S(2)}) copy-start(bf16[640,2048]{1,0:T(8,128)(2,1)} %get-tuple-element.111) | copy-start | bytes 7864324
  1016.4 20.8 %copy-start.13 = (f32[2,1,128]{2,1,0:T(1,128)}, f32[2,1,128]{2,1,0:T(1,128)S(1)}, u32[]{:S(2)}) copy-start(f32[2,1,128]{2,1,0:T(1,128)S(1)} %get-tuple-element.123) | copy-start | bytes 3076
  1017.7 2.1 copy-start
  1017.7 2.9 copy-start.1
  1022.4 4.2 copy-start.3
  1026.6 2.3 copy-start.8
  1026.6 2.3 copy-start.9
  1028.9 3.5 copy-start.5
  1028.9 4.3 copy-start.6
  1033.2 4.5 copy-start.4
